TPU v7x, 32 devices: a whole 2x2x4 slice. The times are simulated.
32 devices in a mesh: chain: 16 (over z, y, x), block: 2 (over core).
Axes of the slice: x: 2, y: 2, z: 4, core: 2. Of those that a mesh axis runs over, the one named last changes fastest.
Arguments:
- site_tensors: bfloat16 [16, 32, 2, 256, 256], P('chain', 'block'), may hold values from -4.5 to 7.5
- sketch: bfloat16 [512, 256], replicated, may hold values from -6 to 6
- bond_sizes: int32 [16, 2, 32], P('chain'), may hold values from 32 to 256, as said below
- kept_ranks: int32 [16, 2, 32], P('chain'), may hold values from 0 to 256, as said below
- couplings: float32 [16, 2, 3], P('chain'), may hold values from -1 to 2.5, as said below
Outputs:
- updated_sites: bfloat16 [16, 32, 2, 256, 256], P('chain', 'block')
Inputs may be any that keep to these rules, and one draw needn't show every extreme that they name: bond_sizes[i, 1] are the block sizes of the bond right of site i and bond_sizes[i, 0] equals bond_sizes[i - 1 mod 16, 1]; every bond has a block of exactly 256. kept_ranks[i, 1] belongs to the bond right of site i and kept_ranks[i, 0] equals kept_ranks[i - 1 mod 16, 1]; a count never exceeds that block's size; some block keeps exactly 256. couplings[i, 0] equals couplings[i - 1 mod 16, 1]; hopping lies in 0.5 to 2.5, the other two in -1 to 1.
All inputs are finite; a program needn't handle non-finite values.
Results may differ from a plain program's by a relative error of at most 0.035.
Values may be sent and summed in bfloat16 or wider, within the bound.
No kernel may reach another device: no remote copies, remote signals or barrier semaphores. Data moves between devices by JAX's collectives and lax.ppermute only.
A program may use at most 128 MiB of HBM per device.

v0:
```python
import math

import jax
import jax.numpy as jnp
from jax import lax
from jax.sharding import PartitionSpec as P

tau_step = 0.5


def shifted(value, axis, by):
    devices = lax.axis_size(axis)
    pairs = [(i, i + by) for i in range(devices) if 0 <= i + by < devices]
    return lax.ppermute(value, axis, pairs)


def shifted_2(value, axis, steps):
    count = lax.axis_size(axis)
    pairs = [(source, (source + steps) % count) for source in range(count)]
    return lax.ppermute(value, axis, pairs)


def gate_terms(coupling):
    hopping = coupling[0]
    ising_term = coupling[1]
    field_term = coupling[2]
    rotation = 0.5 * tau_step * hopping
    middle_scale = jnp.exp(0.25 * tau_step * ising_term)
    weight_empty = jnp.exp(-tau_step * (0.25 * ising_term - 0.5 * field_term))
    weight_full = jnp.exp(-tau_step * (0.25 * ising_term + 0.5 * field_term))
    weight_stay = middle_scale * jnp.cosh(rotation)
    weight_swap = -middle_scale * jnp.sinh(rotation)
    return (weight_empty, weight_stay, weight_swap, weight_full)


def local_mask(site_block, sizes_row, first_sector):
    sector_count = site_block.shape[0]
    block_width = site_block.shape[-1]
    right_ext = jnp.concatenate([sizes_row[1], jnp.zeros((1,), jnp.int32)])
    left_here = lax.dynamic_slice_in_dim(sizes_row[0], first_sector, sector_count)
    right_here = lax.dynamic_slice_in_dim(right_ext, first_sector, sector_count)
    right_next = lax.dynamic_slice_in_dim(right_ext, first_sector + 1, sector_count)
    row_index = jnp.arange(block_width, dtype=jnp.int32)
    row_keep = row_index[None, :] < left_here[:, None]
    col_stay = row_index[None, :] < right_here[:, None]
    col_next = row_index[None, :] < right_next[:, None]
    keep_zero = row_keep[:, :, None] & col_stay[:, None, :]
    keep_one = row_keep[:, :, None] & col_next[:, None, :]
    keep_both = jnp.stack([keep_zero, keep_one], axis=1)
    return jnp.where(keep_both, site_block, jnp.zeros_like(site_block))


def round_product(left_part, right_part):
    return jnp.einsum(
        "kij,kjl->kil", left_part, right_part, preferred_element_type=jnp.float32
    ).astype(jnp.bfloat16)


def compute_pair(left_site, right_site, mid_ranks, coupling, sketch):
    sector_count = left_site.shape[0]
    block_width = left_site.shape[-1]
    kept_count = sketch.shape[1]
    left_zero = left_site[:, 0]
    left_one = left_site[:, 1]
    right_zero = right_site[:, 0]
    right_one = right_site[:, 1]
    stay_stay = round_product(left_zero, right_zero)
    stay_up = round_product(left_zero, right_one)
    below_one, below_stay_up = shifted((left_one[-1:], stay_up[-1:]), "block", 1)
    left_below = jnp.concatenate([below_one, left_one[:-1]], axis=0)
    up_stay = round_product(left_below, right_zero)
    above_up_stay = shifted(up_stay[:1], "block", -1)
    stay_up_prev = jnp.concatenate([below_stay_up, stay_up[:-1]], axis=0)
    up_stay_next = jnp.concatenate([up_stay[1:], above_up_stay], axis=0)
    up_up = round_product(left_below, right_one)
    weight_empty, weight_stay, weight_swap, weight_full = gate_terms(coupling)
    top_left = weight_empty * stay_stay.astype(jnp.float32)
    top_right = weight_stay * stay_up.astype(jnp.float32) + weight_swap * up_stay_next.astype(
        jnp.float32
    )
    bottom_left = weight_swap * stay_up_prev.astype(jnp.float32) + weight_stay * up_stay.astype(
        jnp.float32
    )
    bottom_right = weight_full * up_up.astype(jnp.float32)
    two_site = jnp.concatenate(
        [
            jnp.concatenate([top_left, top_right], axis=2),
            jnp.concatenate([bottom_left, bottom_right], axis=2),
        ],
        axis=1,
    ).astype(jnp.bfloat16)
    sample = jnp.einsum("kab,bc->kac", two_site, sketch, preferred_element_type=jnp.float32)
    keep_mask = (jnp.arange(kept_count, dtype=jnp.int32)[None, :] < mid_ranks[:, None]).astype(
        jnp.float32
    )
    sample = sample * keep_mask[:, None, :]
    gram_matrix = jnp.einsum("kai,kaj->kij", sample, sample, precision=lax.Precision.HIGHEST)
    gram_matrix = (
        gram_matrix + (1.0 - keep_mask)[:, :, None] * jnp.eye(kept_count, dtype=jnp.float32)[None]
    )
    factor = jnp.linalg.cholesky(gram_matrix)
    solved = lax.linalg.triangular_solve(
        factor, sample, left_side=False, lower=True, transpose_a=True
    )
    basis_rows = (solved * math.sqrt(block_width)).astype(jnp.bfloat16)
    coef = jnp.einsum("kar,kab->krb", basis_rows, two_site, preferred_element_type=jnp.float32)
    norm_total = lax.psum(jnp.sum(coef * coef), "block")
    target = float(sector_count * lax.axis_size("block") * kept_count * block_width)
    scaled = (coef * jnp.sqrt(target / norm_total)).astype(jnp.bfloat16)
    return (basis_rows, scaled)


def as_left_site(basis_rows):
    block_width = basis_rows.shape[1] // 2
    above_lower = shifted(basis_rows[:1, block_width:, :], "block", -1)
    lower_parts = jnp.concatenate([basis_rows[1:, block_width:, :], above_lower], axis=0)
    new_zero = basis_rows[:, :block_width, :]
    return jnp.stack([new_zero, lower_parts], axis=1)


def as_right_site(scaled):
    block_width = scaled.shape[2] // 2
    new_zero = scaled[:, :, :block_width]
    new_one = scaled[:, :, block_width:]
    return jnp.stack([new_zero, new_one], axis=1)


def body(site_tensors, sketch, bond_sizes, kept_ranks, couplings):
    sector_count = site_tensors.shape[1]
    first_sector = lax.axis_index("block") * sector_count
    own_site = local_mask(site_tensors[0], bond_sizes[0], first_sector)
    right_ranks = lax.dynamic_slice_in_dim(kept_ranks[0, 1], first_sector, sector_count)
    position = lax.axis_index("chain")
    left_ranks = lax.dynamic_slice_in_dim(kept_ranks[0, 0], first_sector, sector_count)
    partner = shifted_2(own_site, "chain", -1)
    basis_rows, scaled = compute_pair(own_site, partner, right_ranks, couplings[0, 1], sketch)
    settled = as_left_site(basis_rows)
    carried = shifted_2(scaled, "chain", 2)
    basis_odd, scaled_odd = compute_pair(
        as_right_site(carried), settled, left_ranks, couplings[0, 0], sketch
    )
    returned = shifted_2(basis_odd, "chain", -1)
    current = jnp.where(position % 2 == 0, as_right_site(scaled_odd), as_left_site(returned))
    return current[None]


def solution(mesh):
    placed = (
        P("chain", "block", None, None, None),
        P(),
        P("chain", None, None),
        P("chain", None, None),
        P("chain", None, None),
    )
    return jax.shard_map(
        body,
        mesh=mesh,
        in_specs=placed,
        out_specs=P("chain", "block", None, None, None),
        check_vma=False,
    )
```

profile of v0, /device:TPU:0, one launch (start us, length us, event | category | flops | bytes accessed | tf_op | source)
XLA Modules:
  0.0 2235.3 jit_solution(13713614500000138461)
XLA Ops:
  12.7 6.9 collective-permute-start
  27.6 82.2 %collective-permute-done = bf16[16,2,256,256]{2,3,0,1:T(8,128)(2,1)} collective-permute-done((bf16[16,2,256,256]{2,3,0,1:T(8,128)(2,1)}, bf16[16,2,256,256]{2,3,0,1:T(8,128)(2,1)}, u32[]{:S(2)}, u32[]{:S(2)}) %collective-permute-start) | collective-permute-done | bytes 4194336 | tf_op jit(solution)/shard_map/ppermute | solution.py:20
  133.2 14.9 multiply_add_fusion.1
  159.5 187.8 %custom-call.17 = f32[16,128,128]{2,1,0:T(8,128)S(1)} custom-call(f32[16,128,128]{2,1,0:T(8,128)S(1)} %cholesky.198), custom_call_target="Cholesky" | custom-call | tf_op jit(solution)/shard_map/jit(cholesky)/cholesky | solution.py:101
  349.9 157.8 %custom-call.18 = f32[16,1,128,128]{2,3,1,0:T(8,128)} custom-call(f32[16,1,128,128]{3,2,1,0:T(8,128)S(1)} %select_bitcast_fusion.1), custom_call_target="InvertDiagBlocksLowerTriangular" | custom-call | tf_op jit(solution)/shard_map/jit(cholesky)/cholesky | solution.py:101
  515.9 188.7 %custom-call.19 = f32[16,128,128]{2,1,0:T(8,128)S(1)} custom-call(f32[16,128,128]{2,1,0:T(8,128)} %convolution_subtract_fusion.1), custom_call_target="Cholesky" | custom-call | tf_op jit(solution)/shard_map/jit(cholesky)/cholesky | solution.py:101
  712.7 9.4 while.4
  722.1 315.8 %custom-call.20 = f32[16,2,128,128]{2,3,1,0:T(8,128)} custom-call(f32[16,2,128,128]{3,2,1,0:T(8,128)} %bitcast.142), custom_call_target="InvertDiagBlocksLowerTriangular" | custom-call | tf_op jit(solution)/shard_map/triangular_solve/custom-call.0 | solution.py:102
  1037.9 9.0 fusion.6
  1047.0 8.2 fusion.20
  1061.7 8.4 multiply_reduce_fusion.1
  1074.7 6.6 multiply_convert_fusion.1
  1088.6 88.6 %collective-permute-done.4 = bf16[16,256,512]{2,1,0:T(8,128)(2,1)} collective-permute-done((bf16[16,256,512]{2,1,0:T(8,128)(2,1)}, bf16[16,256,512]{2,1,0:T(8,128)(2,1)}, u32[]{:S(2)}, u32[]{:S(2)}) %collective-permute-start.4) | collective-permute-done | bytes 4194336 | tf_op jit(solution)/shard_map/ppermute | solution.py:20
  1204.1 14.9 multiply_add_fusion
  1230.5 187.7 %custom-call.21 = f32[16,128,128]{2,1,0:T(8,128)S(1)} custom-call(f32[16,128,128]{2,1,0:T(8,128)S(1)} %cholesky.201), custom_call_target="Cholesky" | custom-call | tf_op jit(solution)/shard_map/jit(cholesky)/cholesky | solution.py:101
  1420.8 157.1 %custom-call.22 = f32[16,1,128,128]{2,3,1,0:T(8,128)S(1)} custom-call(f32[16,1,128,128]{3,2,1,0:T(8,128)S(1)} %select_bitcast_fusion), custom_call_target="InvertDiagBlocksLowerTriangular" | custom-call | tf_op jit(solution)/shard_map/jit(cholesky)/cholesky | solution.py:101
  1584.9 187.8 %custom-call.23 = f32[16,128,128]{2,1,0:T(8,128)S(1)} custom-call(f32[16,128,128]{2,1,0:T(8,128)S(1)} %convolution_subtract_fusion), custom_call_target="Cholesky" | custom-call | tf_op jit(solution)/shard_map/jit(cholesky)/cholesky | solution.py:101
  1779.2 7.7 while.5
  1786.9 315.1 %custom-call.24 = f32[16,2,128,128]{2,3,1,0:T(8,128)} custom-call(f32[16,2,128,128]{3,2,1,0:T(8,128)S(1)} %bitcast.141), custom_call_target="InvertDiagBlocksLowerTriangular" | custom-call | tf_op jit(solution)/shard_map/triangular_solve/custom-call.0 | solution.py:102
  2102.0 9.1 fusion.3
  2111.1 8.2 fusion.16
  2129.7 8.3 multiply_reduce_fusion
  2142.2 9.2 copy.60
  2156.7 63.5 %collective-permute-done.9 = bf16[16,512,256]{1,2,0:T(8,128)(2,1)} collective-permute-done((bf16[16,512,256]{1,2,0:T(8,128)(2,1)}, bf16[16,512,256]{1,2,0:T(8,128)(2,1)}, u32[]{:S(2)}, u32[]{:S(2)}) %collective-permute-start.9) | collective-permute-done | bytes 4194336 | tf_op jit(solution)/shard_map/ppermute | solution.py:20
  (175 shorter events, 190.9 us)
Async XLA Ops:
  0.0 126.0 %copy-start = (bf16[512,256]{1,0:T(8,128)(2,1)S(1)}, bf16[512,256]{1,0:T(8,128)(2,1)}, u32[]{:S(2)}) copy-start(bf16[512,256]{1,0:T(8,128)(2,1)} %param.9) | copy-start | bytes 786436
  8.8 13.3 copy-start.14
  8.8 16.7 copy-start.15
  12.7 97.1 %collective-permute-start = (bf16[16,2,256,256]{2,3,0,1:T(8,128)(2,1)}, bf16[16,2,256,256]{2,3,0,1:T(8,128)(2,1)}, u32[]{:S(2)}, u32[]{:S(2)}) collective-permute-start(bf16[16,2,256,256]{2,3,0,1:T(8,128)(2,1)} %add_select_fusion), channel_id=1, source_target_pairs={{0,30},{2,0},{4,2},{6,4},{8,6},{10,8},{12,10},{14,12},{16,14},{18,... | collective-permute-start | bytes 12582920 | tf_op jit(solution)/shard_map/ppermute | solution.py:20
  20.6 96.6 %collective-permute-start.1 = (bf16[1,256,256]{1,2,0:T(8,128)(2,1)S(1)}, bf16[1,256,256]{1,2,0:T(8,128)(2,1)S(1)}, u32[]{:S(2)}, u32[]{:S(2)}) collective-permute-start(bf16[1,256,256]{1,2,0:T(8,128)(2,1)S(1)} %slice_bitcast_fusion.21), channel_id=1, source_target_pairs={{0,1},{2,3},{4,5},{6,7},{8,9},{10,11},{12,13},{14,15},{16,17},{18,... | collective-permute-start | bytes 393224 | tf_op jit(solution)/shard_map/ppermute | solution.py:14
  112.7 4.5 collective-permute-start.3
  117.0 8.7 copy-start.17
  120.8 4.0 collective-permute-start.2
  1037.9 17.3 slice-start.2
  1046.9 8.2 slice-start.3
  1047.0 8.2 copy-start.12
  1061.7 8.4 copy-start.6
  1081.4 95.8 %collective-permute-start.4 = (bf16[16,256,512]{2,1,0:T(8,128)(2,1)}, bf16[16,256,512]{2,1,0:T(8,128)(2,1)}, u32[]{:S(2)}, u32[]{:S(2)}) collective-permute-start(bf16[16,256,512]{2,1,0:T(8,128)(2,1)} %multiply_convert_fusion.1), channel_id=1, source_target_pairs={{0,4},{2,6},{4,8},{6,10},{8,12},{10,14},{12,16},{14,18},{16,20},{1... | collective-permute-start | bytes 12582920 | tf_op jit(solution)/shard_map/ppermute | solution.py:20
  1085.4 3.2 collective-permute-start.5
  1088.5 94.8 %copy-start.7 = (bf16[16,512,256]{1,2,0:T(8,128)(2,1)S(1)}, bf16[16,512,256]{1,2,0:T(8,128)(2,1)}, u32[]{:S(2)}) copy-start(bf16[16,512,256]{1,2,0:T(8,128)(2,1)} %copy-done.6) | copy-start | bytes 12582916
  1179.6 9.3 collective-permute-start.8
  1182.0 6.9 collective-permute-start.6
  1191.3 3.2 collective-permute-start.7
  2102.0 17.3 slice-start
  2111.1 8.2 slice-start.1
  2111.1 8.2 copy-start.13
  2126.3 93.9 %collective-permute-start.9 = (bf16[16,512,256]{1,2,0:T(8,128)(2,1)}, bf16[16,512,256]{1,2,0:T(8,128)(2,1)}, u32[]{:S(2)}, u32[]{:S(2)}) collective-permute-start(bf16[16,512,256]{1,2,0:T(8,128)(2,1)} %fusion.1), channel_id=1, source_target_pairs={{0,30},{2,0},{4,2},{6,4},{8,6},{10,8},{12,10},{14,12},{16,14},{18,... | collective-permute-start | bytes 12582920 | tf_op jit(solution)/shard_map/ppermute | solution.py:20
  2221.1 4.7 collective-permute-start.10
  2226.1 8.8 copy-start.1
  (14 other events, 43.7 us)
where the time goes:
time: 2240 us
  other arithmetic  1740 us (78%)
  waiting for transfers between devices  236 us (11%)
  matrix products  134 us (6%)
  local copies, waits for them, and re-layouts  84.5 us (4%)
    another operation x18, other arithmetic, compute_pair(): factor = jnp.linalg.cholesky(gram_matrix)  1070 us
    another operation x6, other arithmetic, compute_pair(): lax.linalg.triangular_solve(factor, sample, left_side=False, lower=True,...  641 us
    ppermute x3, waiting for transfers between devices, shifted_2(): return lax.ppermute(value, axis, pairs)  234 us
  transfers between devices with their start and end apart: 11, of which 5 were waited for; matrix products, arithmetic and copies ran while one was open for 2% of the time, Pallas kernels for 0%

commit v1 on v0

v1 whole, which is shorter than its diff:
```python
import math

import jax
import jax.numpy as jnp
from jax import lax
from jax.experimental import pallas as pl
from jax.experimental.pallas import tpu as pltpu
from jax.sharding import PartitionSpec as P

tau_step = 0.5
SUB = 8
LANES = 128
PANEL = 16
EXACT = lax.Precision.HIGHEST
LAST = (((1,), (1,)), ((), ()))
PLAIN = (((1,), (0,)), ((), ()))


def gate_terms(coupling):
    hopping = coupling[0]
    ising_term = coupling[1]
    field_term = coupling[2]
    rotation = 0.5 * tau_step * hopping
    middle_scale = jnp.exp(0.25 * tau_step * ising_term)
    weight_empty = jnp.exp(-tau_step * (0.25 * ising_term - 0.5 * field_term))
    weight_full = jnp.exp(-tau_step * (0.25 * ising_term + 0.5 * field_term))
    weight_stay = middle_scale * jnp.cosh(rotation)
    weight_swap = -middle_scale * jnp.sinh(rotation)
    return jnp.stack([weight_empty, weight_stay, weight_swap, weight_full])


def local_mask(site_block, sizes_row, first_sector):
    sector_count = site_block.shape[0]
    block_width = site_block.shape[-1]
    right_ext = jnp.concatenate([sizes_row[1], jnp.zeros((1,), jnp.int32)])
    left_here = lax.dynamic_slice_in_dim(sizes_row[0], first_sector, sector_count)
    right_here = lax.dynamic_slice_in_dim(right_ext, first_sector, sector_count)
    right_next = lax.dynamic_slice_in_dim(right_ext, first_sector + 1, sector_count)
    row_index = jnp.arange(block_width, dtype=jnp.int32)
    row_keep = row_index[None, :] < left_here[:, None]
    col_stay = row_index[None, :] < right_here[:, None]
    col_next = row_index[None, :] < right_next[:, None]
    keep_zero = row_keep[:, :, None] & col_stay[:, None, :]
    keep_one = row_keep[:, :, None] & col_next[:, None, :]
    keep_both = jnp.stack([keep_zero, keep_one], axis=1)
    return jnp.where(keep_both, site_block, jnp.zeros_like(site_block))


def dot(left, right, dims, precision=None):
    return lax.dot_general(
        left, right, dims, precision=precision, preferred_element_type=jnp.float32
    )


def spread(row, lane_index):
    return jnp.broadcast_to(row[:, lane_index : lane_index + 1], row.shape)


def refined_reciprocal(value):
    guess = pltpu.reciprocal(value, approx=True)
    return guess * (2.0 - value * guess)


def factor_tile(gram_rows, inverse_rows):
    lane = lax.broadcasted_iota(jnp.int32, (SUB, LANES), 1)

    def at(index):
        return slice(index * SUB, (index + 1) * SUB)

    for start in range(0, LANES, PANEL):
        stop = start + PANEL
        rows = [gram_rows[at(i), :] for i in range(start, stop)]
        later = []
        for step in range(PANEL):
            k = start + step
            row = rows[step]
            pivot = spread(row, k)
            scaled = jnp.where(lane == k, 1.0, row) * refined_reciprocal(pivot)
            unit = jnp.where(lane < k, row, jnp.where(lane == k, 1.0, 0.0))
            inverse_rows[at(k), :] = unit * lax.rsqrt(pivot)
            for other in range(step + 1, PANEL):
                rows[other] = (
                    jnp.where(lane == k, 0.0, rows[other]) - spread(row, start + other) * scaled
                )
            later.append(jnp.where((lane > k) & (lane < stop), 0.0, scaled))
        for i in range(stop, LANES):
            row = jnp.where((lane >= start) & (lane < stop), 0.0, gram_rows[at(i), :])
            for step in range(PANEL):
                row = row - spread(rows[step], i) * later[step]
            gram_rows[at(i), :] = row


def pair_kernel(
    second,
    weights,
    ranks,
    left_ref,
    right_ref,
    sketch_ref,
    basis_ref,
    coef_ref,
    norm_ref,
    two_ref,
    sample_ref,
    gram_ref,
    inverse_ref,
    rows_ref,
    factor_ref,
):
    count, kept, double = sample_ref.shape
    width = double // 2
    tiles = kept // LANES
    row_index = lax.broadcasted_iota(jnp.int32, (kept, 1), 0)
    eye = (
        lax.broadcasted_iota(jnp.int32, (kept, kept), 0)
        == lax.broadcasted_iota(jnp.int32, (kept, kept), 1)
    )

    def left(m, s):
        if second:
            return left_ref[m, :, s * width : (s + 1) * width]
        return left_ref[m, s]

    def right(m, s):
        if second:
            return right_ref[m, :, s * width : (s + 1) * width]
        return right_ref[m, s]

    def product(a, b):
        rounded = dot(a, b, LAST if second else PLAIN).astype(jnp.bfloat16)
        return rounded.astype(jnp.float32)

    w_empty, w_stay, w_swap, w_full = weights[0], weights[1], weights[2], weights[3]

    @pl.loop(0, count)
    def _(m):
        below_zero, below_one = left(m, 0), left(m, 1)
        here_zero, here_one = left(m + 1, 0), left(m + 1, 1)
        same_zero, same_one = right(m, 0), right(m, 1)
        next_zero, next_one = right(m + 1, 0), right(m + 1, 1)
        low, high = slice(0, width), slice(width, double)
        two_ref[m, low, low] = (w_empty * product(here_zero, same_zero)).astype(jnp.bfloat16)
        two_ref[m, low, high] = (
            w_stay * product(here_zero, next_one) + w_swap * product(here_one, next_zero)
        ).astype(jnp.bfloat16)
        two_ref[m, high, low] = (
            w_swap * product(below_zero, same_one) + w_stay * product(below_one, same_zero)
        ).astype(jnp.bfloat16)
        two_ref[m, high, high] = (w_full * product(below_one, next_one)).astype(jnp.bfloat16)
        sample = dot(sketch_ref[...], two_ref[m], LAST)
        keep = row_index < ranks[m]
        sample = jnp.where(keep, sample, 0.0)
        sample_ref[m] = sample
        gram = dot(sample, sample, LAST, EXACT)
        gram_ref[m] = gram + jnp.where(eye & jnp.logical_not(keep), 1.0, 0.0)

    for tile in range(tiles):
        span = slice(tile * LANES, (tile + 1) * LANES)
        for m in range(count):
            rows_ref[pl.ds(m, LANES, stride=SUB), :] = gram_ref[m, span, span]
        factor_tile(rows_ref, factor_ref)
        for m in range(count):
            inverse_ref[m, span, span] = factor_ref[pl.ds(m, LANES, stride=SUB), :]
            if tile + 1 < tiles:
                inverse_ref[m, span, (tile + 1) * LANES :] = jnp.zeros(
                    (LANES, kept - (tile + 1) * LANES), jnp.float32
                )

        @pl.loop(0, count)
        def _(m):
            block = inverse_ref[m, span, span]
            for lower in range(tile + 1, tiles):
                rest = slice(lower * LANES, (lower + 1) * LANES)
                gram_ref[m, rest, span] = dot(gram_ref[m, rest, span], block, LAST, EXACT)
            for row in range(tile + 1, tiles):
                for column in range(tile + 1, row + 1):
                    across = slice(row * LANES, (row + 1) * LANES)
                    down = slice(column * LANES, (column + 1) * LANES)
                    gram_ref[m, across, down] = gram_ref[m, across, down] - dot(
                        gram_ref[m, across, span], gram_ref[m, down, span], LAST, EXACT
                    )
            if tile > 0:
                done = slice(0, tile * LANES)
                carried = dot(gram_ref[m, span, done], inverse_ref[m, done, done], PLAIN, EXACT)
                inverse_ref[m, span, done] = -dot(block, carried, PLAIN, EXACT)

    norm_ref[...] = jnp.zeros_like(norm_ref)

    @pl.loop(0, count)
    def _(m):
        solved = dot(inverse_ref[m], sample_ref[m], PLAIN, EXACT) * math.sqrt(width)
        basis = solved.astype(jnp.bfloat16)
        if second:
            for s in range(2):
                turned = jnp.transpose(solved[:, s * width : (s + 1) * width])
                basis_ref[m, s] = turned.astype(jnp.bfloat16)
        else:
            basis_ref[m] = basis
        coef = dot(basis, two_ref[m], PLAIN)
        norm_ref[...] += jnp.sum(coef * coef, axis=0, keepdims=True)
        rounded = coef.astype(jnp.bfloat16)
        if second:
            for s in range(2):
                coef_ref[m, s] = rounded[:, s * width : (s + 1) * width]
        else:
            coef_ref[m] = rounded


def pair_update(second, weights, ranks, left, right, sketch_turned):
    count = ranks.shape[0]
    kept, double = sketch_turned.shape
    width = double // 2
    shape = (count, 2, width, kept) if second else (count, kept, double)
    coef_shape = (count, 2, kept, width) if second else (count, kept, double)
    vmem = pl.BlockSpec(memory_space=pltpu.VMEM)
    smem = pl.BlockSpec(memory_space=pltpu.SMEM)

    def kernel(*refs):
        pair_kernel(second, *refs)

    basis, coef, norm = pl.pallas_call(
        kernel,
        out_shape=(
            jax.ShapeDtypeStruct(shape, jnp.bfloat16),
            jax.ShapeDtypeStruct(coef_shape, jnp.bfloat16),
            jax.ShapeDtypeStruct((1, double), jnp.float32),
        ),
        in_specs=[smem, smem, vmem, vmem, vmem],
        out_specs=(vmem, vmem, vmem),
        scratch_shapes=[
            pltpu.VMEM((count, double, double), jnp.bfloat16),
            pltpu.VMEM((count, kept, double), jnp.float32),
            pltpu.VMEM((count, kept, kept), jnp.float32),
            pltpu.VMEM((count, kept, kept), jnp.float32),
            pltpu.VMEM((LANES * SUB, LANES), jnp.float32),
            pltpu.VMEM((LANES * SUB, LANES), jnp.float32),
        ],
        compiler_params=pltpu.CompilerParams(vmem_limit_bytes=40 * 2**20),
        cost_estimate=pl.CostEstimate(
            flops=count * 20 * kept * double * double,
            bytes_accessed=8 * count * kept * double * 2,
            transcendentals=0,
        ),
    )(weights, ranks, left, right, sketch_turned)
    return basis, coef, jnp.sum(norm)


def move(value, pairs_of):
    sites, parts = lax.axis_size("chain"), lax.axis_size("block")
    pairs = []
    for site in range(sites):
        for part in range(parts):
            target = pairs_of(site, part)
            if target is None or not 0 <= target[1] < parts:
                continue
            pairs.append((site * parts + part, (target[0] % sites) * parts + target[1]))
    return lax.ppermute(value, ("chain", "block"), pairs)


def group_sum(value, offset):
    total = lax.psum(value, "block")
    return total + move(
        total[None],
        lambda c, b: (c + 1, b) if (c + offset) % 2 == 0 else (c - 1, b),
    )[0]


def body(site_tensors, sketch, bond_sizes, kept_ranks, couplings):
    sectors = site_tensors.shape[1]
    half = sectors // 2
    width = site_tensors.shape[-1]
    kept = sketch.shape[1]
    parts = lax.axis_size("block")
    first_sector = lax.axis_index("block") * sectors
    is_even = lax.axis_index("chain") % 2 == 0
    own = local_mask(site_tensors[0], bond_sizes[0], first_sector)
    sketch_turned = jnp.transpose(sketch)
    first_here = first_sector + jnp.where(is_even, 0, half)

    partner = move(
        jnp.where(is_even, own[half - 1 :], own[: half + 1]),
        lambda c, b: (c + 1, b) if c % 2 == 0 else (c - 1, b),
    )
    edge = move(
        jnp.where(is_even, own[-1], own[0]),
        lambda c, b: (c, b + 1) if c % 2 == 0 else (c, b - 1),
    )
    corner = move(own[-1, 1], lambda c, b: None if c % 2 == 0 else (c - 1, b + 1))
    left = jnp.where(is_even, jnp.concatenate([edge[None], own[:half]]), partner)
    right_zero = jnp.where(
        is_even, partner[:, 0], jnp.concatenate([own[half:, 0], edge[None, 0]])
    )
    right_one = jnp.where(
        is_even, jnp.concatenate([corner[None], partner[:half, 1]]), own[half - 1 :, 1]
    )
    right = jnp.stack([right_zero, right_one], axis=1)
    pair_row = jnp.where(is_even, 1, 0)
    ranks = lax.dynamic_slice(kept_ranks[0], (pair_row, first_here), (1, half))[0]
    weights = gate_terms(lax.dynamic_index_in_dim(couplings[0], pair_row, 0, keepdims=False))
    basis, coef, norm = pair_update(False, weights, ranks, left, right, sketch_turned)
    target = float(sectors * parts * kept * width)
    scale = jnp.sqrt(target / group_sum(norm, 0))

    carried = move(
        jnp.where(is_even, coef, basis), lambda c, b: (c + 2, b) if c % 2 == 0 else (c - 2, b)
    )
    coef_below = move(coef[-1:], lambda c, b: (c + 1, b) if c % 2 == 0 else (c + 1, b + 1))
    basis_above = move(basis[:1], lambda c, b: (c - 1, b - 1) if c % 2 == 0 else (c - 1, b))
    scale_from_left = move(scale[None], lambda c, b: (c + 1, b) if c % 2 == 1 else None)[0]
    scale = jnp.where(is_even, scale_from_left, scale)
    left = jnp.concatenate([coef_below, jnp.where(is_even, carried, coef)])
    right = jnp.concatenate([jnp.where(is_even, basis, carried), basis_above])
    pair_row = jnp.where(is_even, 0, 1)
    ranks = lax.dynamic_slice(kept_ranks[0], (pair_row, first_here), (1, half))[0]
    weights = gate_terms(lax.dynamic_index_in_dim(couplings[0], pair_row, 0, keepdims=False))
    basis, coef, norm = pair_update(True, weights * scale, ranks, left, right, sketch_turned)
    scale = jnp.sqrt(target / group_sum(norm, 1))

    returned = move(
        jnp.where(is_even, basis, coef), lambda c, b: (c - 1, b) if c % 2 == 0 else (c + 1, b)
    )
    lower_above = move(basis[:1, 1], lambda c, b: (c - 1, b - 1) if c % 2 == 0 else None)
    new_left = jnp.stack(
        [
            jnp.concatenate([returned[:, 0], basis[:, 0]]),
            jnp.concatenate([returned[1:, 1], basis[:, 1], lower_above]),
        ],
        axis=1,
    )
    new_right = jnp.concatenate([coef, returned]).astype(jnp.float32) * scale
    return jnp.where(is_even, new_right.astype(jnp.bfloat16), new_left)[None]


def solution(mesh):
    placed = (
        P("chain", "block", None, None, None),
        P(),
        P("chain", None, None),
        P("chain", None, None),
        P("chain", None, None),
    )
    return jax.shard_map(
        body,
        mesh=mesh,
        in_specs=placed,
        out_specs=P("chain", "block", None, None, None),
        check_vma=False,
    )
```

time: 2240 us -> 318 us (0.14)
  other arithmetic: 1740 us -> 20.3 us
  matrix products: 134 us -> 0 us
  waiting for transfers between devices: 236 us -> 111 us
  Pallas kernels: 0 us -> 124 us
  local copies, waits for them, and re-layouts: 84.5 us -> 15.1 us
    another operation x27 -> x4, other arithmetic: 1710 us -> 0.75 us  [the longest x2 0.45 us: body(): jnp.stack([jnp.concatenate([returned[:, 0], basis[:, 0]]), jnp.concatenat...]
    ppermute x11, waiting for transfers between devices: 236 us -> 111 us  [move(): return lax.ppermute(value, ('chain', 'block'), pairs)]
    pallas_call x0 -> x2, Pallas kernels: none -> 124 us  [pair_update(): pl.pallas_call(kernel, out_shape=(jax.ShapeDtypeStruct(shape, jnp.bfloat1...]
    dot_general x14 -> x0, matrix products: 75.5 us -> none  [the longest x2 29.7 us: compute_pair(): jnp.einsum('kai,kaj->kij', sample, sample, precision=lax.Precision.HIGHEST)]
    another operation x10 -> x0, matrix products: 58.3 us -> none  [the longest x6 43.1 us: compute_pair(): lax.linalg.triangular_solve(factor, sample, left_side=False, lower=True,...]
    another operation x21 -> x0, local copies, waits for them, and re-layouts: 26.1 us -> none  [the longest x15 19 us: compute_pair(): lax.linalg.triangular_solve(factor, sample, left_side=False, lower=True,...]
  transfers between devices with their start and end apart: 11 -> 11, of which waited for: 5 -> 5; matrix products, arithmetic and copies ran while one was open for 2% -> 4% of each run, Pallas kernels for 0% -> 0%
where the time goes in v1:
time: 318 us; the launch traced here: 314 us
  Pallas kernels  124 us (39%)
  waiting for transfers between devices  111 us (35%)
  starting transfers between devices  28.3 us (9%)
  other arithmetic  20.3 us (6%)
  local copies, waits for them, and re-layouts  15.1 us (5%)
  between operations  9.72 us (3%)
  blocking collectives  6.07 us (2%)
    pallas_call x2, Pallas kernels, pair_update(): pl.pallas_call(kernel, out_shape=(jax.ShapeDtypeStruct(shape, jnp.bfloat1...  124 us
    ppermute x11, waiting for transfers between devices, move(): return lax.ppermute(value, ('chain', 'block'), pairs)  111 us
    ppermute x11, starting transfers between devices, move(): return lax.ppermute(value, ('chain', 'block'), pairs)  28.3 us
  transfers between devices with their start and end apart: 11, of which 5 were waited for; matrix products, arithmetic and copies ran while one was open for 4% of the time, Pallas kernels for 0%

profile of v1, /device:TPU:0, one launch (start us, length us, event | category | flops | bytes accessed | tf_op | source)
XLA Modules:
  0.0 314.3 jit_solution(9892879871030265656)
XLA Ops:
  2.4 2.5 add_select_fusion
  4.9 1.8 slice_select_fusion
  6.7 2.9 collective-permute-start.1
  9.7 1.5 collective-permute-start
  17.2 44.0 %collective-permute-done.1 = bf16[9,2,256,256]{3,2,1,0:T(8,128)(2,1)} collective-permute-done((bf16[9,2,256,256]{3,2,1,0:T(8,128)(2,1)}, bf16[9,2,256,256]{3,2,1,0:T(8,128)(2,1)}, u32[]{:S(2)}, u32[]{:S(2)}) %collective-permute-start.1) | collective-permute-done | bytes 2359328 | tf_op jit(solution)/shard_map/ppermute | solution.py:257
  62.6 1.5 slice_select_fusion.1
  64.1 1.5 slice_select_fusion.2
  67.7 61.8 %shard_map.55 = (bf16[8,256,512]{2,1,0:T(8,128)(2,1)S(1)}, bf16[8,256,512]{2,1,0:T(8,128)(2,1)S(1)}, f32[1,512]{1,0:T(1,128)S(1)}) custom-call(f32[4]{0:T(128)S(1)} %pad_maximum_fusion.4.refs_0_, s32[8]{0:T(128)S(1)} %get-tuple-element.24.refs_1_, bf16[9,2,256,256]{3,2,1,0:T(8,128)(2,1)S(1)} %maximum_select_fusion.refs_2_, ...), custom_call_target="tpu_custom_call" | custom-call | flops 10737418240 | bytes 16777216 | tf_op jit(solution)/shard_map/pallas_call | solution.py:221
  129.5 1.8 broadcast_select_fusion.3
  131.5 1.8 collective-permute-start.6
  138.9 8.7 %collective-permute-start.5 = (bf16[1,256,512]{2,1,0:T(8,128)(2,1)S(1)}, bf16[1,256,512]{2,1,0:T(8,128)(2,1)S(1)}, u32[]{:S(2)}, u32[]{:S(2)}) collective-permute-start(bf16[1,256,512]{2,1,0:T(8,128)(2,1)S(1)} %slice.105), channel_id=1, source_target_pairs={{0,2},{1,3},{2,5},{4,6},{5,7},{6,9},{8,10},{9,11},{10,13},{12,14},... | collective-permute-start | bytes 786440 | tf_op jit(solution)/shard_map/ppermute | solution.py:257
  147.6 3.0 psum.14
  150.6 2.6 collective-permute-start.3
  153.3 1.7 collective-permute-done.3
  157.6 8.0 %collective-permute-done.4 = f32[1]{0:T(128)} collective-permute-done((f32[1]{0:T(128)}, f32[1]{0:T(128)}, u32[]{:S(2)}, u32[]{:S(2)}) %collective-permute-start.4) | collective-permute-done | bytes 36 | tf_op jit(solution)/shard_map/ppermute | solution.py:257
  166.3 18.7 %collective-permute-done.6 = bf16[8,256,512]{2,1,0:T(8,128)(2,1)} collective-permute-done((bf16[8,256,512]{2,1,0:T(8,128)(2,1)}, bf16[8,256,512]{2,1,0:T(8,128)(2,1)}, u32[]{:S(2)}, u32[]{:S(2)}) %collective-permute-start.6) | collective-permute-done | bytes 2097184 | tf_op jit(solution)/shard_map/ppermute | solution.py:257
  185.0 2.1 broadcast_select_fusion.1
  187.6 62.2 %shard_map.56 = (bf16[8,2,256,256]{3,2,1,0:T(8,128)(2,1)S(1)}, bf16[8,2,256,256]{3,2,1,0:T(8,128)(2,1)S(1)}, f32[1,512]{1,0:T(1,128)S(1)}) custom-call(f32[4]{0:T(128)S(1)} %maximum_multiply_fusion.refs_0_, s32[8]{0:T(128)S(1)} %get-tuple-element.23.refs_1_, bf16[9,256,512]{2,1,0:T(8,128)(2,1)S(1)} %pad_maximum_fusion.2.refs_2_, ...), custom_call_target="tpu_custom_call" | custom-call | flops 10737418240 | bytes 16777216 | tf_op jit(solution)/shard_map/pallas_call | solution.py:221
  249.8 1.8 broadcast_select_fusion
  251.8 6.8 %collective-permute-start.8 = (bf16[8,2,256,256]{3,2,1,0:T(8,128)(2,1)}, bf16[8,2,256,256]{3,2,1,0:T(8,128)(2,1)}, u32[]{:S(2)}, u32[]{:S(2)}) collective-permute-start(bf16[8,2,256,256]{3,2,1,0:T(8,128)(2,1)} %broadcast_select_fusion), channel_id=1, source_target_pairs={{0,30},{1,31},{2,4},{3,5},{4,2},{5,3},{6,8},{7,9},{8,6},{9,7},{10,... | collective-permute-start | bytes 6291464 | tf_op jit(solution)/shard_map/ppermute | solution.py:257
  259.2 3.1 psum.15
  264.8 38.5 %collective-permute-done.9 = f32[1]{0:T(128)} collective-permute-done((f32[1]{0:T(128)}, f32[1]{0:T(128)}, u32[]{:S(2)}, u32[]{:S(2)}) %collective-permute-start.9) | collective-permute-done | bytes 36 | tf_op jit(solution)/shard_map/ppermute | solution.py:257
  309.0 2.8 fusion
  311.8 2.3 copy.15
  (61 shorter events, 21.3 us)
Async XLA Ops:
  4.9 6.3 %copy-start.3 = (bf16[16,2,256,256]{3,2,1,0:T(8,128)(2,1)}, bf16[16,2,256,256]{3,2,1,0:T(8,128)(2,1)S(1)}, u32[]{:S(2)}) copy-start(bf16[16,2,256,256]{3,2,1,0:T(8,128)(2,1)S(1)} %add_select_fusion) | copy-start | bytes 12582916
  4.9 7.0 %copy-start.6 = (f32[1,2,3]{2,1,0:T(2,128)S(1)}, f32[1,2,3]{2,1,0:T(2,128)}, u32[]{:S(2)}) copy-start(f32[1,2,3]{2,1,0:T(2,128)} %param.9) | copy-start | bytes 76
  6.7 54.5 %collective-permute-start.1 = (bf16[9,2,256,256]{3,2,1,0:T(8,128)(2,1)}, bf16[9,2,256,256]{3,2,1,0:T(8,128)(2,1)}, u32[]{:S(2)}, u32[]{:S(2)}) collective-permute-start(bf16[9,2,256,256]{3,2,1,0:T(8,128)(2,1)} %slice_select_fusion), channel_id=1, source_target_pairs={{0,2},{1,3},{2,0},{3,1},{4,6},{5,7},{6,4},{7,5},{8,10},{9,11},{10,... | collective-permute-start | bytes 7077896 | tf_op jit(solution)/shard_map/ppermute | solution.py:257
  9.7 7.5 %collective-permute-start = (bf16[2,256,256]{2,1,0:T(8,128)(2,1)S(1)}, bf16[2,256,256]{2,1,0:T(8,128)(2,1)S(1)}, u32[]{:S(2)}, u32[]{:S(2)}) collective-permute-start(bf16[2,256,256]{2,1,0:T(8,128)(2,1)S(1)} %fusion.1), channel_id=1, source_target_pairs={{0,1},{3,2},{4,5},{7,6},{8,9},{11,10},{12,13},{15,14},{16,17},{19,... | collective-permute-start | bytes 786440 | tf_op jit(solution)/shard_map/ppermute | solution.py:257
  11.2 51.3 %collective-permute-start.2 = (bf16[256,256]{1,0:T(8,128)(2,1)S(1)}, bf16[256,256]{1,0:T(8,128)(2,1)S(1)}, u32[]{:S(2)}, u32[]{:S(2)}) collective-permute-start(bf16[256,256]{1,0:T(8,128)(2,1)S(1)} %slice_bitcast_fusion.4), channel_id=1, source_target_pairs={{2,1},{6,5},{10,9},{14,13},{18,17},{22,21},{26,25},{30,29}} | collective-permute-start | bytes 393224 | tf_op jit(solution)/shard_map/ppermute | solution.py:257
  13.9 3.0 copy-start.5
  13.9 3.2 %copy-start.7 = (s32[1,2,32]{2,1,0:T(2,128)S(1)}, s32[1,2,32]{2,1,0:T(2,128)}, u32[]{:S(2)}) copy-start(s32[1,2,32]{2,1,0:T(2,128)} %param.8) | copy-start | bytes 772
  65.6 1.6 slice-start
  129.5 2.0 copy-start
  131.5 53.5 %collective-permute-start.6 = (bf16[8,256,512]{2,1,0:T(8,128)(2,1)}, bf16[8,256,512]{2,1,0:T(8,128)(2,1)}, u32[]{:S(2)}, u32[]{:S(2)}) collective-permute-start(bf16[8,256,512]{2,1,0:T(8,128)(2,1)} %broadcast_select_fusion.3), channel_id=1, source_target_pairs={{0,4},{1,5},{2,30},{3,31},{4,8},{5,9},{6,2},{7,3},{8,12},{9,13},{1... | collective-permute-start | bytes 6291464 | tf_op jit(solution)/shard_map/ppermute | solution.py:257
  137.0 50.2 %collective-permute-start.7 = (bf16[1,256,512]{2,1,0:T(8,128)(2,1)S(1)}, bf16[1,256,512]{2,1,0:T(8,128)(2,1)S(1)}, u32[]{:S(2)}, u32[]{:S(2)}) collective-permute-start(bf16[1,256,512]{2,1,0:T(8,128)(2,1)S(1)} %slice.106), channel_id=1, source_target_pairs={{1,30},{2,0},{3,1},{5,2},{6,4},{7,5},{9,6},{10,8},{11,9},{13,10},{... | collective-permute-start | bytes 786440 | tf_op jit(solution)/shard_map/ppermute | solution.py:257
  138.9 48.5 %collective-permute-start.5 = (bf16[1,256,512]{2,1,0:T(8,128)(2,1)S(1)}, bf16[1,256,512]{2,1,0:T(8,128)(2,1)S(1)}, u32[]{:S(2)}, u32[]{:S(2)}) collective-permute-start(bf16[1,256,512]{2,1,0:T(8,128)(2,1)S(1)} %slice.105), channel_id=1, source_target_pairs={{0,2},{1,3},{2,5},{4,6},{5,7},{6,9},{8,10},{9,11},{10,13},{12,14},... | collective-permute-start | bytes 786440 | tf_op jit(solution)/shard_map/ppermute | solution.py:257
  150.6 4.3 %collective-permute-start.3 = (f32[1]{0:T(128)}, f32[1]{0:T(128)}, u32[]{:S(2)}, u32[]{:S(2)}) collective-permute-start(f32[1]{0:T(128)} %bitcast.26), channel_id=1, source_target_pairs={{0,2},{1,3},{2,0},{3,1},{4,6},{5,7},{6,4},{7,5},{8,10},{9,11},{10,... | collective-permute-start | bytes 20 | tf_op jit(solution)/shard_map/ppermute | solution.py:257
  156.3 9.3 %collective-permute-start.4 = (f32[1]{0:T(128)}, f32[1]{0:T(128)}, u32[]{:S(2)}, u32[]{:S(2)}) collective-permute-start(f32[1]{0:T(128)} %bitcast.28), channel_id=1, source_target_pairs={{2,4},{3,5},{6,8},{7,9},{10,12},{11,13},{14,16},{15,17},{18,20},{1... | collective-permute-start | bytes 20 | tf_op jit(solution)/shard_map/ppermute | solution.py:257
  249.8 2.0 copy-start.1
  251.8 52.8 %collective-permute-start.8 = (bf16[8,2,256,256]{3,2,1,0:T(8,128)(2,1)}, bf16[8,2,256,256]{3,2,1,0:T(8,128)(2,1)}, u32[]{:S(2)}, u32[]{:S(2)}) collective-permute-start(bf16[8,2,256,256]{3,2,1,0:T(8,128)(2,1)} %broadcast_select_fusion), channel_id=1, source_target_pairs={{0,30},{1,31},{2,4},{3,5},{4,2},{5,3},{6,8},{7,9},{8,6},{9,7},{10,... | collective-permute-start | bytes 6291464 | tf_op jit(solution)/shard_map/ppermute | solution.py:257
  262.3 41.0 %collective-permute-start.9 = (f32[1]{0:T(128)}, f32[1]{0:T(128)}, u32[]{:S(2)}, u32[]{:S(2)}) collective-permute-start(f32[1]{0:T(128)} %bitcast.33), channel_id=1, source_target_pairs={{0,30},{1,31},{2,4},{3,5},{4,2},{5,3},{6,8},{7,9},{8,6},{9,7},{10,... | collective-permute-start | bytes 20 | tf_op jit(solution)/shard_map/ppermute | solution.py:257
  263.0 44.4 %collective-permute-start.10 = (bf16[1,256,256]{2,1,0:T(8,128)(2,1)}, bf16[1,256,256]{2,1,0:T(8,128)(2,1)S(1)}, u32[]{:S(2)}, u32[]{:S(2)}) collective-permute-start(bf16[1,256,256]{2,1,0:T(8,128)(2,1)} %slice_bitcast_fusion.6), channel_id=1, source_target_pairs={{1,30},{5,2},{9,6},{13,10},{17,14},{21,18},{25,22},{29,26}} | collective-permute-start | bytes 393224 | tf_op jit(solution)/shard_map/ppermute | solution.py:257
  264.8 42.4 %copy-start.4 = (bf16[8,256,256]{2,1,0:T(8,128)(2,1)S(1)}, bf16[8,256,256]{2,1,0:T(8,128)(2,1)}, u32[]{:S(2)}) copy-start(bf16[8,256,256]{2,1,0:T(8,128)(2,1)} %get-tuple-element.17) | copy-start | bytes 3145732
  307.4 1.6 copy-start.2

commit v2 on v1

v2 whole, which is shorter than its diff:
```python
import math

import jax
import jax.numpy as jnp
from jax import lax
from jax.experimental import pallas as pl
from jax.experimental.pallas import tpu as pltpu
from jax.sharding import PartitionSpec as P

tau_step = 0.5
SUB = 8
LANES = 128
PANEL = 32
PART = 8
UNROLL = 2
FIRST = (((0,), (0,)), ((), ()))
LAST = (((1,), (1,)), ((), ()))
PLAIN = (((1,), (0,)), ((), ()))


def gate_terms(coupling):
    hopping = coupling[0]
    ising_term = coupling[1]
    field_term = coupling[2]
    rotation = 0.5 * tau_step * hopping
    middle_scale = jnp.exp(0.25 * tau_step * ising_term)
    weight_empty = jnp.exp(-tau_step * (0.25 * ising_term - 0.5 * field_term))
    weight_full = jnp.exp(-tau_step * (0.25 * ising_term + 0.5 * field_term))
    weight_stay = middle_scale * jnp.cosh(rotation)
    weight_swap = -middle_scale * jnp.sinh(rotation)
    return jnp.stack([weight_empty, weight_stay, weight_swap, weight_full])


def local_mask(site_block, sizes_row, first_sector):
    sector_count = site_block.shape[0]
    block_width = site_block.shape[-1]
    right_ext = jnp.concatenate([sizes_row[1], jnp.zeros((1,), jnp.int32)])
    left_here = lax.dynamic_slice_in_dim(sizes_row[0], first_sector, sector_count)
    right_here = lax.dynamic_slice_in_dim(right_ext, first_sector, sector_count)
    right_next = lax.dynamic_slice_in_dim(right_ext, first_sector + 1, sector_count)
    row_index = jnp.arange(block_width, dtype=jnp.int32)
    row_keep = row_index[None, :] < left_here[:, None]
    col_stay = row_index[None, :] < right_here[:, None]
    col_next = row_index[None, :] < right_next[:, None]
    keep_zero = row_keep[:, :, None] & col_stay[:, None, :]
    keep_one = row_keep[:, :, None] & col_next[:, None, :]
    keep_both = jnp.stack([keep_zero, keep_one], axis=1)
    return jnp.where(keep_both, site_block, jnp.zeros_like(site_block))


def dot(left, right, dims):
    return lax.dot_general(left, right, dims, preferred_element_type=jnp.float32)


def spread(row, lane_index):
    return jnp.take_along_axis(row, lane_index, axis=1)


def refined_reciprocal(value):
    guess = pltpu.reciprocal(value, approx=True)
    return guess * (2.0 - value * guess)


def factor_panel(rows_ref, first, tile):
    lanes = rows_ref.shape[0] * LANES
    lane = lax.broadcasted_iota(jnp.int32, (SUB, lanes), 1)
    zero = jnp.zeros((SUB, LANES), jnp.int32)
    mine = slice(tile * LANES, (tile + 1) * LANES)
    stop = first + PANEL
    inside = (lane >= first) & (lane < stop)

    def load(index):
        at = slice(index * SUB, (index + 1) * SUB)
        return jnp.concatenate([rows_ref[half, at, :] for half in range(lanes // LANES)], axis=1)

    def wide(value):
        return jnp.concatenate([value] * (lanes // LANES), axis=1)

    def store(index, value):
        at = slice(index * SUB, (index + 1) * SUB)
        for half in range(lanes // LANES):
            rows_ref[half, at, :] = value[:, half * LANES : (half + 1) * LANES]

    for start in range(0, PANEL, PART):
        rows = [load(start + i) for i in range(PART)]
        base = first - tile * LANES + start
        entry = [
            [spread(rows[i][:, mine], base + j + zero) if j >= i else None for j in range(PART)]
            for i in range(PART)
        ]
        later = []
        for step in range(PART):
            k = first + start + step
            inverted = refined_reciprocal(entry[step][step])
            unit = jnp.where(lane == k, 1.0, rows[step])
            for other in range(step + 1, PART):
                ratio = entry[step][other] * inverted
                for column in range(other, PART):
                    entry[other][column] = entry[other][column] - ratio * entry[step][column]
                rows[other] = jnp.where(lane == k, 0.0, rows[other]) - wide(ratio) * unit
            done = jnp.where((lane > k) & (lane < stop), 0.0, unit)
            store(start + step, done * wide(lax.rsqrt(entry[step][step])))
            hidden = jnp.where((lane > k) & (lane < first + start + PART), 0.0, unit)
            later.append(hidden * wide(inverted))
        for i in range(start + PART, PANEL):
            hide = (lane >= first + start) & (lane < first + start + PART)
            row = jnp.where(hide, 0.0, load(i))
            for step in range(PART):
                row = row - wide(spread(rows[step][:, mine], first - tile * LANES + i + zero)) * later[step]
            store(i, row)


def in_parts(value):
    high = value.astype(jnp.bfloat16)
    rest = value - high.astype(jnp.float32)
    middle = rest.astype(jnp.bfloat16)
    return high, middle, (rest - middle.astype(jnp.float32)).astype(jnp.bfloat16)


def pair_kernel(
    second,
    weights,
    ranks,
    left_ref,
    right_ref,
    sketch_ref,
    basis_ref,
    coef_ref,
    norm_ref,
    two_ref,
    sample_ref,
    gram_ref,
    inverse_ref,
    rows_ref,
):
    count, kept, double = sample_ref.shape
    width = double // 2
    row_index = lax.broadcasted_iota(jnp.int32, (kept, 1), 0)
    eye = (
        lax.broadcasted_iota(jnp.int32, (kept, kept), 0)
        == lax.broadcasted_iota(jnp.int32, (kept, kept), 1)
    )

    def left(m, s):
        if second:
            return left_ref[m, :, s * width : (s + 1) * width]
        return left_ref[m, s]

    def right(m, s):
        if second:
            return right_ref[m, :, s * width : (s + 1) * width]
        return right_ref[m, s]

    def product(a, b):
        rounded = dot(a, b, LAST if second else PLAIN).astype(jnp.bfloat16)
        return rounded.astype(jnp.float32)

    w_empty, w_stay, w_swap, w_full = weights[0], weights[1], weights[2], weights[3]

    @pl.loop(0, count, unroll=UNROLL)
    def _(m):
        below_zero, below_one = left(m, 0), left(m, 1)
        here_zero, here_one = left(m + 1, 0), left(m + 1, 1)
        same_zero, same_one = right(m, 0), right(m, 1)
        next_zero, next_one = right(m + 1, 0), right(m + 1, 1)
        low, high = slice(0, width), slice(width, double)
        two_ref[m, low, low] = (w_empty * product(here_zero, same_zero)).astype(jnp.bfloat16)
        two_ref[m, low, high] = (
            w_stay * product(here_zero, next_one) + w_swap * product(here_one, next_zero)
        ).astype(jnp.bfloat16)
        two_ref[m, high, low] = (
            w_swap * product(below_zero, same_one) + w_stay * product(below_one, same_zero)
        ).astype(jnp.bfloat16)
        two_ref[m, high, high] = (w_full * product(below_one, next_one)).astype(jnp.bfloat16)
        sample = dot(sketch_ref[...], two_ref[m], LAST)
        keep = row_index < ranks[m]
        sample = jnp.where(keep, sample, 0.0)
        sample_ref[m] = sample
        high_part, middle_part, low_part = in_parts(sample)
        cross = dot(high_part, middle_part, LAST) + dot(high_part, low_part, LAST)
        gram = dot(high_part, high_part, LAST) + (
            dot(middle_part, middle_part, LAST) + (cross + jnp.transpose(cross))
        )
        gram_ref[m] = gram + jnp.where(eye & jnp.logical_not(keep), 1.0, 0.0)

    lane = lax.broadcasted_iota(jnp.int32, (1, kept), 1)
    for tile in range(kept // LANES):
        @pl.loop(0, LANES // PANEL)
        def _(panel):
            first = pl.multiple_of(tile * LANES + panel * PANEL, PANEL)
            here = pl.ds(first, PANEL)
            stop = first + PANEL
            for m in range(count):
                for half in range(kept // LANES):
                    span = slice(half * LANES, (half + 1) * LANES)
                    rows_ref[half, pl.ds(m, PANEL, stride=SUB), :] = gram_ref[m, here, span]
            factor_panel(rows_ref, first, tile)
            for m in range(count):
                solved = jnp.concatenate(
                    [
                        rows_ref[half, pl.ds(m, PANEL, stride=SUB), :]
                        for half in range(kept // LANES)
                    ],
                    axis=1,
                )
                inverse_ref[m, here, :] = jnp.where(lane < stop, solved, 0.0)
                high, middle, low = in_parts(solved)
                one = jnp.concatenate([high, high, middle, middle, high, low], axis=0)
                two = jnp.concatenate([high, middle, high, middle, low, high], axis=0)
                change = dot(one, two, FIRST)
                kept_part = jnp.where((lane >= first) & (lane < stop), 0.0, gram_ref[m])
                gram_ref[m] = kept_part - change

    norm_ref[...] = jnp.zeros_like(norm_ref)

    @pl.loop(0, count, unroll=UNROLL)
    def _(m):
        inverse_high, inverse_middle, _ = in_parts(inverse_ref[m])
        sample_high, sample_middle, _ = in_parts(sample_ref[m])
        solved = dot(inverse_high, sample_high, PLAIN) + (
            dot(inverse_high, sample_middle, PLAIN) + dot(inverse_middle, sample_high, PLAIN)
        )
        solved = solved * math.sqrt(width)
        basis = solved.astype(jnp.bfloat16)
        if second:
            for s in range(2):
                turned = jnp.transpose(solved[:, s * width : (s + 1) * width])
                basis_ref[m, s] = turned.astype(jnp.bfloat16)
        else:
            basis_ref[m] = basis
        coef = dot(basis, two_ref[m], PLAIN)
        norm_ref[...] += jnp.sum(coef * coef, axis=0, keepdims=True)
        rounded = coef.astype(jnp.bfloat16)
        if second:
            for s in range(2):
                coef_ref[m, s] = rounded[:, s * width : (s + 1) * width]
        else:
            coef_ref[m] = rounded


def pair_update(second, weights, ranks, left, right, sketch_turned):
    count = ranks.shape[0]
    kept, double = sketch_turned.shape
    width = double // 2
    shape = (count, 2, width, kept) if second else (count, kept, double)
    coef_shape = (count, 2, kept, width) if second else (count, kept, double)
    vmem = pl.BlockSpec(memory_space=pltpu.VMEM)
    smem = pl.BlockSpec(memory_space=pltpu.SMEM)

    def kernel(*refs):
        pair_kernel(second, *refs)

    basis, coef, norm = pl.pallas_call(
        kernel,
        out_shape=(
            jax.ShapeDtypeStruct(shape, jnp.bfloat16),
            jax.ShapeDtypeStruct(coef_shape, jnp.bfloat16),
            jax.ShapeDtypeStruct((1, double), jnp.float32),
        ),
        in_specs=[smem, smem, vmem, vmem, vmem],
        out_specs=(vmem, vmem, vmem),
        scratch_shapes=[
            pltpu.VMEM((count, double, double), jnp.bfloat16),
            pltpu.VMEM((count, kept, double), jnp.float32),
            pltpu.VMEM((count, kept, kept), jnp.float32),
            pltpu.VMEM((count, kept, kept), jnp.float32),
            pltpu.VMEM((kept // LANES, PANEL * SUB, LANES), jnp.float32),
        ],
        compiler_params=pltpu.CompilerParams(vmem_limit_bytes=40 * 2**20),
        cost_estimate=pl.CostEstimate(
            flops=count * 20 * kept * double * double,
            bytes_accessed=8 * count * kept * double * 2,
            transcendentals=0,
        ),
    )(weights, ranks, left, right, sketch_turned)
    return basis, coef, jnp.sum(norm)


def move(value, target_of):
    sites, parts = lax.axis_size("chain"), lax.axis_size("block")
    pairs = []
    for site in range(sites):
        for part in range(parts):
            target = target_of(site, part)
            if target is not None and 0 <= target[1] < parts:
                pairs.append((site * parts + part, (target[0] % sites) * parts + target[1]))
    return lax.ppermute(value, ("chain", "block"), pairs)


def by_parity(even_target, odd_target):
    return lambda c, b: even_target(c, b) if c % 2 == 0 else odd_target(c, b)


def nowhere(c, b):
    return None


def joined(*parts):
    return jnp.concatenate(parts, axis=0)


def body(site_tensors, sketch, bond_sizes, kept_ranks, couplings):
    sectors = site_tensors.shape[1]
    half = sectors // 2
    early = half // 2
    width = site_tensors.shape[-1]
    kept = sketch.shape[1]
    parts = lax.axis_size("block")
    first_sector = lax.axis_index("block") * sectors
    is_even = lax.axis_index("chain") % 2 == 0
    first_here = first_sector + jnp.where(is_even, 0, half)

    def pick(even_value, odd_value):
        return jnp.where(is_even, even_value, odd_value)

    def bond(row):
        ranks = lax.dynamic_slice(kept_ranks[0], (row, first_here), (1, half))[0]
        weights = gate_terms(lax.dynamic_index_in_dim(couplings[0], row, 0, keepdims=False))
        return ranks[:early], ranks[early:], weights

    own = local_mask(site_tensors[0], bond_sizes[0], first_sector)
    sketch_turned = jnp.transpose(sketch)

    across = by_parity(lambda c, b: (c + 1, b), lambda c, b: (c - 1, b))
    sent = pick(own[half - 1 : half + early], own[: early + 1])
    got_early = move(sent, across)
    edge = move(
        pick(own[-1], own[0]), by_parity(lambda c, b: (c, b + 1), lambda c, b: (c, b - 1))
    )
    corner = move(own[-1:, 1], by_parity(nowhere, lambda c, b: (c - 1, b + 1)))
    sent = pick(own[half + early :], own[early + 1 : half + 1])
    sent, got_early = lax.optimization_barrier((sent, got_early))
    got_late = move(sent, across)
    ranks_early, ranks_late, weights = bond(pick(1, 0))

    left = pick(joined(edge[None], own[:early]), got_early)
    right_zero = pick(got_early[:, 0], own[half : half + early + 1, 0])
    right_one = pick(joined(corner, got_early[:early, 1]), own[half - 1 : half + early, 1])
    right = jnp.stack([right_zero, right_one], axis=1)
    basis_early, coef_early, norm_early = pair_update(
        False, weights, ranks_early, left, right, sketch_turned
    )

    along = by_parity(lambda c, b: (c + 2, b), lambda c, b: (c - 2, b))
    carried_early = move(pick(coef_early, basis_early), along)
    basis_above = move(
        basis_early[:1], by_parity(lambda c, b: (c - 1, b - 1), lambda c, b: (c - 1, b))
    )

    left = pick(own[early - 1 : half], joined(got_early[early:], got_late))
    right_zero = pick(
        joined(got_early[early:, 0], got_late[:, 0]), joined(own[half + early :, 0], edge[:1])
    )
    right_one = pick(
        joined(got_early[early - 1 :, 1], got_late[: half - early - 1, 1]),
        own[half + early - 1 :, 1],
    )
    right = jnp.stack([right_zero, right_one], axis=1)
    basis_late, coef_late, norm_late = pair_update(
        False, weights, ranks_late, left, right, sketch_turned
    )
    norm_even = norm_early + norm_late

    sent = pick(coef_late, basis_late)
    carried_next = move(sent[:1], along)
    coef_below = move(
        coef_late[-1:], by_parity(lambda c, b: (c + 1, b), lambda c, b: (c + 1, b + 1))
    )
    carried_late = move(sent[1:], along)

    ranks_early, ranks_late, weights = bond(pick(0, 1))
    left = joined(coef_below, pick(carried_early, coef_early))
    right = pick(joined(basis_early, basis_late[:1]), joined(carried_early, carried_next))
    new_basis_early, new_coef_early, norm_early = pair_update(
        True, weights, ranks_early, left, right, sketch_turned
    )
    back = by_parity(lambda c, b: (c - 1, b), lambda c, b: (c + 1, b))
    returned_early = move(pick(new_basis_early, new_coef_early), back)
    lower_above = move(
        new_basis_early[:1, 1], by_parity(lambda c, b: (c - 1, b - 1), nowhere)
    )

    left = pick(
        joined(carried_early[-1:], carried_next, carried_late), joined(coef_early[-1:], coef_late)
    )
    right = joined(pick(basis_late, joined(carried_next, carried_late)), basis_above)
    new_basis_late, new_coef_late, norm_late = pair_update(
        True, weights, ranks_late, left, right, sketch_turned
    )
    returned_late = move(pick(new_basis_late, new_coef_late), back)

    norms = lax.psum(jnp.stack([norm_even, norm_early + norm_late]), "block")
    from_left = move(norms, by_parity(nowhere, lambda c, b: (c + 1, b)))
    from_second = move(norms[:1], by_parity(lambda c, b: (c + 2, b), nowhere))
    target = float(sectors * parts * kept * width)
    scale = jnp.sqrt(target / (from_left[0] + from_second[0]))
    scale = scale * jnp.sqrt(target / (scale * scale * (norms[1] + from_left[1])))

    new_left = jnp.stack(
        [
            joined(returned_early[:, 0], returned_late[:, 0], new_basis_early[:, 0], new_basis_late[:, 0]),
            joined(
                returned_early[1:, 1],
                returned_late[:, 1],
                new_basis_early[:, 1],
                new_basis_late[:, 1],
                lower_above,
            ),
        ],
        axis=1,
    )
    new_right = joined(new_coef_early, new_coef_late, returned_early, returned_late)
    new_right = (new_right.astype(jnp.float32) * scale).astype(jnp.bfloat16)
    return pick(new_right, new_left)[None]


def solution(mesh):
    placed = (
        P("chain", "block", None, None, None),
        P(),
        P("chain", None, None),
        P("chain", None, None),
        P("chain", None, None),
    )
    return jax.shard_map(
        body,
        mesh=mesh,
        in_specs=placed,
        out_specs=P("chain", "block", None, None, None),
        check_vma=False,
    )
```

time: 318 us -> 248 us (0.78)
  Pallas kernels: 124 us -> 76.8 us
  waiting for transfers between devices: 111 us -> 63.8 us
  local copies, waits for them, and re-layouts: 15.1 us -> 32.6 us
  other arithmetic: 20.3 us -> 31.2 us
  blocking collectives: 6.07 us -> 2.44 us
    pallas_call x2 -> x4, Pallas kernels: 124 us -> 76.8 us  [pair_update(): pl.pallas_call(kernel, out_shape=(jax.ShapeDtypeStruct(shape, jnp.bfloat1...]
    ppermute x11 -> x14, waiting for transfers between devices: 111 us -> 63.8 us  [move(): return lax.ppermute(value, ('chain', 'block'), pairs)]
    unnamed x17 -> x45, local copies, waits for them, and re-layouts: 1.86 us -> 11 us
    slice x6 -> x20, local copies, waits for them, and re-layouts: 4.93 us -> 12.9 us  [the longest x1 2.1 us: body(): left = pick(joined(edge[None], own[:early]), got_early)]
    select_n x9 -> x15, other arithmetic: 13.9 us -> 17.5 us  [pick(): return jnp.where(is_even, even_value, odd_value)]
    psum x2 -> x1, blocking collectives: 6.07 us -> 2.44 us  [body(): norms = lax.psum(jnp.stack([norm_even, norm_early + norm_late]), 'block')]
    concatenate x2, other arithmetic: 0.41 us -> 3.61 us  [joined(): return jnp.concatenate(parts, axis=0)]
    ppermute x11 -> x14, starting transfers between devices: 28.3 us -> 29.5 us  [move(): return lax.ppermute(value, ('chain', 'block'), pairs)]
  transfers between devices with their start and end apart: 11 -> 14, of which waited for: 5 -> 4; matrix products, arithmetic and copies ran while one was open for 4% -> 15% of each run, Pallas kernels for 0% -> 15%
where the time goes in v2:
time: 248 us; the launch traced here: 247 us
  Pallas kernels  76.8 us (31%)
  waiting for transfers between devices  63.8 us (26%)
  local copies, waits for them, and re-layouts  32.6 us (13%)
  other arithmetic  31.2 us (13%)
  starting transfers between devices  29.5 us (12%)
  between operations  11 us (4%)
    pallas_call x4, Pallas kernels, pair_update(): pl.pallas_call(kernel, out_shape=(jax.ShapeDtypeStruct(shape, jnp.bfloat1...  76.8 us
    ppermute x14, waiting for transfers between devices, move(): return lax.ppermute(value, ('chain', 'block'), pairs)  63.8 us
    ppermute x14, starting transfers between devices, move(): return lax.ppermute(value, ('chain', 'block'), pairs)  29.5 us
    select_n x15, other arithmetic, pick(): return jnp.where(is_even, even_value, odd_value)  17.5 us
    unnamed x45, local copies, waits for them, and re-layouts  11 us
  transfers between devices with their start and end apart: 14, of which 4 were waited for; matrix products, arithmetic and copies ran while one was open for 15% of the time, Pallas kernels for 15%

profile of v2, /device:TPU:0, one launch (start us, length us, event | category | flops | bytes accessed | tf_op | source)
XLA Modules:
  0.0 247.3 jit_solution(868563631904602689)
XLA Ops:
  2.4 2.5 %add_select_fusion = bf16[16,2,256,256]{3,2,1,0:T(8,128)(2,1)S(1)} fusion(pred[16,1,256,256]{3,2,1,0:T(8,128)(4,1)S(1)} %get-tuple-element.44, pred[16,1,256,256]{3,2,1,0:T(8,128)(4,1)S(1)} %get-tuple-element.43, bf16[1,16,2,256,256]{4,3,2,1,0:T(8,128)(2,1)} %param.5), kind=kLoop, calls=%fused_computation.1 | loop fusion | flops 4194304 | bytes 10485760 | tf_op jit(solution)/shard_map/jit(_where)/select_n | solution.py:48
  4.9 2.0 copy-done.5
  9.4 3.0 %collective-permute-start.2 = (bf16[2,256,256]{2,1,0:T(8,128)(2,1)S(1)}, bf16[2,256,256]{2,1,0:T(8,128)(2,1)S(1)}, u32[]{:S(2)}, u32[]{:S(2)}) collective-permute-start(bf16[2,256,256]{2,1,0:T(8,128)(2,1)S(1)} %fusion.5), channel_id=1, source_target_pairs={{0,1},{3,2},{4,5},{7,6},{8,9},{11,10},{12,13},{15,14},{16,17},{19,... | collective-permute-start | bytes 786440 | tf_op jit(solution)/shard_map/ppermute | solution.py:287
  12.4 2.9 %slice_select_fusion = bf16[5,2,256,256]{3,2,1,0:T(8,128)(2,1)} fusion(bf16[16,2,256,256]{3,2,1,0:T(8,128)(2,1)} %copy-done.5, pred[]{:T(512)S(6)} %eq.5), kind=kLoop, calls=%fused_computation.8 | loop fusion | flops 655360 | bytes 3932161 | tf_op jit(solution)/shard_map/jit(_where)/select_n | solution.py:314
  20.7 2.1 fusion.7
  28.0 18.9 %collective-permute-done = bf16[5,2,256,256]{3,2,1,0:T(8,128)(2,1)S(1)} collective-permute-done((bf16[5,2,256,256]{3,2,1,0:T(8,128)(2,1)}, bf16[5,2,256,256]{3,2,1,0:T(8,128)(2,1)S(1)}, u32[]{:S(2)}, u32[]{:S(2)}) %collective-permute-start) | collective-permute-done | bytes 1310752 | tf_op jit(solution)/shard_map/ppermute | solution.py:287
  51.4 19.1 %shard_map.56 = (bf16[4,256,512]{2,1,0:T(8,128)(2,1)S(1)}, bf16[4,256,512]{2,1,0:T(8,128)(2,1)S(1)}, f32[1,512]{1,0:T(1,128)S(1)}) custom-call(f32[4]{0:T(128)S(1)} %pad_maximum_fusion.5.refs_0_, s32[4]{0:T(128)S(1)} %get-tuple-element.57.refs_1_, bf16[5,2,256,256]{3,2,1,0:T(8,128)(2,1)S(1)} %maximum_select_fusion.refs_2_, ...), custom_call_target="tpu_custom_call" | custom-call | flops 5368709120 | bytes 8388608 | tf_op jit(solution)/shard_map/pallas_call | solution.py:253
  71.6 2.1 collective-permute-start.5
  75.4 19.1 %shard_map.55 = (bf16[4,256,512]{2,1,0:T(8,128)(2,1)S(1)}, bf16[4,256,512]{2,1,0:T(8,128)(2,1)S(1)}, f32[1,512]{1,0:T(1,128)S(1)}) custom-call(f32[4]{0:T(128)S(1)} %pad_maximum_fusion.5.refs_0_, s32[4]{0:T(128)S(1)} %get-tuple-element.58.refs_1_, bf16[5,2,256,256]{3,2,1,0:T(8,128)(2,1)S(1)} %slice_select_fusion.1.refs_2_, ...), custom_call_target="tpu_custom_call" | custom-call | flops 5368709120 | bytes 8388608 | tf_op jit(solution)/shard_map/pallas_call | solution.py:253
  104.1 7.4 %collective-permute-start.3 = (bf16[1,256,512]{2,1,0:T(8,128)(2,1)}, bf16[1,256,512]{2,1,0:T(8,128)(2,1)}, u32[]{:S(2)}, u32[]{:S(2)}) collective-permute-start(bf16[1,256,512]{2,1,0:T(8,128)(2,1)} %slice.206), channel_id=1, source_target_pairs={{0,2},{1,3},{2,5},{4,6},{5,7},{6,9},{8,10},{9,11},{10,13},{12,14},... | collective-permute-start | bytes 786440 | tf_op jit(solution)/shard_map/ppermute | solution.py:287
  111.5 2.3 broadcast_select_fusion.2
  117.3 2.4 pad_maximum_fusion.2.refs_2_
  119.7 6.5 %collective-permute-done.6 = bf16[1,256,512]{2,1,0:T(8,128)(2,1)} collective-permute-done((bf16[1,256,512]{2,1,0:T(8,128)(2,1)}, bf16[1,256,512]{2,1,0:T(8,128)(2,1)}, u32[]{:S(2)}, u32[]{:S(2)}) %collective-permute-start.6) | collective-permute-done | bytes 262176 | tf_op jit(solution)/shard_map/ppermute | solution.py:287
  129.0 2.7 %maximum_select_fusion.1 = (bf16[5,256,512]{2,1,0:T(8,128)(2,1)}, bf16[5,256,512]{2,1,0:T(8,128)(2,1)S(1)}) fusion(bf16[1,256,512]{2,1,0:T(8,128)(2,1)S(1)} %copy-done.16, bf16[4,256,512]{2,1,0:T(8,128)(2,1)S(1)} %get-tuple-element.23, bf16[1,256,512]{2,1,0:T(8,128)(2,1)} %collective-permute-done.6, bf16[4,256,512]{2,1,0:T(8,128)(2,1)} %collective-permute-done.5, ...), kind=kLoop, calls=%fused_computation.14 | loop fusion | flops 4587520 | bytes 7602177 | tf_op jit(solution)/shard_map/jit(_where)/select_n | solution.py:314
  131.7 19.2 %shard_map.58 = (bf16[4,2,256,256]{3,2,1,0:T(8,128)(2,1)S(1)}, bf16[4,2,256,256]{3,2,1,0:T(8,128)(2,1)S(1)}, f32[1,512]{1,0:T(1,128)S(1)}) custom-call(f32[4]{0:T(128)S(1)} %pad_maximum_fusion.4.refs_0_, s32[4]{0:T(128)S(1)} %get-tuple-element.56.refs_1_, bf16[5,256,512]{2,1,0:T(8,128)(2,1)S(1)} %get-tuple-element.42.refs_2_, ...), custom_call_target="tpu_custom_call" | custom-call | flops 5368709120 | bytes 8388608 | tf_op jit(solution)/shard_map/pallas_call | solution.py:253
  154.3 19.2 %shard_map.57 = (bf16[4,2,256,256]{3,2,1,0:T(8,128)(2,1)S(1)}, bf16[4,2,256,256]{3,2,1,0:T(8,128)(2,1)S(1)}, f32[1,512]{1,0:T(1,128)S(1)}) custom-call(f32[4]{0:T(128)S(1)} %pad_maximum_fusion.4.refs_0_, s32[4]{0:T(128)S(1)} %get-tuple-element.55.refs_1_, bf16[5,256,512]{2,1,0:T(8,128)(2,1)S(1)} %copy-done.2, bf16[5,256,512]{2,1,0:T(8,128)(2,1)S(1)} %copy-done.3, ...), custom_call_target="tpu_custom_call" | custom-call | flops 5368709120 | bytes 8388608 | tf_op jit(solution)/shard_map/pallas_call | solution.py:253
  176.5 2.4 psum.7
  180.8 2.2 collective-permute-start.12
  183.0 2.8 %fusion.8 = (bf16[4,2,256,256]{3,2,0,1:T(8,128)(2,1)S(1)}, bf16[4,2,256,256]{3,2,0,1:T(8,128)(2,1)}, bf16[1,4,2,256,256]{4,3,1,2,0:T(8,128)(2,1)}) fusion(bf16[4,2,256,256]{3,2,1,0:T(8,128)(2,1)S(1)} %get-tuple-element.27, bf16[4,2,256,256]{3,2,1,0:T(8,128)(2,1)} %copy-done.4, pred[]{:T(512)S(6)} %eq.5), kind=kLoop, calls=%fused_computation.68 | loop fusion | flops 524288 | bytes 5242881 | tf_op jit(solution)/shard_map/pallas_call | solution.py:253
  185.8 5.3 %collective-permute-start.9 = (bf16[4,2,256,256]{3,2,0,1:T(8,128)(2,1)}, bf16[4,2,256,256]{3,2,0,1:T(8,128)(2,1)}, u32[]{:S(2)}, u32[]{:S(2)}) collective-permute-start(bf16[4,2,256,256]{3,2,0,1:T(8,128)(2,1)} %get-tuple-element.39), channel_id=1, source_target_pairs={{0,30},{1,31},{2,4},{3,5},{4,2},{5,3},{6,8},{7,9},{8,6},{9,7},{10,... | collective-permute-start | bytes 3145736 | tf_op jit(solution)/shard_map/ppermute | solution.py:287
  198.0 17.7 %collective-permute-done.9 = bf16[4,2,256,256]{3,2,0,1:T(8,128)(2,1)} collective-permute-done((bf16[4,2,256,256]{3,2,0,1:T(8,128)(2,1)}, bf16[4,2,256,256]{3,2,0,1:T(8,128)(2,1)}, u32[]{:S(2)}, u32[]{:S(2)}) %collective-permute-start.9) | collective-permute-done | bytes 1048608 | tf_op jit(solution)/shard_map/ppermute | solution.py:287
  216.8 20.7 %collective-permute-done.10 = bf16[4,2,256,256]{3,2,1,0:T(8,128)(2,1)} collective-permute-done((bf16[4,2,256,256]{3,2,1,0:T(8,128)(2,1)}, bf16[4,2,256,256]{3,2,1,0:T(8,128)(2,1)}, u32[]{:S(2)}, u32[]{:S(2)}) %collective-permute-start.10) | collective-permute-done | bytes 1048608 | tf_op jit(solution)/shard_map/ppermute | solution.py:287
  242.1 2.8 %fusion = bf16[1,16,2,256,256]{4,3,1,2,0:T(8,128)(2,1)S(1)} fusion(bf16[1,4,2,256,256]{4,3,1,2,0:T(8,128)(2,1)} %bitcast.36, bf16[1,4,2,256,256]{4,3,1,2,0:T(8,128)(2,1)S(1)} %copy-done.10, bf16[1,16,1,256,256]{4,3,1,2,0:T(8,128)(2,1)S(1)} %bitcast.102, bf16[1,16,1,256,256]{4,3,1,2,0:T(8,128)(2,1)S(1)} %maximum_bitcast_fusion, f32[]{:T(128)S(6)} %mul.108, ...), kind=kLoop, calls=%fused_computation.2 | loop fusion | flops 31457280 | bytes 12582917 | tf_op jit(solution)/shard_map/jit(_where)/select_n | solution.py:314
  245.0 2.3 copy.49
  (123 shorter events, 48.4 us)
Async XLA Ops:
  7.6 41.5 %collective-permute-start.4 = (bf16[1,256,256]{2,1,0:T(8,128)(2,1)}, bf16[1,256,256]{2,1,0:T(8,128)(2,1)S(1)}, u32[]{:S(2)}, u32[]{:S(2)}) collective-permute-start(bf16[1,256,256]{2,1,0:T(8,128)(2,1)} %slice_bitcast_fusion.11), channel_id=1, source_target_pairs={{2,1},{6,5},{10,9},{14,13},{18,17},{22,21},{26,25},{30,29}} | collective-permute-start | bytes 393224 | tf_op jit(solution)/shard_map/ppermute | solution.py:287
  9.3 7.8 %copy-start.18 = (f32[1,2,3]{2,1,0:T(2,128)S(1)}, f32[1,2,3]{2,1,0:T(2,128)}, u32[]{:S(2)}) copy-start(f32[1,2,3]{2,1,0:T(2,128)} %param.9) | copy-start | bytes 76
  9.3 7.8 %copy-start.19 = (s32[1,2,32]{2,1,0:T(2,128)S(1)}, s32[1,2,32]{2,1,0:T(2,128)}, u32[]{:S(2)}) copy-start(s32[1,2,32]{2,1,0:T(2,128)} %param.8) | copy-start | bytes 772
  9.4 18.6 %collective-permute-start.2 = (bf16[2,256,256]{2,1,0:T(8,128)(2,1)S(1)}, bf16[2,256,256]{2,1,0:T(8,128)(2,1)S(1)}, u32[]{:S(2)}, u32[]{:S(2)}) collective-permute-start(bf16[2,256,256]{2,1,0:T(8,128)(2,1)S(1)} %fusion.5), channel_id=1, source_target_pairs={{0,1},{3,2},{4,5},{7,6},{8,9},{11,10},{12,13},{15,14},{16,17},{19,... | collective-permute-start | bytes 786440 | tf_op jit(solution)/shard_map/ppermute | solution.py:287
  15.3 31.6 %collective-permute-start = (bf16[5,2,256,256]{3,2,1,0:T(8,128)(2,1)}, bf16[5,2,256,256]{3,2,1,0:T(8,128)(2,1)S(1)}, u32[]{:S(2)}, u32[]{:S(2)}) collective-permute-start(bf16[5,2,256,256]{3,2,1,0:T(8,128)(2,1)} %slice_select_fusion), channel_id=1, source_target_pairs={{0,2},{1,3},{2,0},{3,1},{4,6},{5,7},{6,4},{7,5},{8,10},{9,11},{10,... | collective-permute-start | bytes 3932168 | tf_op jit(solution)/shard_map/ppermute | solution.py:287
  22.8 3.9 %copy-start.17 = (bf16[512,256]{1,0:T(8,128)(2,1)S(1)}, bf16[512,256]{1,0:T(8,128)(2,1)}, u32[]{:S(2)}) copy-start(bf16[512,256]{1,0:T(8,128)(2,1)} %param.6) | copy-start | bytes 786436
  46.9 2.2 copy-start.7
  46.9 26.9 %collective-permute-start.1 = (bf16[4,2,256,256]{3,2,0,1:T(8,128)(2,1)}, bf16[4,2,256,256]{3,2,0,1:T(8,128)(2,1)S(1)}, u32[]{:S(2)}, u32[]{:S(2)}) collective-permute-start(bf16[4,2,256,256]{3,2,0,1:T(8,128)(2,1)} %copy_select_fusion), channel_id=1, source_target_pairs={{0,2},{1,3},{2,0},{3,1},{4,6},{5,7},{6,4},{7,5},{8,10},{9,11},{10,... | collective-permute-start | bytes 3145736 | tf_op jit(solution)/shard_map/ppermute | solution.py:287
  70.5 3.2 %copy-start.8 = (bf16[5,2,256,256]{3,2,1,0:T(8,128)(2,1)S(1)}, bf16[5,2,256,256]{3,2,1,0:T(8,128)(2,1)}, u32[]{:S(2)}) copy-start(bf16[5,2,256,256]{3,2,1,0:T(8,128)(2,1)} %copy-done.7) | copy-start | bytes 3932164
  71.6 39.9 %collective-permute-start.5 = (bf16[4,256,512]{2,1,0:T(8,128)(2,1)}, bf16[4,256,512]{2,1,0:T(8,128)(2,1)}, u32[]{:S(2)}, u32[]{:S(2)}) collective-permute-start(bf16[4,256,512]{2,1,0:T(8,128)(2,1)} %broadcast_select_fusion.3), channel_id=1, source_target_pairs={{0,4},{1,5},{2,30},{3,31},{4,8},{5,9},{6,2},{7,3},{8,12},{9,13},{1... | collective-permute-start | bytes 3145736 | tf_op jit(solution)/shard_map/ppermute | solution.py:287
  94.6 2.7 %copy-start.9 = (bf16[4,256,512]{2,1,0:T(8,128)(2,1)}, bf16[4,256,512]{2,1,0:T(8,128)(2,1)S(1)}, u32[]{:S(2)}) copy-start(bf16[4,256,512]{2,1,0:T(8,128)(2,1)S(1)} %broadcast_select_fusion.1) | copy-start | bytes 3145732
  95.8 30.4 %collective-permute-start.7 = (bf16[3,256,512]{2,1,0:T(8,128)(2,1)}, bf16[3,256,512]{2,1,0:T(8,128)(2,1)}, u32[]{:S(2)}, u32[]{:S(2)}) collective-permute-start(bf16[3,256,512]{2,1,0:T(8,128)(2,1)} %slice.254), channel_id=1, source_target_pairs={{0,4},{1,5},{2,30},{3,31},{4,8},{5,9},{6,2},{7,3},{8,12},{9,13},{1... | collective-permute-start | bytes 2359304 | tf_op jit(solution)/shard_map/ppermute | solution.py:287
  98.9 28.7 %collective-permute-start.8 = (bf16[1,256,512]{2,1,0:T(8,128)(2,1)}, bf16[1,256,512]{2,1,0:T(8,128)(2,1)}, u32[]{:S(2)}, u32[]{:S(2)}) collective-permute-start(bf16[1,256,512]{2,1,0:T(8,128)(2,1)} %slice.222), channel_id=1, source_target_pairs={{1,30},{2,0},{3,1},{5,2},{6,4},{7,5},{9,6},{10,8},{11,9},{13,10},{... | collective-permute-start | bytes 786440 | tf_op jit(solution)/shard_map/ppermute | solution.py:287
  104.1 13.2 %collective-permute-start.3 = (bf16[1,256,512]{2,1,0:T(8,128)(2,1)}, bf16[1,256,512]{2,1,0:T(8,128)(2,1)}, u32[]{:S(2)}, u32[]{:S(2)}) collective-permute-start(bf16[1,256,512]{2,1,0:T(8,128)(2,1)} %slice.206), channel_id=1, source_target_pairs={{0,2},{1,3},{2,5},{4,6},{5,7},{6,9},{8,10},{9,11},{10,13},{12,14},... | collective-permute-start | bytes 786440 | tf_op jit(solution)/shard_map/ppermute | solution.py:287
  111.5 14.8 %collective-permute-start.6 = (bf16[1,256,512]{2,1,0:T(8,128)(2,1)}, bf16[1,256,512]{2,1,0:T(8,128)(2,1)}, u32[]{:S(2)}, u32[]{:S(2)}) collective-permute-start(bf16[1,256,512]{2,1,0:T(8,128)(2,1)} %slice.252), channel_id=1, source_target_pairs={{0,4},{1,5},{2,30},{3,31},{4,8},{5,9},{6,2},{7,3},{8,12},{9,13},{1... | collective-permute-start | bytes 786440 | tf_op jit(solution)/shard_map/ppermute | solution.py:287
  179.5 15.4 %collective-permute-start.11 = (f32[2]{0:T(128)S(1)}, f32[2]{0:T(128)S(1)}, u32[]{:S(2)}, u32[]{:S(2)}) collective-permute-start(f32[2]{0:T(128)S(1)} %psum.7), channel_id=1, source_target_pairs={{2,4},{3,5},{6,8},{7,9},{10,12},{11,13},{14,16},{15,17},{18,20},{1... | collective-permute-start | bytes 32 | tf_op jit(solution)/shard_map/ppermute | solution.py:287
  180.8 14.6 %collective-permute-start.12 = (f32[1]{0:T(128)}, f32[1]{0:T(128)}, u32[]{:S(2)}, u32[]{:S(2)}) collective-permute-start(f32[1]{0:T(128)} %get-tuple-element.54), channel_id=1, source_target_pairs={{0,4},{1,5},{4,8},{5,9},{8,12},{9,13},{12,16},{13,17},{16,20},{17,... | collective-permute-start | bytes 20 | tf_op jit(solution)/shard_map/ppermute | solution.py:287
  185.8 8.2 %copy-start.11 = (bf16[4,2,256,256]{3,2,0,1:T(8,128)(2,1)}, bf16[4,2,256,256]{3,2,0,1:T(8,128)(2,1)S(1)}, u32[]{:S(2)}) copy-start(bf16[4,2,256,256]{3,2,0,1:T(8,128)(2,1)S(1)} %get-tuple-element.38) | copy-start | bytes 3145732
  185.8 29.9 %collective-permute-start.9 = (bf16[4,2,256,256]{3,2,0,1:T(8,128)(2,1)}, bf16[4,2,256,256]{3,2,0,1:T(8,128)(2,1)}, u32[]{:S(2)}, u32[]{:S(2)}) collective-permute-start(bf16[4,2,256,256]{3,2,0,1:T(8,128)(2,1)} %get-tuple-element.39), channel_id=1, source_target_pairs={{0,30},{1,31},{2,4},{3,5},{4,2},{5,3},{6,8},{7,9},{8,6},{9,7},{10,... | collective-permute-start | bytes 3145736 | tf_op jit(solution)/shard_map/ppermute | solution.py:287
  192.2 45.3 %collective-permute-start.10 = (bf16[4,2,256,256]{3,2,1,0:T(8,128)(2,1)}, bf16[4,2,256,256]{3,2,1,0:T(8,128)(2,1)}, u32[]{:S(2)}, u32[]{:S(2)}) collective-permute-start(bf16[4,2,256,256]{3,2,1,0:T(8,128)(2,1)} %broadcast_select_fusion), channel_id=1, source_target_pairs={{0,30},{1,31},{2,4},{3,5},{4,2},{5,3},{6,8},{7,9},{8,6},{9,7},{10,... | collective-permute-start | bytes 3145736 | tf_op jit(solution)/shard_map/ppermute | solution.py:287
  192.5 48.6 %collective-permute-start.13 = (bf16[1,256,256]{2,1,0:T(8,128)(2,1)S(1)}, bf16[1,256,256]{2,1,0:T(8,128)(2,1)S(1)}, u32[]{:S(2)}, u32[]{:S(2)}) collective-permute-start(bf16[1,256,256]{2,1,0:T(8,128)(2,1)S(1)} %slice_bitcast_fusion.13), channel_id=1, source_target_pairs={{1,30},{5,2},{9,6},{13,10},{17,14},{21,18},{25,22},{29,26}} | collective-permute-start | bytes 393224 | tf_op jit(solution)/shard_map/ppermute | solution.py:287
  194.9 43.6 %copy-start.12 = (bf16[4,2,256,256]{3,2,0,1:T(8,128)(2,1)S(1)}, bf16[4,2,256,256]{3,2,0,1:T(8,128)(2,1)}, u32[]{:S(2)}) copy-start(bf16[4,2,256,256]{3,2,0,1:T(8,128)(2,1)} %copy-done.11) | copy-start | bytes 3145732
  238.5 2.3 copy-start.13
  238.6 2.3 copy-start.14
  (11 other events, 15.3 us)

commit v3 on v2

v3 whole, which is shorter than its diff:
```python
import math

import jax
import jax.numpy as jnp
from jax import lax
from jax.experimental import pallas as pl
from jax.experimental.pallas import tpu as pltpu
from jax.sharding import PartitionSpec as P

tau_step = 0.5
SUB = 8
LANES = 128
PANEL = 32
PART = 8
UNROLL = 2
FIRST = (((0,), (0,)), ((), ()))
LAST = (((1,), (1,)), ((), ()))
PLAIN = (((1,), (0,)), ((), ()))


def gate_terms(hopping, ising_term, field_term):
    rotation = 0.5 * tau_step * hopping
    middle_scale = jnp.exp(0.25 * tau_step * ising_term)
    weight_empty = jnp.exp(-tau_step * (0.25 * ising_term - 0.5 * field_term))
    weight_full = jnp.exp(-tau_step * (0.25 * ising_term + 0.5 * field_term))
    grown, shrunk = jnp.exp(rotation), jnp.exp(-rotation)
    weight_stay = middle_scale * (0.5 * (grown + shrunk))
    weight_swap = -middle_scale * (0.5 * (grown - shrunk))
    return weight_empty, weight_stay, weight_swap, weight_full


def dot(left, right, dims):
    return lax.dot_general(left, right, dims, preferred_element_type=jnp.float32)


def spread(row, lane_index):
    return jnp.take_along_axis(row, lane_index, axis=1)


def refined_reciprocal(value):
    guess = pltpu.reciprocal(value, approx=True)
    return guess * (2.0 - value * guess)


def factor_panel(rows_ref, first, tile):
    lanes = rows_ref.shape[0] * LANES
    lane = lax.broadcasted_iota(jnp.int32, (SUB, lanes), 1)
    zero = jnp.zeros((SUB, LANES), jnp.int32)
    mine = slice(tile * LANES, (tile + 1) * LANES)
    stop = first + PANEL

    def load(index):
        at = slice(index * SUB, (index + 1) * SUB)
        return jnp.concatenate([rows_ref[half, at, :] for half in range(lanes // LANES)], axis=1)

    def wide(value):
        return jnp.concatenate([value] * (lanes // LANES), axis=1)

    def store(index, value):
        at = slice(index * SUB, (index + 1) * SUB)
        for half in range(lanes // LANES):
            rows_ref[half, at, :] = value[:, half * LANES : (half + 1) * LANES]

    for start in range(0, PANEL, PART):
        rows = [load(start + i) for i in range(PART)]
        base = first - tile * LANES + start
        entry = [
            [spread(rows[i][:, mine], base + j + zero) if j >= i else None for j in range(PART)]
            for i in range(PART)
        ]
        later = []
        for step in range(PART):
            k = first + start + step
            inverted = refined_reciprocal(entry[step][step])
            unit = jnp.where(lane == k, 1.0, rows[step])
            for other in range(step + 1, PART):
                ratio = entry[step][other] * inverted
                for column in range(other, PART):
                    entry[other][column] = entry[other][column] - ratio * entry[step][column]
                rows[other] = jnp.where(lane == k, 0.0, rows[other]) - wide(ratio) * unit
            done = jnp.where((lane > k) & (lane < stop), 0.0, unit)
            store(start + step, done * wide(lax.rsqrt(entry[step][step])))
            hidden = jnp.where((lane > k) & (lane < first + start + PART), 0.0, unit)
            later.append(hidden * wide(inverted))
        for i in range(start + PART, PANEL):
            hide = (lane >= first + start) & (lane < first + start + PART)
            row = jnp.where(hide, 0.0, load(i))
            for step in range(PART):
                row = row - wide(spread(rows[step][:, mine], first - tile * LANES + i + zero)) * later[step]
            store(i, row)


def in_parts(value):
    high = value.astype(jnp.bfloat16)
    rest = value - high.astype(jnp.float32)
    middle = rest.astype(jnp.bfloat16)
    return high, middle, (rest - middle.astype(jnp.float32)).astype(jnp.bfloat16)


def run_copies(plan, semaphores):
    copies = [
        pltpu.make_async_copy(source, place, semaphores.at[index])
        for index, (source, place) in enumerate(plan)
    ]
    for copy in copies:
        copy.start()
    for copy in copies:
        copy.wait()


def run_by_parity(even_plan, odd_plan, semaphores):
    is_even = lax.rem(lax.axis_index("chain"), 2) == 0

    @pl.when(is_even)
    def _():
        run_copies(even_plan, semaphores)

    @pl.when(jnp.logical_not(is_even))
    def _():
        run_copies(odd_plan, semaphores)


def first_plans(late, half, early, operands, left, right):
    own, got_early, got_late, edge, corner = operands
    own = own.at[0]
    if late:
        n = half - early
        even = [
            (own.at[pl.ds(early - 1, n + 1)], left),
            (got_early.at[pl.ds(early, 1), 0], right.at[pl.ds(0, 1), 0]),
            (got_late.at[pl.ds(0, n), 0], right.at[pl.ds(1, n), 0]),
            (got_early.at[pl.ds(early - 1, 2), 1], right.at[pl.ds(0, 2), 1]),
        ]
        if n > 1:
            even.append((got_late.at[pl.ds(0, n - 1), 1], right.at[pl.ds(2, n - 1), 1]))
        odd = [
            (got_early.at[pl.ds(early, 1)], left.at[pl.ds(0, 1)]),
            (got_late.at[pl.ds(0, n)], left.at[pl.ds(1, n)]),
            (own.at[pl.ds(half + early, n), 0], right.at[pl.ds(0, n), 0]),
            (edge.at[pl.ds(0, 1), 0], right.at[pl.ds(n, 1), 0]),
            (own.at[pl.ds(half + early - 1, n + 1), 1], right.at[pl.ds(0, n + 1), 1]),
        ]
    else:
        n = early
        even = [
            (edge, left.at[pl.ds(0, 1)]),
            (own.at[pl.ds(0, n)], left.at[pl.ds(1, n)]),
            (got_early.at[pl.ds(0, n + 1), 0], right.at[pl.ds(0, n + 1), 0]),
            (corner, right.at[pl.ds(0, 1), 1]),
            (got_early.at[pl.ds(0, n), 1], right.at[pl.ds(1, n), 1]),
        ]
        odd = [
            (got_early, left),
            (own.at[pl.ds(half, n + 1), 0], right.at[pl.ds(0, n + 1), 0]),
            (own.at[pl.ds(half - 1, n + 1), 1], right.at[pl.ds(0, n + 1), 1]),
        ]
    return even, odd


def second_plans(late, half, early, operands, left, right):
    keep_early, keep_late, carried_early, carried_next, carried_late, beside = operands
    if late:
        n = half - early
        even = [
            (carried_early.at[pl.ds(early - 1, 1)], left.at[pl.ds(0, 1)]),
            (carried_late, left.at[pl.ds(1, n)]),
            (keep_late, right.at[pl.ds(0, n)]),
            (beside, right.at[pl.ds(n, 1)]),
        ]
        odd = [
            (keep_early.at[pl.ds(early - 1, 1)], left.at[pl.ds(0, 1)]),
            (keep_late, left.at[pl.ds(1, n)]),
            (carried_late, right.at[pl.ds(0, n)]),
            (beside, right.at[pl.ds(n, 1)]),
        ]
    else:
        n = early
        even = [
            (beside, left.at[pl.ds(0, 1)]),
            (carried_early, left.at[pl.ds(1, n)]),
            (keep_early, right.at[pl.ds(0, n)]),
            (keep_late.at[pl.ds(0, 1)], right.at[pl.ds(n, 1)]),
        ]
        odd = [
            (beside, left.at[pl.ds(0, 1)]),
            (keep_early, left.at[pl.ds(1, n)]),
            (carried_early, right.at[pl.ds(0, n)]),
            (carried_next, right.at[pl.ds(n, 1)]),
        ]
    return even, odd


def pair_kernel(second, late, sectors, refs):
    half = sectors // 2
    early = half // 2
    sizes, partner_sizes, ranks, couplings = refs[:4]
    operand_count = 6 if second else 5
    operands = refs[4 : 4 + operand_count]
    sketch_ref = refs[4 + operand_count]
    outputs = refs[5 + operand_count : -11]
    (
        left_ref,
        right_ref,
        basis_ref,
        coef_ref,
        two_ref,
        sample_ref,
        gram_ref,
        inverse_ref,
        rows_ref,
        in_semaphores,
        out_semaphores,
    ) = refs[-11:]
    send, keep, norm_ref, *extras = outputs
    count, kept, double = sample_ref.shape
    width = double // 2
    plans = second_plans if second else first_plans
    run_by_parity(*plans(late, half, early, operands, left_ref, right_ref), in_semaphores)

    parity = lax.rem(lax.axis_index("chain"), 2)
    is_even = parity == 0
    first = lax.axis_index("block") * sectors + parity * half + (early if late else 0)
    bond = parity if second else 1 - parity
    total = sizes.shape[2]

    def left_size(sector):
        at = jnp.clip(sector, 0, total - 1)
        return jnp.where(is_even, sizes[0, 0, at], partner_sizes[0, 0, at])

    def middle_size(sector):
        at = jnp.clip(sector, 0, total - 1)
        size = jnp.where(is_even, sizes[0, 1, at], sizes[0, 0, at])
        return jnp.where(sector < total, size, 0)

    def right_size(sector):
        at = jnp.clip(sector, 0, total - 1)
        size = jnp.where(is_even, partner_sizes[0, 1, at], sizes[0, 1, at])
        return jnp.where(sector < total, size, 0)

    row_index = lax.broadcasted_iota(jnp.int32, (kept, 1), 0)
    eye = (
        lax.broadcasted_iota(jnp.int32, (kept, kept), 0)
        == lax.broadcasted_iota(jnp.int32, (kept, kept), 1)
    )
    block_row = lax.broadcasted_iota(jnp.int32, (width, width), 0)
    block_column = lax.broadcasted_iota(jnp.int32, (width, width), 1)
    column = lax.broadcasted_iota(jnp.int32, (1, width), 1)

    def left(m, s, sector):
        if second:
            return left_ref[m, :, s * width : (s + 1) * width]
        inside = (column < middle_size(sector + s)).astype(jnp.float32).astype(jnp.bfloat16)
        return left_ref[m, s] * inside

    def right(m, s):
        if second:
            return right_ref[m, :, s * width : (s + 1) * width]
        return right_ref[m, s]

    def product(a, b):
        rounded = dot(a, b, LAST if second else PLAIN).astype(jnp.bfloat16)
        return rounded.astype(jnp.float32)

    def put(m, rows, columns, value, row_limit, column_limit):
        if not second:
            value = jnp.where(
                (block_row < row_limit) & (block_column < column_limit), value, 0.0
            )
        two_ref[m, rows, columns] = value.astype(jnp.bfloat16)

    w_empty, w_stay, w_swap, w_full = gate_terms(
        *(jnp.full((1, width), couplings[0, bond, term], jnp.float32) for term in range(3))
    )

    @pl.loop(0, count, unroll=min(UNROLL, count))
    def _(m):
        sector = first + m
        below_zero, below_one = left(m, 0, sector - 1), left(m, 1, sector - 1)
        here_zero, here_one = left(m + 1, 0, sector), left(m + 1, 1, sector)
        same_zero, same_one = right(m, 0), right(m, 1)
        next_zero, next_one = right(m + 1, 0), right(m + 1, 1)
        low, high = slice(0, width), slice(width, double)
        rows_low, rows_high = left_size(sector), left_size(sector - 1)
        columns_low, columns_high = right_size(sector), right_size(sector + 1)
        put(m, low, low, w_empty * product(here_zero, same_zero), rows_low, columns_low)
        put(
            m,
            low,
            high,
            w_stay * product(here_zero, next_one) + w_swap * product(here_one, next_zero),
            rows_low,
            columns_high,
        )
        put(
            m,
            high,
            low,
            w_swap * product(below_zero, same_one) + w_stay * product(below_one, same_zero),
            rows_high,
            columns_low,
        )
        put(m, high, high, w_full * product(below_one, next_one), rows_high, columns_high)
        sample = dot(sketch_ref[...], two_ref[m], LAST)
        keep_rows = row_index < ranks[0, bond, sector]
        sample = jnp.where(keep_rows, sample, 0.0)
        sample_ref[m] = sample
        high_part, middle_part, low_part = in_parts(sample)
        cross = dot(high_part, middle_part, LAST) + dot(high_part, low_part, LAST)
        gram = dot(high_part, high_part, LAST) + (
            dot(middle_part, middle_part, LAST) + (cross + jnp.transpose(cross))
        )
        gram_ref[m] = gram + jnp.where(eye & jnp.logical_not(keep_rows), 1.0, 0.0)

    lane = lax.broadcasted_iota(jnp.int32, (1, kept), 1)
    for tile in range(kept // LANES):
        @pl.loop(0, LANES // PANEL)
        def _(panel):
            first = pl.multiple_of(tile * LANES + panel * PANEL, PANEL)
            here = pl.ds(first, PANEL)
            stop = first + PANEL
            for m in range(count):
                for half in range(kept // LANES):
                    span = slice(half * LANES, (half + 1) * LANES)
                    rows_ref[half, pl.ds(m, PANEL, stride=SUB), :] = gram_ref[m, here, span]
            factor_panel(rows_ref, first, tile)
            for m in range(count):
                solved = jnp.concatenate(
                    [
                        rows_ref[half, pl.ds(m, PANEL, stride=SUB), :]
                        for half in range(kept // LANES)
                    ],
                    axis=1,
                )
                inverse_ref[m, here, :] = jnp.where(lane < stop, solved, 0.0)
                high, middle, low = in_parts(solved)
                one = jnp.concatenate([high, high, middle, middle, high, low], axis=0)
                two = jnp.concatenate([high, middle, high, middle, low, high], axis=0)
                change = dot(one, two, FIRST)
                kept_part = jnp.where((lane >= first) & (lane < stop), 0.0, gram_ref[m])
                gram_ref[m] = kept_part - change

    norm_ref[...] = jnp.zeros_like(norm_ref)

    @pl.loop(0, count, unroll=min(UNROLL, count))
    def _(m):
        inverse_high, inverse_middle, _ = in_parts(inverse_ref[m])
        sample_high, sample_middle, _ = in_parts(sample_ref[m])
        solved = dot(inverse_high, sample_high, PLAIN) + (
            dot(inverse_high, sample_middle, PLAIN) + dot(inverse_middle, sample_high, PLAIN)
        )
        solved = solved * math.sqrt(width)
        basis = solved.astype(jnp.bfloat16)
        if second:
            for s in range(2):
                turned = jnp.transpose(solved[:, s * width : (s + 1) * width])
                basis_ref[m, s] = turned.astype(jnp.bfloat16)
        else:
            basis_ref[m] = basis
        coef = dot(basis, two_ref[m], PLAIN)
        norm_ref[...] += jnp.sum(coef * coef, axis=0, keepdims=True)
        rounded = coef.astype(jnp.bfloat16)
        if second:
            for s in range(2):
                coef_ref[m, s] = rounded[:, s * width : (s + 1) * width]
        else:
            coef_ref[m] = rounded


    if second:
        even, odd = [(basis_ref, send), (coef_ref, keep)], [(coef_ref, send), (basis_ref, keep)]
        if not late:
            both = [(basis_ref.at[pl.ds(0, 1), 1], extras[0])]
    else:
        even, odd = [(coef_ref, send), (basis_ref, keep)], [(basis_ref, send), (coef_ref, keep)]
        if late:
            both = [(coef_ref.at[pl.ds(count - 1, 1)], extras[0])]
            even.append((coef_ref.at[pl.ds(0, 1)], extras[1]))
            odd.append((basis_ref.at[pl.ds(0, 1)], extras[1]))
        else:
            both = [(basis_ref.at[pl.ds(0, 1)], extras[0])]
    if not (second and late):
        even, odd = even + both, odd + both
    run_by_parity(even, odd, out_semaphores)


def pair_update(second, late, sizes, partner_sizes, ranks, couplings, operands, sketch_turned):
    kept, double = sketch_turned.shape
    width = double // 2
    sectors = sizes.shape[2] // lax.axis_size("block")
    half = sectors // 2
    early = half // 2
    count = half - early if late else early
    block = (2, width, kept) if second else (kept, double)
    coef_block = (2, kept, width) if second else (kept, double)
    extra = [(1, width, kept)] if second else [(1, kept, double)]
    if late:
        extra = [] if second else extra * 2
    left_shape = (count + 1, kept, double) if second else (count + 1, 2, width, width)
    vmem = pl.BlockSpec(memory_space=pltpu.VMEM)
    smem = pl.BlockSpec(memory_space=pltpu.SMEM)
    anywhere = pl.BlockSpec(memory_space=pl.ANY)

    def kernel(*refs):
        pair_kernel(second, late, sectors, refs)

    return pl.pallas_call(
        kernel,
        out_shape=[
            jax.ShapeDtypeStruct((count, *block), jnp.bfloat16),
            jax.ShapeDtypeStruct((count, *block), jnp.bfloat16),
            jax.ShapeDtypeStruct((1, double), jnp.float32),
            *(jax.ShapeDtypeStruct(shape, jnp.bfloat16) for shape in extra),
        ],
        in_specs=[smem] * 4 + [anywhere] * len(operands) + [vmem],
        out_specs=[anywhere, anywhere, vmem] + [anywhere] * len(extra),
        scratch_shapes=[
            pltpu.VMEM(left_shape, jnp.bfloat16),
            pltpu.VMEM(left_shape, jnp.bfloat16),
            pltpu.VMEM((count, *block), jnp.bfloat16),
            pltpu.VMEM((count, *coef_block), jnp.bfloat16),
            pltpu.VMEM((count, double, double), jnp.bfloat16),
            pltpu.VMEM((count, kept, double), jnp.float32),
            pltpu.VMEM((count, kept, kept), jnp.float32),
            pltpu.VMEM((count, kept, kept), jnp.float32),
            pltpu.VMEM((kept // LANES, PANEL * SUB, LANES), jnp.float32),
            pltpu.SemaphoreType.DMA((5,)),
            pltpu.SemaphoreType.DMA((4,)),
        ],
        compiler_params=pltpu.CompilerParams(vmem_limit_bytes=32 * 2**20),
        cost_estimate=pl.CostEstimate(
            flops=(count + 12) * 50 * kept * double * double,
            bytes_accessed=8 * count * kept * double * 2,
            transcendentals=0,
        ),
    )(sizes, partner_sizes, ranks, couplings, *operands, sketch_turned)


def place_kernel(last, half, scale_ref, refs):
    early = half // 2
    n = half - early
    if last:
        returned, _, out, buffer, in_semaphores, out_semaphores = refs
        parts = [(returned, half + early, n)]
        odd = [
            (returned.at[pl.ds(0, n), 0], out.at[0, pl.ds(early, n), 0]),
            (returned.at[pl.ds(0, n), 1], out.at[0, pl.ds(early - 1, n), 1]),
        ]
    else:
        keep_early, keep_late, returned, lower, out, buffer, in_semaphores, out_semaphores = refs
        parts = [(keep_early, 0, early), (keep_late, early, n), (returned, half, early)]
        odd = [
            (returned.at[pl.ds(0, early), 0], out.at[0, pl.ds(0, early), 0]),
            (keep_early.at[pl.ds(0, early), 0], out.at[0, pl.ds(half, early), 0]),
            (keep_early.at[pl.ds(0, early), 1], out.at[0, pl.ds(half - 1, early), 1]),
            (keep_late.at[pl.ds(0, n), 0], out.at[0, pl.ds(half + early, n), 0]),
            (keep_late.at[pl.ds(0, n), 1], out.at[0, pl.ds(half + early - 1, n), 1]),
            (lower, out.at[0, pl.ds(2 * half - 1, 1), 1]),
        ]
        if early > 1:
            odd.append((returned.at[pl.ds(1, early - 1), 1], out.at[0, pl.ds(0, early - 1), 1]))
    is_even = lax.rem(lax.axis_index("chain"), 2) == 0

    @pl.when(jnp.logical_not(is_even))
    def _():
        run_copies(odd, out_semaphores)

    @pl.when(is_even)
    def _():
        coming, going, filled = [], [], 0
        for index, (source, start, size) in enumerate(parts):
            room = buffer.at[pl.ds(filled, size)]
            coming.append(pltpu.make_async_copy(source, room, in_semaphores.at[index]))
            going.append(
                pltpu.make_async_copy(room, out.at[0, pl.ds(start, size)], out_semaphores.at[index])
            )
            filled += size
        for copy in coming:
            copy.start()
        filled = 0
        for index, (source, start, size) in enumerate(parts):
            coming[index].wait()

            @pl.loop(filled, filled + size)
            def _(sector):
                for s in range(2):
                    scaled = buffer[sector, s].astype(jnp.float32) * scale_ref[0]
                    buffer[sector, s] = scaled.astype(jnp.bfloat16)

            going[index].start()
            filled += size
        for copy in going:
            copy.wait()


def place(last, half, scale, operands, site):
    anywhere = pl.BlockSpec(memory_space=pl.ANY)
    early = half // 2
    rows = half - early if last else half + early

    def kernel(scale_ref, *refs):
        place_kernel(last, half, scale_ref, refs)

    return pl.pallas_call(
        kernel,
        out_shape=jax.ShapeDtypeStruct(site.shape, site.dtype),
        in_specs=[pl.BlockSpec(memory_space=pltpu.SMEM)] + [anywhere] * len(operands),
        out_specs=anywhere,
        scratch_shapes=[
            pltpu.VMEM((rows, *site.shape[2:]), site.dtype),
            pltpu.SemaphoreType.DMA((3,)),
            pltpu.SemaphoreType.DMA((7,)),
        ],
        input_output_aliases={2: 0} if last else {},
        compiler_params=pltpu.CompilerParams(vmem_limit_bytes=16 * 2**20),
        cost_estimate=pl.CostEstimate(
            flops=0, bytes_accessed=2 * rows * site.size // site.shape[1] * 2, transcendentals=0
        ),
    )(scale, *operands)


def move(value, target_of):
    sites, parts = lax.axis_size("chain"), lax.axis_size("block")
    pairs = []
    for site in range(sites):
        for part in range(parts):
            target = target_of(site, part)
            if target is not None and 0 <= target[1] < parts:
                pairs.append((site * parts + part, (target[0] % sites) * parts + target[1]))
    return lax.ppermute(value, ("chain", "block"), pairs)


def by_parity(even_target, odd_target):
    return lambda c, b: even_target(c, b) if c % 2 == 0 else odd_target(c, b)


def nowhere(c, b):
    return None


def joined(*parts):
    return jnp.concatenate(parts, axis=0)


def body(site_tensors, sketch, bond_sizes, kept_ranks, couplings):
    sectors = site_tensors.shape[1]
    half = sectors // 2
    early = half // 2
    width = site_tensors.shape[-1]
    kept = sketch.shape[1]
    parts = lax.axis_size("block")
    is_even = lax.axis_index("chain") % 2 == 0
    own = site_tensors[0]
    sketch_turned = jnp.transpose(sketch)

    def pick(even_value, odd_value):
        return jnp.where(is_even, even_value, odd_value)

    def update(second, late, *operands):
        return pair_update(
            second, late, bond_sizes, partner_sizes, kept_ranks, couplings, operands, sketch_turned
        )

    across = by_parity(lambda c, b: (c + 1, b), lambda c, b: (c - 1, b))
    got_early = move(pick(own[half - 1 : half + early], own[: early + 1]), across)
    partner_sizes = move(bond_sizes, across)
    edge = move(
        pick(own[-1:], own[:1]), by_parity(lambda c, b: (c, b + 1), lambda c, b: (c, b - 1))
    )
    corner = move(own[-1:, 1], by_parity(nowhere, lambda c, b: (c - 1, b + 1)))
    sent = pick(own[half + early :], own[early + 1 : half + 1])
    sent, got_early = lax.optimization_barrier((sent, got_early))
    got_late = move(sent, across)
    send_early, keep_early, norm_early, basis_first = update(
        False, False, site_tensors, got_early, got_early, edge, corner
    )

    along = by_parity(lambda c, b: (c + 2, b), lambda c, b: (c - 2, b))
    carried_early = move(send_early, along)
    basis_above = move(
        basis_first, by_parity(lambda c, b: (c - 1, b - 1), lambda c, b: (c - 1, b))
    )
    send_late, keep_late, norm_late, coef_last, send_next = update(
        False, True, site_tensors, got_early, got_late, edge, corner
    )
    norm_even = jnp.sum(norm_early) + jnp.sum(norm_late)
    carried_next = move(send_next, along)
    coef_below = move(
        coef_last, by_parity(lambda c, b: (c + 1, b), lambda c, b: (c + 1, b + 1))
    )
    send_late, carried_early, carried_next, coef_below = lax.optimization_barrier(
        (send_late, carried_early, carried_next, coef_below)
    )
    carried_late = move(send_late, along)

    back = by_parity(lambda c, b: (c - 1, b), lambda c, b: (c + 1, b))
    send_early, kept_early, norm_early, lower_first = update(
        True, False, keep_early, keep_late, carried_early, carried_next, carried_next, coef_below
    )
    returned_early = move(send_early, back)
    lower_above = move(lower_first, by_parity(lambda c, b: (c - 1, b - 1), nowhere))
    send_late, kept_late, norm_late = update(
        True, True, keep_early, keep_late, carried_early, carried_next, carried_late, basis_above
    )
    send_late, returned_early = lax.optimization_barrier((send_late, returned_early))
    returned_late = move(send_late, back)

    norm_odd = jnp.sum(norm_early) + jnp.sum(norm_late)
    norms = lax.psum(jnp.stack([norm_even, norm_odd]), "block")
    from_left = move(norms, by_parity(nowhere, lambda c, b: (c + 1, b)))
    from_second = move(norms[:1], by_parity(lambda c, b: (c + 2, b), nowhere))
    target = float(sectors * parts * kept * width)
    scale = jnp.sqrt(target / (from_left[0] + from_second[0]))
    scale = scale * jnp.sqrt(target / (scale * scale * (norms[1] + from_left[1])))
    scale = scale[None]

    site = place(
        False, half, scale, (kept_early, kept_late, returned_early, lower_above), site_tensors
    )
    return place(True, half, scale, (returned_late, site), site_tensors)


def solution(mesh):
    placed = (
        P("chain", "block", None, None, None),
        P(),
        P("chain", None, None),
        P("chain", None, None),
        P("chain", None, None),
    )
    return jax.shard_map(
        body,
        mesh=mesh,
        in_specs=placed,
        out_specs=P("chain", "block", None, None, None),
        check_vma=False,
    )
```

time: 248 us -> 200 us (0.81)
  local copies, waits for them, and re-layouts: 32.6 us -> 6.72 us
  other arithmetic: 31.2 us -> 6.89 us
  Pallas kernels: 76.8 us -> 84.6 us
  starting transfers between devices: 29.5 us -> 22.5 us
  blocking collectives: 2.44 us -> 9.11 us
  between operations: 11 us -> 5.78 us
    select_n x15 -> x3, other arithmetic: 17.5 us -> 4.18 us  [pick(): return jnp.where(is_even, even_value, odd_value)]
    slice x20 -> x0, local copies, waits for them, and re-layouts: 13.1 us -> none  [the longest x1 2.1 us: body(): left = pick(joined(edge[None], own[:early]), got_early)]
    pallas_call x4 -> x6, Pallas kernels: 76.8 us -> 84.6 us  [the longest x4 81.1 us: pair_update(): pl.pallas_call(kernel, out_shape=[jax.ShapeDtypeStruct((count, *block), j...]
    ppermute x14 -> x15, starting transfers between devices: 29.5 us -> 22.5 us  [move(): return lax.ppermute(value, ('chain', 'block'), pairs)]
    psum x1, blocking collectives: 2.44 us -> 9.11 us  [body(): norms = lax.psum(jnp.stack([norm_even, norm_odd]), 'block')]
    unnamed x45 -> x17, local copies, waits for them, and re-layouts: 11 us -> 4.53 us
    squeeze x5 -> x0, local copies, waits for them, and re-layouts: 3.9 us -> none  [the longest x1 1.15 us: body(): returned_early[:, 0]]
    concatenate x3 -> x0, other arithmetic: 3.69 us -> none  [the longest x2 3.61 us: joined(): return jnp.concatenate(parts, axis=0)]
  transfers between devices with their start and end apart: 14 -> 15, of which waited for: 4 -> 4; matrix products, arithmetic and copies ran while one was open for 15% -> 3% of each run, Pallas kernels for 15% -> 42%
where the time goes in v3:
time: 200 us; the launch traced here: 199 us
  Pallas kernels  84.6 us (42%)
  waiting for transfers between devices  64 us (32%)
  starting transfers between devices  22.5 us (11%)
  blocking collectives  9.11 us (5%)
  other arithmetic  6.89 us (3%)
  local copies, waits for them, and re-layouts  6.72 us (3%)
  between operations  5.78 us (3%)
    pallas_call x4, Pallas kernels, pair_update(): pl.pallas_call(kernel, out_shape=[jax.ShapeDtypeStruct((count, *block), j...  81.1 us
    ppermute x15, waiting for transfers between devices, move(): return lax.ppermute(value, ('chain', 'block'), pairs)  64 us
    ppermute x15, starting transfers between devices, move(): return lax.ppermute(value, ('chain', 'block'), pairs)  22.5 us
    psum x1, blocking collectives, body(): norms = lax.psum(jnp.stack([norm_even, norm_odd]), 'block')  9.11 us
    unnamed x17, local copies, waits for them, and re-layouts  4.53 us
    select_n x3, other arithmetic, pick(): return jnp.where(is_even, even_value, odd_value)  4.18 us
  transfers between devices with their start and end apart: 15, of which 4 were waited for; matrix products, arithmetic and copies ran while one was open for 3% of the time, Pallas kernels for 42%

profile of v3, /device:TPU:0, one launch (start us, length us, event | category | flops | bytes accessed | tf_op | source)
XLA Modules:
  0.0 199.5 jit_solution(2358410382746871652)
XLA Ops:
  0.0 3.1 %select_bitcast_fusion = bf16[5,2,256,256]{3,2,1,0:T(8,128)(2,1)} fusion(bf16[1,16,2,256,256]{4,3,2,1,0:T(8,128)(2,1)} %refs_4_.3, pred[]{:T(512)S(6)} %eq.5), kind=kLoop, calls=%fused_computation | loop fusion | flops 655360 | bytes 3932161 | tf_op jit(solution)/shard_map/jit(_where)/select_n | solution.py:556
  3.1 3.0 %collective-permute-start.1 = (bf16[5,2,256,256]{3,2,1,0:T(8,128)(2,1)}, bf16[5,2,256,256]{3,2,1,0:T(8,128)(2,1)S(1)}, u32[]{:S(2)}, u32[]{:S(2)}) collective-permute-start(bf16[5,2,256,256]{3,2,1,0:T(8,128)(2,1)} %select_bitcast_fusion), channel_id=1, source_target_pairs={{0,2},{1,3},{2,0},{3,1},{4,6},{5,7},{6,4},{7,5},{8,10},{9,11},{10,... | collective-permute-start | bytes 3932168 | tf_op jit(solution)/shard_map/ppermute | solution.py:529
  7.7 2.1 %collective-permute-start.2 = (bf16[1,2,256,256]{3,2,1,0:T(8,128)(2,1)S(1)}, bf16[1,2,256,256]{3,2,1,0:T(8,128)(2,1)S(1)}, u32[]{:S(2)}, u32[]{:S(2)}) collective-permute-start(bf16[1,2,256,256]{3,2,1,0:T(8,128)(2,1)S(1)} %select_bitcast_fusion.2), channel_id=1, source_target_pairs={{0,1},{3,2},{4,5},{7,6},{8,9},{11,10},{12,13},{15,14},{16,17},{19,... | collective-permute-start | bytes 786440 | tf_op jit(solution)/shard_map/ppermute | solution.py:529
  11.0 24.0 %collective-permute-done.1.refs_5_.refs_6_ = bf16[5,2,256,256]{3,2,1,0:T(8,128)(2,1)S(1)} collective-permute-done((bf16[5,2,256,256]{3,2,1,0:T(8,128)(2,1)}, bf16[5,2,256,256]{3,2,1,0:T(8,128)(2,1)S(1)}, u32[]{:S(2)}, u32[]{:S(2)}) %collective-permute-start.1) | collective-permute-done | bytes 1310752 | tf_op jit(solution)/shard_map/ppermute | solution.py:529
  35.0 1.7 collective-permute-start.4
  36.8 2.2 %copy-done.1 = bf16[1,16,2,256,256]{4,3,2,1,0:T(8,128)(2,1)S(1)} copy-done((bf16[1,16,2,256,256]{4,3,2,1,0:T(8,128)(2,1)S(1)}, bf16[1,16,2,256,256]{4,3,2,1,0:T(8,128)(2,1)}, u32[]{:S(2)}) %copy-start.1) | copy-done | bytes 4194328
  39.0 20.1 %shard_map.55 = (bf16[4,256,512]{2,1,0:T(8,128)(2,1)S(1)}, bf16[4,256,512]{2,1,0:T(8,128)(2,1)S(1)}, f32[1,512]{1,0:T(1,128)S(1)}, bf16[1,256,512]{2,1,0:T(8,128)(2,1)S(1)}) custom-call(s32[1,2,32]{2,1,0:T(2,128)S(1)} %copy-done.4, s32[1,2,32]{2,1,0:T(2,128)S(1)} %collective-permute-done.refs_1_, s32[1,2,32]{2,1,0:T(2,128)S(1)} %copy-done.5, ...), custom_call_target="tpu_custom_call" | custom-call | flops 53687091200 | bytes 8388608 | tf_op jit(solution)/shard_map/pallas_call | solution.py:406
  59.1 1.6 collective-permute-start.5
  60.6 20.3 %shard_map.56 = (bf16[4,256,512]{2,1,0:T(8,128)(2,1)S(1)}, bf16[4,256,512]{2,1,0:T(8,128)(2,1)S(1)}, f32[1,512]{1,0:T(1,128)S(1)}, bf16[1,256,512]{2,1,0:T(8,128)(2,1)S(1)}, bf16[1,256,512]{2,1,0:T(8,128)(2,1)S(1)}) custom-call(s32[1,2,32]{2,1,0:T(2,128)S(1)} %copy-done.4, s32[1,2,32]{2,1,0:T(2,128)S(1)} %collective-permute-done.refs_1_, ...), custom_call_target="tpu_custom_call" | custom-call | flops 53687091200 | bytes 8388608 | tf_op jit(solution)/shard_map/pallas_call | solution.py:406
  80.9 1.6 collective-permute-start.6
  82.5 5.3 %collective-permute-start.7 = (bf16[1,256,512]{2,1,0:T(8,128)(2,1)S(1)}, bf16[1,256,512]{2,1,0:T(8,128)(2,1)S(1)}, u32[]{:S(2)}, u32[]{:S(2)}) collective-permute-start(bf16[1,256,512]{2,1,0:T(8,128)(2,1)S(1)} %get-tuple-element.38), channel_id=1, source_target_pairs={{0,2},{1,3},{2,5},{4,6},{5,7},{6,9},{8,10},{9,11},{10,13},{12,14},... | collective-permute-start | bytes 786440 | tf_op jit(solution)/shard_map/ppermute | solution.py:529
  87.8 1.3 collective-permute-start.9
  89.1 5.2 %collective-permute-done.6.refs_7_.refs_8_ = bf16[1,256,512]{2,1,0:T(8,128)(2,1)S(1)} collective-permute-done((bf16[1,256,512]{2,1,0:T(8,128)(2,1)S(1)}, bf16[1,256,512]{2,1,0:T(8,128)(2,1)S(1)}, u32[]{:S(2)}, u32[]{:S(2)}) %collective-permute-start.6) | collective-permute-done | bytes 262176 | tf_op jit(solution)/shard_map/ppermute | solution.py:529
  94.3 19.9 %shard_map.57 = (bf16[4,2,256,256]{3,2,1,0:T(8,128)(2,1)S(1)}, bf16[4,2,256,256]{3,2,1,0:T(8,128)(2,1)S(1)}, f32[1,512]{1,0:T(1,128)S(1)}, bf16[1,256,256]{2,1,0:T(8,128)(2,1)S(1)}) custom-call(s32[1,2,32]{2,1,0:T(2,128)S(1)} %copy-done.4, s32[1,2,32]{2,1,0:T(2,128)S(1)} %collective-permute-done.refs_1_, s32[1,2,32]{2,1,0:T(2,128)S(1)} %copy-done.5, ...), custom_call_target="tpu_custom_call" | custom-call | flops 53687091200 | bytes 8388608 | tf_op jit(solution)/shard_map/pallas_call | solution.py:406
  114.3 1.4 collective-permute-start.12
  115.7 24.1 %collective-permute-done.8.refs_8_ = bf16[4,256,512]{2,1,0:T(8,128)(2,1)S(1)} collective-permute-done((bf16[4,256,512]{2,1,0:T(8,128)(2,1)S(1)}, bf16[4,256,512]{2,1,0:T(8,128)(2,1)S(1)}, u32[]{:S(2)}, u32[]{:S(2)}) %collective-permute-start.8) | collective-permute-done | bytes 1048608 | tf_op jit(solution)/shard_map/ppermute | solution.py:529
  139.7 20.8 %shard_map.58 = (bf16[4,2,256,256]{3,2,1,0:T(8,128)(2,1)}, bf16[4,2,256,256]{3,2,1,0:T(8,128)(2,1)S(1)}, f32[1,512]{1,0:T(1,128)S(1)}) custom-call(s32[1,2,32]{2,1,0:T(2,128)S(1)} %copy-done.4, s32[1,2,32]{2,1,0:T(2,128)S(1)} %collective-permute-done.refs_1_, s32[1,2,32]{2,1,0:T(2,128)S(1)} %copy-done.5, f32[1,2,3]{2,1,0:T(2,128)S(1)} %copy-done.6, ...), custom_call_target="tpu_custom_call" | custom-call | flops 53687091200 | bytes 8388608 | tf_op jit(solution)/shard_map/pallas_call | solution.py:406
  167.5 9.1 %psum.7 = f32[2]{0:T(128)S(1)} all-reduce(f32[2]{0:T(128)S(1)} %pad_maximum_fusion), channel_id=1, replica_groups=mesh['chain'=16,'block'=2] {'block'}, use_global_device_ids=true, to_apply=%region_4.5 | all-reduce | flops 2 | bytes 16 | tf_op jit(solution)/shard_map/psum | solution.py:608
  177.3 1.3 collective-permute-start.10
  178.6 1.9 collective-permute-start.11
  180.5 10.7 %collective-permute-done.10 = f32[2]{0:T(128)S(1)} collective-permute-done((f32[2]{0:T(128)S(1)}, f32[2]{0:T(128)S(1)}, u32[]{:S(2)}, u32[]{:S(2)}) %collective-permute-start.10) | collective-permute-done | bytes 40 | tf_op jit(solution)/shard_map/ppermute | solution.py:529
  194.6 1.2 copy-done.3
  195.8 2.1 %shard_map.59.refs_1_ = bf16[1,16,2,256,256]{4,3,2,1,0:T(8,128)(2,1)} custom-call(f32[1]{0:T(128)} %bitcast.10.scale_ref, bf16[4,2,256,256]{3,2,1,0:T(8,128)(2,1)S(1)} %get-tuple-element.49.refs_0_, bf16[4,2,256,256]{3,2,1,0:T(8,128)(2,1)S(1)} %copy-done.3, bf16[4,2,256,256]{3,2,1,0:T(8,128)(2,1)S(1)} %collective-permute-done.12.refs_2_, ...), custom_call_target="tpu_custom_call" | custom-call | bytes 6291456 | tf_op jit(solution)/shard_map/pallas_call | solution.py:503
  198.0 1.3 shard_map.60
  (41 shorter events, 8.6 us)
Async XLA Ops:
  0.0 7.7 %copy-start = (bf16[1,16,2,256,256]{4,3,2,1,0:T(8,128)(2,1)S(1)}, bf16[1,16,2,256,256]{4,3,2,1,0:T(8,128)(2,1)}, u32[]{:S(2)}) copy-start(bf16[1,16,2,256,256]{4,3,2,1,0:T(8,128)(2,1)} %refs_4_.3) | copy-start | bytes 12582916
  0.0 10.9 %copy-start.7 = (bf16[512,256]{1,0:T(8,128)(2,1)S(1)}, bf16[512,256]{1,0:T(8,128)(2,1)}, u32[]{:S(2)}) copy-start(bf16[512,256]{1,0:T(8,128)(2,1)} %param.6) | copy-start | bytes 786436
  0.0 36.8 %copy-start.4 = (s32[1,2,32]{2,1,0:T(2,128)S(1)}, s32[1,2,32]{2,1,0:T(2,128)}, u32[]{:S(2)}) copy-start(s32[1,2,32]{2,1,0:T(2,128)} %refs_0_.7) | copy-start | bytes 772
  0.0 36.8 %copy-start.5 = (s32[1,2,32]{2,1,0:T(2,128)S(1)}, s32[1,2,32]{2,1,0:T(2,128)}, u32[]{:S(2)}) copy-start(s32[1,2,32]{2,1,0:T(2,128)} %refs_2_.7) | copy-start | bytes 772
  0.0 36.8 %copy-start.6 = (f32[1,2,3]{2,1,0:T(2,128)S(1)}, f32[1,2,3]{2,1,0:T(2,128)}, u32[]{:S(2)}) copy-start(f32[1,2,3]{2,1,0:T(2,128)} %refs_3_.7) | copy-start | bytes 76
  3.1 31.9 %collective-permute-start.1 = (bf16[5,2,256,256]{3,2,1,0:T(8,128)(2,1)}, bf16[5,2,256,256]{3,2,1,0:T(8,128)(2,1)S(1)}, u32[]{:S(2)}, u32[]{:S(2)}) collective-permute-start(bf16[5,2,256,256]{3,2,1,0:T(8,128)(2,1)} %select_bitcast_fusion), channel_id=1, source_target_pairs={{0,2},{1,3},{2,0},{3,1},{4,6},{5,7},{6,4},{7,5},{8,10},{9,11},{10,... | collective-permute-start | bytes 3932168 | tf_op jit(solution)/shard_map/ppermute | solution.py:529
  6.0 30.7 %collective-permute-start = (s32[1,2,32]{2,1,0:T(2,128)}, s32[1,2,32]{2,1,0:T(2,128)S(1)}, u32[]{:S(2)}, u32[]{:S(2)}) collective-permute-start(s32[1,2,32]{2,1,0:T(2,128)} %refs_0_.7), channel_id=1, source_target_pairs={{0,2},{1,3},{2,0},{3,1},{4,6},{5,7},{6,4},{7,5},{8,10},{9,11},{10,... | collective-permute-start | bytes 776 | tf_op jit(solution)/shard_map/ppermute | solution.py:529
  7.0 29.8 %collective-permute-start.3 = (bf16[1,256,256]{2,1,0:T(8,128)(2,1)S(1)}, bf16[1,256,256]{2,1,0:T(8,128)(2,1)S(1)}, u32[]{:S(2)}, u32[]{:S(2)}) collective-permute-start(bf16[1,256,256]{2,1,0:T(8,128)(2,1)S(1)} %slice_bitcast_fusion), channel_id=1, source_target_pairs={{2,1},{6,5},{10,9},{14,13},{18,17},{22,21},{26,25},{30,29}} | collective-permute-start | bytes 393224 | tf_op jit(solution)/shard_map/ppermute | solution.py:529
  7.7 29.1 %collective-permute-start.2 = (bf16[1,2,256,256]{3,2,1,0:T(8,128)(2,1)S(1)}, bf16[1,2,256,256]{3,2,1,0:T(8,128)(2,1)S(1)}, u32[]{:S(2)}, u32[]{:S(2)}) collective-permute-start(bf16[1,2,256,256]{3,2,1,0:T(8,128)(2,1)S(1)} %select_bitcast_fusion.2), channel_id=1, source_target_pairs={{0,1},{3,2},{4,5},{7,6},{8,9},{11,10},{12,13},{15,14},{16,17},{19,... | collective-permute-start | bytes 786440 | tf_op jit(solution)/shard_map/ppermute | solution.py:529
  35.0 25.6 %collective-permute-start.4 = (bf16[4,2,256,256]{3,2,1,0:T(8,128)(2,1)}, bf16[4,2,256,256]{3,2,1,0:T(8,128)(2,1)S(1)}, u32[]{:S(2)}, u32[]{:S(2)}) collective-permute-start(bf16[4,2,256,256]{3,2,1,0:T(8,128)(2,1)} %select_bitcast_fusion.1), channel_id=1, source_target_pairs={{0,2},{1,3},{2,0},{3,1},{4,6},{5,7},{6,4},{7,5},{8,10},{9,11},{10,... | collective-permute-start | bytes 3145736 | tf_op jit(solution)/shard_map/ppermute | solution.py:529
  36.8 2.2 %copy-start.1 = (bf16[1,16,2,256,256]{4,3,2,1,0:T(8,128)(2,1)S(1)}, bf16[1,16,2,256,256]{4,3,2,1,0:T(8,128)(2,1)}, u32[]{:S(2)}) copy-start(bf16[1,16,2,256,256]{4,3,2,1,0:T(8,128)(2,1)} %refs_4_.3) | copy-start | bytes 12582916
  59.1 30.0 %collective-permute-start.5 = (bf16[4,256,512]{2,1,0:T(8,128)(2,1)S(1)}, bf16[4,256,512]{2,1,0:T(8,128)(2,1)S(1)}, u32[]{:S(2)}, u32[]{:S(2)}) collective-permute-start(bf16[4,256,512]{2,1,0:T(8,128)(2,1)S(1)} %get-tuple-element.36), channel_id=1, source_target_pairs={{0,4},{1,5},{2,30},{3,31},{4,8},{5,9},{6,2},{7,3},{8,12},{9,13},{1... | collective-permute-start | bytes 3145736 | tf_op jit(solution)/shard_map/ppermute | solution.py:529
  80.9 13.4 %collective-permute-start.6 = (bf16[1,256,512]{2,1,0:T(8,128)(2,1)S(1)}, bf16[1,256,512]{2,1,0:T(8,128)(2,1)S(1)}, u32[]{:S(2)}, u32[]{:S(2)}) collective-permute-start(bf16[1,256,512]{2,1,0:T(8,128)(2,1)S(1)} %get-tuple-element.37), channel_id=1, source_target_pairs={{0,4},{1,5},{2,30},{3,31},{4,8},{5,9},{6,2},{7,3},{8,12},{9,13},{1... | collective-permute-start | bytes 786440 | tf_op jit(solution)/shard_map/ppermute | solution.py:529
  82.5 11.8 %collective-permute-start.7 = (bf16[1,256,512]{2,1,0:T(8,128)(2,1)S(1)}, bf16[1,256,512]{2,1,0:T(8,128)(2,1)S(1)}, u32[]{:S(2)}, u32[]{:S(2)}) collective-permute-start(bf16[1,256,512]{2,1,0:T(8,128)(2,1)S(1)} %get-tuple-element.38), channel_id=1, source_target_pairs={{0,2},{1,3},{2,5},{4,6},{5,7},{6,9},{8,10},{9,11},{10,13},{12,14},... | collective-permute-start | bytes 786440 | tf_op jit(solution)/shard_map/ppermute | solution.py:529
  87.8 27.9 %collective-permute-start.9 = (bf16[1,256,512]{2,1,0:T(8,128)(2,1)S(1)}, bf16[1,256,512]{2,1,0:T(8,128)(2,1)S(1)}, u32[]{:S(2)}, u32[]{:S(2)}) collective-permute-start(bf16[1,256,512]{2,1,0:T(8,128)(2,1)S(1)} %get-tuple-element.44), channel_id=1, source_target_pairs={{1,30},{2,0},{3,1},{5,2},{6,4},{7,5},{9,6},{10,8},{11,9},{13,10},{... | collective-permute-start | bytes 786440 | tf_op jit(solution)/shard_map/ppermute | solution.py:529
  94.3 45.4 %collective-permute-start.8 = (bf16[4,256,512]{2,1,0:T(8,128)(2,1)S(1)}, bf16[4,256,512]{2,1,0:T(8,128)(2,1)S(1)}, u32[]{:S(2)}, u32[]{:S(2)}) collective-permute-start(bf16[4,256,512]{2,1,0:T(8,128)(2,1)S(1)} %get-tuple-element.43), channel_id=1, source_target_pairs={{0,4},{1,5},{2,30},{3,31},{4,8},{5,9},{6,2},{7,3},{8,12},{9,13},{1... | collective-permute-start | bytes 3145736 | tf_op jit(solution)/shard_map/ppermute | solution.py:529
  114.3 47.3 %collective-permute-start.12 = (bf16[4,2,256,256]{3,2,1,0:T(8,128)(2,1)S(1)}, bf16[4,2,256,256]{3,2,1,0:T(8,128)(2,1)S(1)}, u32[]{:S(2)}, u32[]{:S(2)}) collective-permute-start(bf16[4,2,256,256]{3,2,1,0:T(8,128)(2,1)S(1)} %get-tuple-element.47), channel_id=1, source_target_pairs={{0,30},{1,31},{2,4},{3,5},{4,2},{5,3},{6,8},{7,9},{8,6},{9,7},{10,... | collective-permute-start | bytes 3145736 | tf_op jit(solution)/shard_map/ppermute | solution.py:529
  160.5 1.0 copy-start.2
  161.5 36.4 %collective-permute-start.13 = (bf16[4,2,256,256]{3,2,1,0:T(8,128)(2,1)}, bf16[4,2,256,256]{3,2,1,0:T(8,128)(2,1)S(1)}, u32[]{:S(2)}, u32[]{:S(2)}) collective-permute-start(bf16[4,2,256,256]{3,2,1,0:T(8,128)(2,1)} %get-tuple-element.48), channel_id=1, source_target_pairs={{0,30},{1,31},{2,4},{3,5},{4,2},{5,3},{6,8},{7,9},{8,6},{9,7},{10,... | collective-permute-start | bytes 3145736 | tf_op jit(solution)/shard_map/ppermute | solution.py:529
  166.9 27.7 %collective-permute-start.14 = (bf16[1,256,256]{2,1,0:T(8,128)(2,1)S(1)}, bf16[1,256,256]{2,1,0:T(8,128)(2,1)S(1)}, u32[]{:S(2)}, u32[]{:S(2)}) collective-permute-start(bf16[1,256,256]{2,1,0:T(8,128)(2,1)S(1)} %get-tuple-element.52), channel_id=1, source_target_pairs={{1,30},{5,2},{9,6},{13,10},{17,14},{21,18},{25,22},{29,26}} | collective-permute-start | bytes 393224 | tf_op jit(solution)/shard_map/ppermute | solution.py:529
  177.3 13.9 %collective-permute-start.10 = (f32[2]{0:T(128)S(1)}, f32[2]{0:T(128)S(1)}, u32[]{:S(2)}, u32[]{:S(2)}) collective-permute-start(f32[2]{0:T(128)S(1)} %psum.7), channel_id=1, source_target_pairs={{2,4},{3,5},{6,8},{7,9},{10,12},{11,13},{14,16},{15,17},{18,20},{1... | collective-permute-start | bytes 32 | tf_op jit(solution)/shard_map/ppermute | solution.py:529
  178.6 13.2 %collective-permute-start.11 = (f32[1]{0:T(128)}, f32[1]{0:T(128)}, u32[]{:S(2)}, u32[]{:S(2)}) collective-permute-start(f32[1]{0:T(128)} %get-tuple-element.56), channel_id=1, source_target_pairs={{0,4},{1,5},{4,8},{5,9},{8,12},{9,13},{12,16},{13,17},{16,20},{17,... | collective-permute-start | bytes 20 | tf_op jit(solution)/shard_map/ppermute | solution.py:529
  194.6 1.2 copy-start.3

commit v4 on v3

--- a/solution.py
+++ b/solution.py
@@ -120,79 +120,85 @@
         run_copies(odd_plan, semaphores)
 
 
-def first_plans(late, half, early, operands, left, right):
+def chunk_sizes(half):
+    early = max(half // 2, 1)
+    return early, early - 1
+
+
+def cut(line, first, count, place):
+    plan = []
+    for source, start, size in line:
+        low, high = max(first, start), min(first + count, start + size)
+        if low < high:
+            plan.append((source(low - start, high - low), place(low - first, high - low)))
+    return plan
+
+
+def whole(ref):
+    return lambda start, size: ref.at[pl.ds(start, size)]
+
+
+def plane(ref, s):
+    return lambda start, size: ref.at[pl.ds(start, size), s]
+
+
+def first_plans(first_of, count, half, early, operands, left, right):
     own, got_early, got_late, edge, corner = operands
     own = own.at[0]
-    if late:
-        n = half - early
-        even = [
-            (own.at[pl.ds(early - 1, n + 1)], left),
-            (got_early.at[pl.ds(early, 1), 0], right.at[pl.ds(0, 1), 0]),
-            (got_late.at[pl.ds(0, n), 0], right.at[pl.ds(1, n), 0]),
-            (got_early.at[pl.ds(early - 1, 2), 1], right.at[pl.ds(0, 2), 1]),
+    late, sectors = half - early, 2 * half
+
+    def plans(first, left_line, right_line, extra):
+        zero_line = [(plane(ref, 0), start, size) for ref, start, size in right_line]
+        one_line = [(plane(ref, 1), start, size) for ref, start, size in right_line]
+        return [
+            *cut([(whole(ref), start, size) for ref, start, size in left_line], first - 1, count + 1, whole(left)),
+            *cut(zero_line, first, count + 1, plane(right, 0)),
+            *cut(one_line + extra, first - 1, count + 1, plane(right, 1)),
         ]
-        if n > 1:
-            even.append((got_late.at[pl.ds(0, n - 1), 1], right.at[pl.ds(2, n - 1), 1]))
-        odd = [
-            (got_early.at[pl.ds(early, 1)], left.at[pl.ds(0, 1)]),
-            (got_late.at[pl.ds(0, n)], left.at[pl.ds(1, n)]),
-            (own.at[pl.ds(half + early, n), 0], right.at[pl.ds(0, n), 0]),
-            (edge.at[pl.ds(0, 1), 0], right.at[pl.ds(n, 1), 0]),
-            (own.at[pl.ds(half + early - 1, n + 1), 1], right.at[pl.ds(0, n + 1), 1]),
+
+    even = plans(
+        first_of[0],
+        [(edge, -1, 1), (own, 0, sectors)],
+        [(got_early, 0, early + 1), (got_late, early + 1, late)],
+        [(whole(corner), -1, 1)],
+    )
+    odd = plans(
+        first_of[1],
+        [(got_late, half - 1, late), (got_early, sectors - early - 1, early + 1)],
+        [(own, 0, sectors), (edge, sectors, 1)],
+        [],
+    )
+    return even, odd
+
+
+def second_plans(first_of, count, half, early, operands, left, right):
+    keep_early, keep_late, carried_early, carried_late, far, near = operands
+    late, sectors = half - early, 2 * half
+
+    def plans(first, left_line, right_line):
+        return [
+            *cut([(whole(ref), start, size) for ref, start, size in left_line], first - 1, count + 1, whole(left)),
+            *cut([(whole(ref), start, size) for ref, start, size in right_line], first, count + 1, whole(right)),
         ]
-    else:
-        n = early
-        even = [
-            (edge, left.at[pl.ds(0, 1)]),
-            (own.at[pl.ds(0, n)], left.at[pl.ds(1, n)]),
-            (got_early.at[pl.ds(0, n + 1), 0], right.at[pl.ds(0, n + 1), 0]),
-            (corner, right.at[pl.ds(0, 1), 1]),
-            (got_early.at[pl.ds(0, n), 1], right.at[pl.ds(1, n), 1]),
-        ]
-        odd = [
-            (got_early, left),
-            (own.at[pl.ds(half, n + 1), 0], right.at[pl.ds(0, n + 1), 0]),
-            (own.at[pl.ds(half - 1, n + 1), 1], right.at[pl.ds(0, n + 1), 1]),
-        ]
-    return even, odd
-
-
-def second_plans(late, half, early, operands, left, right):
-    keep_early, keep_late, carried_early, carried_next, carried_late, beside = operands
-    if late:
-        n = half - early
-        even = [
-            (carried_early.at[pl.ds(early - 1, 1)], left.at[pl.ds(0, 1)]),
-            (carried_late, left.at[pl.ds(1, n)]),
-            (keep_late, right.at[pl.ds(0, n)]),
-            (beside, right.at[pl.ds(n, 1)]),
-        ]
-        odd = [
-            (keep_early.at[pl.ds(early - 1, 1)], left.at[pl.ds(0, 1)]),
-            (keep_late, left.at[pl.ds(1, n)]),
-            (carried_late, right.at[pl.ds(0, n)]),
-            (beside, right.at[pl.ds(n, 1)]),
-        ]
-    else:
-        n = early
-        even = [
-            (beside, left.at[pl.ds(0, 1)]),
-            (carried_early, left.at[pl.ds(1, n)]),
-            (keep_early, right.at[pl.ds(0, n)]),
-            (keep_late.at[pl.ds(0, 1)], right.at[pl.ds(n, 1)]),
-        ]
-        odd = [
-            (beside, left.at[pl.ds(0, 1)]),
-            (keep_early, left.at[pl.ds(1, n)]),
-            (carried_early, right.at[pl.ds(0, n)]),
-            (carried_next, right.at[pl.ds(n, 1)]),
-        ]
+
+    even = plans(
+        first_of[0],
+        [(far, -1, 1), (carried_early, 0, early), (carried_late, early, late)],
+        [(keep_early, 0, early), (keep_late, early, late), (near, half, 1)],
+    )
+    odd = plans(
+        first_of[1],
+        [(near, half - 1, 1), (keep_late, half, late), (keep_early, sectors - early, early)],
+        [(carried_late, half, late), (carried_early, sectors - early, early), (far, sectors, 1)],
+    )
     return even, odd
 
 
 def pair_kernel(second, late, sectors, refs):
     half = sectors // 2
-    early = half // 2
+    early, next_early = chunk_sizes(half)
+    part = next_early if second else early
+    first_of = (part, half) if late else (0, sectors - part)
     sizes, partner_sizes, ranks, couplings = refs[:4]
     operand_count = 6 if second else 5
     operands = refs[4 : 4 + operand_count]
@@ -215,11 +221,11 @@
     count, kept, double = sample_ref.shape
     width = double // 2
     plans = second_plans if second else first_plans
-    run_by_parity(*plans(late, half, early, operands, left_ref, right_ref), in_semaphores)
+    run_by_parity(*plans(first_of, count, half, early, operands, left_ref, right_ref), in_semaphores)
 
     parity = lax.rem(lax.axis_index("chain"), 2)
     is_even = parity == 0
-    first = lax.axis_index("block") * sectors + parity * half + (early if late else 0)
+    first = lax.axis_index("block") * sectors + jnp.where(is_even, *first_of)
     bond = parity if second else 1 - parity
     total = sizes.shape[2]
 
@@ -366,20 +372,17 @@
             coef_ref[m] = rounded
 
 
+    basis_first = basis_ref.at[pl.ds(0, 1)]
+    coef_last = coef_ref.at[pl.ds(count - 1, 1)]
     if second:
         even, odd = [(basis_ref, send), (coef_ref, keep)], [(coef_ref, send), (basis_ref, keep)]
-        if not late:
-            both = [(basis_ref.at[pl.ds(0, 1), 1], extras[0])]
+        if extras:
+            even.append((basis_ref.at[pl.ds(0, 1), 1], extras[0]))
+            odd.append((basis_ref.at[pl.ds(0, 1), 1], extras[0]))
     else:
         even, odd = [(coef_ref, send), (basis_ref, keep)], [(basis_ref, send), (coef_ref, keep)]
-        if late:
-            both = [(coef_ref.at[pl.ds(count - 1, 1)], extras[0])]
-            even.append((coef_ref.at[pl.ds(0, 1)], extras[1]))
-            odd.append((basis_ref.at[pl.ds(0, 1)], extras[1]))
-        else:
-            both = [(basis_ref.at[pl.ds(0, 1)], extras[0])]
-    if not (second and late):
-        even, odd = even + both, odd + both
+        even.append((coef_last if late else basis_first, extras[0]))
+        odd.append((basis_first if late else coef_last, extras[0]))
     run_by_parity(even, odd, out_semaphores)
 
 
@@ -388,13 +391,14 @@
     width = double // 2
     sectors = sizes.shape[2] // lax.axis_size("block")
     half = sectors // 2
-    early = half // 2
-    count = half - early if late else early
+    early, next_early = chunk_sizes(half)
+    part = next_early if second else early
+    count = half - part if late else part
     block = (2, width, kept) if second else (kept, double)
     coef_block = (2, kept, width) if second else (kept, double)
-    extra = [(1, width, kept)] if second else [(1, kept, double)]
-    if late:
-        extra = [] if second else extra * 2
+    extra = [(1, kept, double)]
+    if second:
+        extra = [(1, width, kept)] if not late or next_early == 0 else []
     left_shape = (count + 1, kept, double) if second else (count + 1, 2, width, width)
     vmem = pl.BlockSpec(memory_space=pltpu.VMEM)
     smem = pl.BlockSpec(memory_space=pltpu.SMEM)
@@ -423,8 +427,8 @@
             pltpu.VMEM((count, kept, kept), jnp.float32),
             pltpu.VMEM((count, kept, kept), jnp.float32),
             pltpu.VMEM((kept // LANES, PANEL * SUB, LANES), jnp.float32),
-            pltpu.SemaphoreType.DMA((5,)),
-            pltpu.SemaphoreType.DMA((4,)),
+            pltpu.SemaphoreType.DMA((8,)),
+            pltpu.SemaphoreType.DMA((3,)),
         ],
         compiler_params=pltpu.CompilerParams(vmem_limit_bytes=32 * 2**20),
         cost_estimate=pl.CostEstimate(
@@ -436,28 +440,29 @@
 
 
 def place_kernel(last, half, scale_ref, refs):
-    early = half // 2
-    n = half - early
+    _, early = chunk_sizes(half)
+    late, sectors = half - early, 2 * half
     if last:
-        returned, _, out, buffer, in_semaphores, out_semaphores = refs
-        parts = [(returned, half + early, n)]
-        odd = [
-            (returned.at[pl.ds(0, n), 0], out.at[0, pl.ds(early, n), 0]),
-            (returned.at[pl.ds(0, n), 1], out.at[0, pl.ds(early - 1, n), 1]),
-        ]
+        returned_late, _, out, buffer, in_semaphores, out_semaphores = refs
+        even_line = [(returned_late, half, late)]
+        odd_line = [(returned_late, early, late)]
+        lower_line = []
     else:
-        keep_early, keep_late, returned, lower, out, buffer, in_semaphores, out_semaphores = refs
-        parts = [(keep_early, 0, early), (keep_late, early, n), (returned, half, early)]
-        odd = [
-            (returned.at[pl.ds(0, early), 0], out.at[0, pl.ds(0, early), 0]),
-            (keep_early.at[pl.ds(0, early), 0], out.at[0, pl.ds(half, early), 0]),
-            (keep_early.at[pl.ds(0, early), 1], out.at[0, pl.ds(half - 1, early), 1]),
-            (keep_late.at[pl.ds(0, n), 0], out.at[0, pl.ds(half + early, n), 0]),
-            (keep_late.at[pl.ds(0, n), 1], out.at[0, pl.ds(half + early - 1, n), 1]),
-            (lower, out.at[0, pl.ds(2 * half - 1, 1), 1]),
-        ]
-        if early > 1:
-            odd.append((returned.at[pl.ds(1, early - 1), 1], out.at[0, pl.ds(0, early - 1), 1]))
+        if early:
+            keep_late, lower, keep_early, returned_early = refs[:4]
+            even_line = [(keep_early, 0, early), (keep_late, early, late), (returned_early, sectors - early, early)]
+            odd_line = [(returned_early, 0, early), (keep_late, half, late), (keep_early, sectors - early, early)]
+        else:
+            keep_late, lower = refs[:2]
+            even_line, odd_line = [(keep_late, 0, late)], [(keep_late, half, late)]
+        lower_line = [(whole(lower), sectors, 1)]
+        out, buffer, in_semaphores, out_semaphores = refs[-4:]
+    target = out.at[0]
+    zero_line = [(plane(ref, 0), start, size) for ref, start, size in odd_line]
+    one_line = [(plane(ref, 1), start, size) for ref, start, size in odd_line]
+    odd = cut(zero_line, 0, sectors, plane(target, 0))
+    odd += cut(one_line + lower_line, 1, sectors, plane(target, 1))
+    parts = even_line
     is_even = lax.rem(lax.axis_index("chain"), 2) == 0
 
     @pl.when(jnp.logical_not(is_even))
@@ -494,7 +499,7 @@
 
 def place(last, half, scale, operands, site):
     anywhere = pl.BlockSpec(memory_space=pl.ANY)
-    early = half // 2
+    _, early = chunk_sizes(half)
     rows = half - early if last else half + early
 
     def kernel(scale_ref, *refs):
@@ -544,7 +549,7 @@
 def body(site_tensors, sketch, bond_sizes, kept_ranks, couplings):
     sectors = site_tensors.shape[1]
     half = sectors // 2
-    early = half // 2
+    early, next_early = chunk_sizes(half)
     width = site_tensors.shape[-1]
     kept = sketch.shape[1]
     parts = lax.axis_size("block")
@@ -561,50 +566,55 @@
         )
 
     across = by_parity(lambda c, b: (c + 1, b), lambda c, b: (c - 1, b))
-    got_early = move(pick(own[half - 1 : half + early], own[: early + 1]), across)
+    got_early = move(pick(own[sectors - early - 1 :], own[: early + 1]), across)
     partner_sizes = move(bond_sizes, across)
     edge = move(
         pick(own[-1:], own[:1]), by_parity(lambda c, b: (c, b + 1), lambda c, b: (c, b - 1))
     )
     corner = move(own[-1:, 1], by_parity(nowhere, lambda c, b: (c - 1, b + 1)))
-    sent = pick(own[half + early :], own[early + 1 : half + 1])
+    sent = pick(own[half - 1 : sectors - early - 1], own[early + 1 : half + 1])
     sent, got_early = lax.optimization_barrier((sent, got_early))
     got_late = move(sent, across)
-    send_early, keep_early, norm_early, basis_first = update(
+    send_early, keep_early, norm_early, halo_early = update(
         False, False, site_tensors, got_early, got_early, edge, corner
     )
 
     along = by_parity(lambda c, b: (c + 2, b), lambda c, b: (c - 2, b))
+    far = move(
+        halo_early, by_parity(lambda c, b: (c - 1, b - 1), lambda c, b: (c + 1, b + 1))
+    )
     carried_early = move(send_early, along)
-    basis_above = move(
-        basis_first, by_parity(lambda c, b: (c - 1, b - 1), lambda c, b: (c - 1, b))
-    )
-    send_late, keep_late, norm_late, coef_last, send_next = update(
+    send_late, keep_late, norm_late, halo_late = update(
         False, True, site_tensors, got_early, got_late, edge, corner
     )
     norm_even = jnp.sum(norm_early) + jnp.sum(norm_late)
-    carried_next = move(send_next, along)
-    coef_below = move(
-        coef_last, by_parity(lambda c, b: (c + 1, b), lambda c, b: (c + 1, b + 1))
-    )
-    send_late, carried_early, carried_next, coef_below = lax.optimization_barrier(
-        (send_late, carried_early, carried_next, coef_below)
-    )
+    send_late, carried_early = lax.optimization_barrier((send_late, carried_early))
+    near = move(halo_late, across)
     carried_late = move(send_late, along)
 
     back = by_parity(lambda c, b: (c - 1, b), lambda c, b: (c + 1, b))
-    send_early, kept_early, norm_early, lower_first = update(
-        True, False, keep_early, keep_late, carried_early, carried_next, carried_next, coef_below
-    )
-    returned_early = move(send_early, back)
+    norm_odd = 0.0
+    first_parts = ()
+    if next_early:
+        send_early, kept_early, norm_early, lower_first = update(
+            True, False, keep_early, keep_early, carried_early, carried_early, far, far
+        )
+        norm_odd = jnp.sum(norm_early)
+        send_early, carried_late = lax.optimization_barrier((send_early, carried_late))
+        returned_early = move(send_early, back)
+        first_parts = (kept_early, returned_early)
+    send_late, kept_late, norm_late, *lower = update(
+        True, True, keep_early, keep_late, carried_early, carried_late, far, near
+    )
+    if next_early == 0:
+        lower_first = lower[0]
     lower_above = move(lower_first, by_parity(lambda c, b: (c - 1, b - 1), nowhere))
-    send_late, kept_late, norm_late = update(
-        True, True, keep_early, keep_late, carried_early, carried_next, carried_late, basis_above
-    )
-    send_late, returned_early = lax.optimization_barrier((send_late, returned_early))
+    if next_early:
+        send_late, returned_early = lax.optimization_barrier((send_late, returned_early))
+        first_parts = (kept_early, returned_early)
     returned_late = move(send_late, back)
 
-    norm_odd = jnp.sum(norm_early) + jnp.sum(norm_late)
+    norm_odd = norm_odd + jnp.sum(norm_late)
     norms = lax.psum(jnp.stack([norm_even, norm_odd]), "block")
     from_left = move(norms, by_parity(nowhere, lambda c, b: (c + 1, b)))
     from_second = move(norms[:1], by_parity(lambda c, b: (c + 2, b), nowhere))
@@ -613,9 +623,7 @@
     scale = scale * jnp.sqrt(target / (scale * scale * (norms[1] + from_left[1])))
     scale = scale[None]
 
-    site = place(
-        False, half, scale, (kept_early, kept_late, returned_early, lower_above), site_tensors
-    )
+    site = place(False, half, scale, (kept_late, lower_above, *first_parts), site_tensors)
     return place(True, half, scale, (returned_late, site), site_tensors)
 
 

time: 200 us -> 183 us (0.915)
  waiting for transfers between devices: 64 us -> 43 us
  starting transfers between devices: 22.5 us -> 26.2 us
    ppermute x15 -> x14, waiting for transfers between devices: 64 us -> 43 us  [move(): return lax.ppermute(value, ('chain', 'block'), pairs)]
    ppermute x15 -> x14, starting transfers between devices: 22.5 us -> 26.2 us  [move(): return lax.ppermute(value, ('chain', 'block'), pairs)]
    unnamed x17 -> x19, local copies, waits for them, and re-layouts: 4.53 us -> 5 us
  transfers between devices with their start and end apart: 15 -> 14, of which waited for: 4 -> 4; matrix products, arithmetic and copies ran while one was open for 3% -> 3% of each run, Pallas kernels for 42% -> 46%
where the time goes in v4:
time: 183 us
  Pallas kernels  85 us (46%)
  waiting for transfers between devices  43 us (23%)
  starting transfers between devices  26.2 us (14%)
  blocking collectives  9.04 us (5%)
  local copies, waits for them, and re-layouts  7.17 us (4%)
  other arithmetic  6.86 us (4%)
  between operations  5.67 us (3%)
    pallas_call x4, Pallas kernels, pair_update(): pl.pallas_call(kernel, out_shape=[jax.ShapeDtypeStruct((count, *block), j...  81.5 us
    ppermute x14, waiting for transfers between devices, move(): return lax.ppermute(value, ('chain', 'block'), pairs)  43 us
    ppermute x14, starting transfers between devices, move(): return lax.ppermute(value, ('chain', 'block'), pairs)  26.2 us
    psum x1, blocking collectives, body(): norms = lax.psum(jnp.stack([norm_even, norm_odd]), 'block')  9.04 us
    unnamed x19, local copies, waits for them, and re-layouts  5 us
    select_n x3, other arithmetic, pick(): return jnp.where(is_even, even_value, odd_value)  4.18 us
  transfers between devices with their start and end apart: 14, of which 4 were waited for; matrix products, arithmetic and copies ran while one was open for 3% of the time, Pallas kernels for 46%

profile of v4, /device:TPU:0, one launch (start us, length us, event | category | flops | bytes accessed | tf_op | source)
XLA Modules:
  0.0 182.9 jit_solution(12375500867100874737)
XLA Ops:
  0.0 3.1 %select_bitcast_fusion = bf16[5,2,256,256]{3,2,1,0:T(8,128)(2,1)} fusion(bf16[1,16,2,256,256]{4,3,2,1,0:T(8,128)(2,1)} %refs_4_.3, pred[]{:T(512)S(6)} %eq.5), kind=kLoop, calls=%fused_computation | loop fusion | flops 655360 | bytes 3932161 | tf_op jit(solution)/shard_map/jit(_where)/select_n | solution.py:561
  3.1 2.9 %collective-permute-start.1 = (bf16[5,2,256,256]{3,2,1,0:T(8,128)(2,1)}, bf16[5,2,256,256]{3,2,1,0:T(8,128)(2,1)S(1)}, u32[]{:S(2)}, u32[]{:S(2)}) collective-permute-start(bf16[5,2,256,256]{3,2,1,0:T(8,128)(2,1)} %select_bitcast_fusion), channel_id=1, source_target_pairs={{0,2},{1,3},{2,0},{3,1},{4,6},{5,7},{6,4},{7,5},{8,10},{9,11},{10,... | collective-permute-start | bytes 3932168 | tf_op jit(solution)/shard_map/ppermute | solution.py:534
  6.0 0.9 slice_bitcast_fusion
  7.7 2.2 %collective-permute-start.2 = (bf16[1,2,256,256]{3,2,1,0:T(8,128)(2,1)S(1)}, bf16[1,2,256,256]{3,2,1,0:T(8,128)(2,1)S(1)}, u32[]{:S(2)}, u32[]{:S(2)}) collective-permute-start(bf16[1,2,256,256]{3,2,1,0:T(8,128)(2,1)S(1)} %select_bitcast_fusion.2), channel_id=1, source_target_pairs={{0,1},{3,2},{4,5},{7,6},{8,9},{11,10},{12,13},{15,14},{16,17},{19,... | collective-permute-start | bytes 786440 | tf_op jit(solution)/shard_map/ppermute | solution.py:534
  10.0 1.1 select_bitcast_fusion.1
  11.2 23.8 %collective-permute-done.1.refs_5_.refs_6_ = bf16[5,2,256,256]{3,2,1,0:T(8,128)(2,1)S(1)} collective-permute-done((bf16[5,2,256,256]{3,2,1,0:T(8,128)(2,1)}, bf16[5,2,256,256]{3,2,1,0:T(8,128)(2,1)S(1)}, u32[]{:S(2)}, u32[]{:S(2)}) %collective-permute-start.1) | collective-permute-done | bytes 1310752 | tf_op jit(solution)/shard_map/ppermute | solution.py:534
  35.0 1.7 collective-permute-start.4
  36.8 2.2 %copy-done.1 = bf16[1,16,2,256,256]{4,3,2,1,0:T(8,128)(2,1)S(1)} copy-done((bf16[1,16,2,256,256]{4,3,2,1,0:T(8,128)(2,1)S(1)}, bf16[1,16,2,256,256]{4,3,2,1,0:T(8,128)(2,1)}, u32[]{:S(2)}) %copy-start.1) | copy-done | bytes 4194328
  39.0 20.1 %shard_map.55 = (bf16[4,256,512]{2,1,0:T(8,128)(2,1)S(1)}, bf16[4,256,512]{2,1,0:T(8,128)(2,1)S(1)}, f32[1,512]{1,0:T(1,128)S(1)}, bf16[1,256,512]{2,1,0:T(8,128)(2,1)S(1)}) custom-call(s32[1,2,32]{2,1,0:T(2,128)S(1)} %copy-done.5, s32[1,2,32]{2,1,0:T(2,128)S(1)} %collective-permute-done.refs_1_, s32[1,2,32]{2,1,0:T(2,128)S(1)} %copy-done.6, ...), custom_call_target="tpu_custom_call" | custom-call | flops 53687091200 | bytes 8388608 | tf_op jit(solution)/shard_map/pallas_call | solution.py:410
  59.7 1.6 collective-permute-start.5
  61.3 20.3 %shard_map.56 = (bf16[4,256,512]{2,1,0:T(8,128)(2,1)S(1)}, bf16[4,256,512]{2,1,0:T(8,128)(2,1)S(1)}, f32[1,512]{1,0:T(1,128)S(1)}, bf16[1,256,512]{2,1,0:T(8,128)(2,1)S(1)}) custom-call(s32[1,2,32]{2,1,0:T(2,128)S(1)} %copy-done.5, s32[1,2,32]{2,1,0:T(2,128)S(1)} %collective-permute-done.refs_1_, s32[1,2,32]{2,1,0:T(2,128)S(1)} %copy-done.6, ...), custom_call_target="tpu_custom_call" | custom-call | flops 53687091200 | bytes 8388608 | tf_op jit(solution)/shard_map/pallas_call | solution.py:410
  81.6 4.9 %collective-permute-start.8 = (bf16[1,256,512]{2,1,0:T(8,128)(2,1)S(1)}, bf16[1,256,512]{2,1,0:T(8,128)(2,1)S(1)}, u32[]{:S(2)}, u32[]{:S(2)}) collective-permute-start(bf16[1,256,512]{2,1,0:T(8,128)(2,1)S(1)} %get-tuple-element.42), channel_id=1, source_target_pairs={{0,2},{1,3},{2,0},{3,1},{4,6},{5,7},{6,4},{7,5},{8,10},{9,11},{10,... | collective-permute-start | bytes 786440 | tf_op jit(solution)/shard_map/ppermute | solution.py:534
  86.7 1.9 %collective-permute-start.7 = (bf16[4,256,512]{2,1,0:T(8,128)(2,1)S(1)}, bf16[4,256,512]{2,1,0:T(8,128)(2,1)S(1)}, u32[]{:S(2)}, u32[]{:S(2)}) collective-permute-start(bf16[4,256,512]{2,1,0:T(8,128)(2,1)S(1)} %get-tuple-element.40), channel_id=1, source_target_pairs={{0,4},{1,5},{2,30},{3,31},{4,8},{5,9},{6,2},{7,3},{8,12},{9,13},{1... | collective-permute-start | bytes 3145736 | tf_op jit(solution)/shard_map/ppermute | solution.py:534
  88.6 18.1 %shard_map.57 = (bf16[3,2,256,256]{3,2,1,0:T(8,128)(2,1)S(1)}, bf16[3,2,256,256]{3,2,1,0:T(8,128)(2,1)S(1)}, f32[1,512]{1,0:T(1,128)S(1)}, bf16[1,256,256]{2,1,0:T(8,128)(2,1)S(1)}) custom-call(s32[1,2,32]{2,1,0:T(2,128)S(1)} %copy-done.5, s32[1,2,32]{2,1,0:T(2,128)S(1)} %collective-permute-done.refs_1_, s32[1,2,32]{2,1,0:T(2,128)S(1)} %copy-done.6, ...), custom_call_target="tpu_custom_call" | custom-call | flops 50331648000 | bytes 6291456 | tf_op jit(solution)/shard_map/pallas_call | solution.py:410
  107.4 6.4 %collective-permute-done.7.refs_7_ = bf16[4,256,512]{2,1,0:T(8,128)(2,1)S(1)} collective-permute-done((bf16[4,256,512]{2,1,0:T(8,128)(2,1)S(1)}, bf16[4,256,512]{2,1,0:T(8,128)(2,1)S(1)}, u32[]{:S(2)}, u32[]{:S(2)}) %collective-permute-start.7) | collective-permute-done | bytes 1048608 | tf_op jit(solution)/shard_map/ppermute | solution.py:534
  113.8 5.7 %collective-permute-start.11 = (bf16[3,2,256,256]{3,2,1,0:T(8,128)(2,1)S(1)}, bf16[3,2,256,256]{3,2,1,0:T(8,128)(2,1)S(1)}, u32[]{:S(2)}, u32[]{:S(2)}) collective-permute-start(bf16[3,2,256,256]{3,2,1,0:T(8,128)(2,1)S(1)} %get-tuple-element.45), channel_id=1, source_target_pairs={{0,30},{1,31},{2,4},{3,5},{4,2},{5,3},{6,8},{7,9},{8,6},{9,7},{10,... | collective-permute-start | bytes 2359304 | tf_op jit(solution)/shard_map/ppermute | solution.py:534
  119.4 23.0 %shard_map.58 = (bf16[5,2,256,256]{3,2,1,0:T(8,128)(2,1)}, bf16[5,2,256,256]{3,2,1,0:T(8,128)(2,1)S(1)}, f32[1,512]{1,0:T(1,128)S(1)}) custom-call(s32[1,2,32]{2,1,0:T(2,128)S(1)} %copy-done.5, s32[1,2,32]{2,1,0:T(2,128)S(1)} %collective-permute-done.refs_1_, s32[1,2,32]{2,1,0:T(2,128)S(1)} %copy-done.6, f32[1,2,3]{2,1,0:T(2,128)S(1)} %copy-done.7, ...), custom_call_target="tpu_custom_call" | custom-call | flops 57042534400 | bytes 10485760 | tf_op jit(solution)/shard_map/pallas_call | solution.py:410
  149.3 9.0 %psum.7 = f32[2]{0:T(128)S(1)} all-reduce(f32[2]{0:T(128)S(1)} %pad_maximum_fusion), channel_id=1, replica_groups=mesh['chain'=16,'block'=2] {'block'}, use_global_device_ids=true, to_apply=%region_4.5 | all-reduce | flops 2 | bytes 16 | tf_op jit(solution)/shard_map/psum | solution.py:618
  159.0 1.3 collective-permute-start.9
  160.3 1.9 %collective-permute-start.10 = (f32[1]{0:T(128)}, f32[1]{0:T(128)}, u32[]{:S(2)}, u32[]{:S(2)}) collective-permute-start(f32[1]{0:T(128)} %get-tuple-element.54), channel_id=1, source_target_pairs={{0,4},{1,5},{4,8},{5,9},{8,12},{9,13},{12,16},{13,17},{16,20},{17,... | collective-permute-start | bytes 20 | tf_op jit(solution)/shard_map/ppermute | solution.py:534
  162.3 12.5 %collective-permute-done.9 = f32[2]{0:T(128)S(1)} collective-permute-done((f32[2]{0:T(128)S(1)}, f32[2]{0:T(128)S(1)}, u32[]{:S(2)}, u32[]{:S(2)}) %collective-permute-start.9) | collective-permute-done | bytes 40 | tf_op jit(solution)/shard_map/ppermute | solution.py:534
  178.1 1.1 copy-done.3
  179.2 2.0 %shard_map.59.refs_1_ = bf16[1,16,2,256,256]{4,3,2,1,0:T(8,128)(2,1)} custom-call(f32[1]{0:T(128)} %bitcast.10.scale_ref, bf16[5,2,256,256]{3,2,1,0:T(8,128)(2,1)S(1)} %get-tuple-element.47.refs_0_, bf16[1,256,256]{2,1,0:T(8,128)(2,1)S(1)} %collective-permute-done.13.refs_1_, bf16[3,2,256,256]{3,2,1,0:T(8,128)(2,1)S(1)} %get-tuple-element.49.refs_2_, ...), custom_call_target="tpu_custom_call" | custom-call | bytes 5767168 | tf_op jit(solution)/shard_map/pallas_call | solution.py:508
  181.2 1.5 shard_map.60
  (41 shorter events, 8.1 us)
Async XLA Ops:
  0.0 7.6 %copy-start = (bf16[1,16,2,256,256]{4,3,2,1,0:T(8,128)(2,1)S(1)}, bf16[1,16,2,256,256]{4,3,2,1,0:T(8,128)(2,1)}, u32[]{:S(2)}) copy-start(bf16[1,16,2,256,256]{4,3,2,1,0:T(8,128)(2,1)} %refs_4_.3) | copy-start | bytes 12582916
  3.1 31.9 %collective-permute-start.1 = (bf16[5,2,256,256]{3,2,1,0:T(8,128)(2,1)}, bf16[5,2,256,256]{3,2,1,0:T(8,128)(2,1)S(1)}, u32[]{:S(2)}, u32[]{:S(2)}) collective-permute-start(bf16[5,2,256,256]{3,2,1,0:T(8,128)(2,1)} %select_bitcast_fusion), channel_id=1, source_target_pairs={{0,2},{1,3},{2,0},{3,1},{4,6},{5,7},{6,4},{7,5},{8,10},{9,11},{10,... | collective-permute-start | bytes 3932168 | tf_op jit(solution)/shard_map/ppermute | solution.py:534
  6.0 30.7 %collective-permute-start = (s32[1,2,32]{2,1,0:T(2,128)}, s32[1,2,32]{2,1,0:T(2,128)S(1)}, u32[]{:S(2)}, u32[]{:S(2)}) collective-permute-start(s32[1,2,32]{2,1,0:T(2,128)} %refs_0_.7), channel_id=1, source_target_pairs={{0,2},{1,3},{2,0},{3,1},{4,6},{5,7},{6,4},{7,5},{8,10},{9,11},{10,... | collective-permute-start | bytes 776 | tf_op jit(solution)/shard_map/ppermute | solution.py:534
  6.9 29.8 %collective-permute-start.3 = (bf16[1,256,256]{2,1,0:T(8,128)(2,1)S(1)}, bf16[1,256,256]{2,1,0:T(8,128)(2,1)S(1)}, u32[]{:S(2)}, u32[]{:S(2)}) collective-permute-start(bf16[1,256,256]{2,1,0:T(8,128)(2,1)S(1)} %slice_bitcast_fusion), channel_id=1, source_target_pairs={{2,1},{6,5},{10,9},{14,13},{18,17},{22,21},{26,25},{30,29}} | collective-permute-start | bytes 393224 | tf_op jit(solution)/shard_map/ppermute | solution.py:534
  7.7 3.4 %copy-start.8 = (bf16[512,256]{1,0:T(8,128)(2,1)S(1)}, bf16[512,256]{1,0:T(8,128)(2,1)}, u32[]{:S(2)}) copy-start(bf16[512,256]{1,0:T(8,128)(2,1)} %param.6) | copy-start | bytes 786436
  7.7 29.1 %copy-start.5 = (s32[1,2,32]{2,1,0:T(2,128)S(1)}, s32[1,2,32]{2,1,0:T(2,128)}, u32[]{:S(2)}) copy-start(s32[1,2,32]{2,1,0:T(2,128)} %refs_0_.7) | copy-start | bytes 772
  7.7 29.1 %copy-start.6 = (s32[1,2,32]{2,1,0:T(2,128)S(1)}, s32[1,2,32]{2,1,0:T(2,128)}, u32[]{:S(2)}) copy-start(s32[1,2,32]{2,1,0:T(2,128)} %refs_2_.7) | copy-start | bytes 772
  7.7 29.1 %copy-start.7 = (f32[1,2,3]{2,1,0:T(2,128)S(1)}, f32[1,2,3]{2,1,0:T(2,128)}, u32[]{:S(2)}) copy-start(f32[1,2,3]{2,1,0:T(2,128)} %refs_3_.7) | copy-start | bytes 76
  7.7 29.0 %collective-permute-start.2 = (bf16[1,2,256,256]{3,2,1,0:T(8,128)(2,1)S(1)}, bf16[1,2,256,256]{3,2,1,0:T(8,128)(2,1)S(1)}, u32[]{:S(2)}, u32[]{:S(2)}) collective-permute-start(bf16[1,2,256,256]{3,2,1,0:T(8,128)(2,1)S(1)} %select_bitcast_fusion.2), channel_id=1, source_target_pairs={{0,1},{3,2},{4,5},{7,6},{8,9},{11,10},{12,13},{15,14},{16,17},{19,... | collective-permute-start | bytes 786440 | tf_op jit(solution)/shard_map/ppermute | solution.py:534
  35.0 26.3 %collective-permute-start.4 = (bf16[4,2,256,256]{3,2,1,0:T(8,128)(2,1)}, bf16[4,2,256,256]{3,2,1,0:T(8,128)(2,1)S(1)}, u32[]{:S(2)}, u32[]{:S(2)}) collective-permute-start(bf16[4,2,256,256]{3,2,1,0:T(8,128)(2,1)} %select_bitcast_fusion.1), channel_id=1, source_target_pairs={{0,2},{1,3},{2,0},{3,1},{4,6},{5,7},{6,4},{7,5},{8,10},{9,11},{10,... | collective-permute-start | bytes 3145736 | tf_op jit(solution)/shard_map/ppermute | solution.py:534
  36.8 2.2 %copy-start.1 = (bf16[1,16,2,256,256]{4,3,2,1,0:T(8,128)(2,1)S(1)}, bf16[1,16,2,256,256]{4,3,2,1,0:T(8,128)(2,1)}, u32[]{:S(2)}) copy-start(bf16[1,16,2,256,256]{4,3,2,1,0:T(8,128)(2,1)} %refs_4_.3) | copy-start | bytes 12582916
  59.0 29.6 %collective-permute-start.6 = (bf16[1,256,512]{2,1,0:T(8,128)(2,1)S(1)}, bf16[1,256,512]{2,1,0:T(8,128)(2,1)S(1)}, u32[]{:S(2)}, u32[]{:S(2)}) collective-permute-start(bf16[1,256,512]{2,1,0:T(8,128)(2,1)S(1)} %get-tuple-element.36), channel_id=1, source_target_pairs={{1,30},{2,5},{5,2},{6,9},{9,6},{10,13},{13,10},{14,17},{17,14},{18... | collective-permute-start | bytes 786440 | tf_op jit(solution)/shard_map/ppermute | solution.py:534
  59.7 27.0 %collective-permute-start.5 = (bf16[4,256,512]{2,1,0:T(8,128)(2,1)S(1)}, bf16[4,256,512]{2,1,0:T(8,128)(2,1)S(1)}, u32[]{:S(2)}, u32[]{:S(2)}) collective-permute-start(bf16[4,256,512]{2,1,0:T(8,128)(2,1)S(1)} %get-tuple-element.34), channel_id=1, source_target_pairs={{0,4},{1,5},{2,30},{3,31},{4,8},{5,9},{6,2},{7,3},{8,12},{9,13},{1... | collective-permute-start | bytes 3145736 | tf_op jit(solution)/shard_map/ppermute | solution.py:534
  81.6 37.8 %collective-permute-start.8 = (bf16[1,256,512]{2,1,0:T(8,128)(2,1)S(1)}, bf16[1,256,512]{2,1,0:T(8,128)(2,1)S(1)}, u32[]{:S(2)}, u32[]{:S(2)}) collective-permute-start(bf16[1,256,512]{2,1,0:T(8,128)(2,1)S(1)} %get-tuple-element.42), channel_id=1, source_target_pairs={{0,2},{1,3},{2,0},{3,1},{4,6},{5,7},{6,4},{7,5},{8,10},{9,11},{10,... | collective-permute-start | bytes 786440 | tf_op jit(solution)/shard_map/ppermute | solution.py:534
  86.7 27.0 %collective-permute-start.7 = (bf16[4,256,512]{2,1,0:T(8,128)(2,1)S(1)}, bf16[4,256,512]{2,1,0:T(8,128)(2,1)S(1)}, u32[]{:S(2)}, u32[]{:S(2)}) collective-permute-start(bf16[4,256,512]{2,1,0:T(8,128)(2,1)S(1)} %get-tuple-element.40), channel_id=1, source_target_pairs={{0,4},{1,5},{2,30},{3,31},{4,8},{5,9},{6,2},{7,3},{8,12},{9,13},{1... | collective-permute-start | bytes 3145736 | tf_op jit(solution)/shard_map/ppermute | solution.py:534
  106.7 0.7 copy-start.4
  113.8 28.7 %collective-permute-start.11 = (bf16[3,2,256,256]{3,2,1,0:T(8,128)(2,1)S(1)}, bf16[3,2,256,256]{3,2,1,0:T(8,128)(2,1)S(1)}, u32[]{:S(2)}, u32[]{:S(2)}) collective-permute-start(bf16[3,2,256,256]{3,2,1,0:T(8,128)(2,1)S(1)} %get-tuple-element.45), channel_id=1, source_target_pairs={{0,30},{1,31},{2,4},{3,5},{4,2},{5,3},{6,8},{7,9},{8,6},{9,7},{10,... | collective-permute-start | bytes 2359304 | tf_op jit(solution)/shard_map/ppermute | solution.py:534
  142.5 0.9 copy-start.2
  143.3 37.9 %collective-permute-start.12 = (bf16[5,2,256,256]{3,2,1,0:T(8,128)(2,1)}, bf16[5,2,256,256]{3,2,1,0:T(8,128)(2,1)S(1)}, u32[]{:S(2)}, u32[]{:S(2)}) collective-permute-start(bf16[5,2,256,256]{3,2,1,0:T(8,128)(2,1)} %get-tuple-element.46), channel_id=1, source_target_pairs={{0,30},{1,31},{2,4},{3,5},{4,2},{5,3},{6,8},{7,9},{8,6},{9,7},{10,... | collective-permute-start | bytes 3932168 | tf_op jit(solution)/shard_map/ppermute | solution.py:534
  148.7 29.4 %collective-permute-start.13 = (bf16[1,256,256]{2,1,0:T(8,128)(2,1)}, bf16[1,256,256]{2,1,0:T(8,128)(2,1)S(1)}, u32[]{:S(2)}, u32[]{:S(2)}) collective-permute-start(bf16[1,256,256]{2,1,0:T(8,128)(2,1)} %copy-done.4), channel_id=1, source_target_pairs={{1,30},{5,2},{9,6},{13,10},{17,14},{21,18},{25,22},{29,26}} | collective-permute-start | bytes 393224 | tf_op jit(solution)/shard_map/ppermute | solution.py:534
  159.0 15.8 %collective-permute-start.9 = (f32[2]{0:T(128)S(1)}, f32[2]{0:T(128)S(1)}, u32[]{:S(2)}, u32[]{:S(2)}) collective-permute-start(f32[2]{0:T(128)S(1)} %psum.7), channel_id=1, source_target_pairs={{2,4},{3,5},{6,8},{7,9},{10,12},{11,13},{14,16},{15,17},{18,20},{1... | collective-permute-start | bytes 32 | tf_op jit(solution)/shard_map/ppermute | solution.py:534
  160.3 15.1 %collective-permute-start.10 = (f32[1]{0:T(128)}, f32[1]{0:T(128)}, u32[]{:S(2)}, u32[]{:S(2)}) collective-permute-start(f32[1]{0:T(128)} %get-tuple-element.54), channel_id=1, source_target_pairs={{0,4},{1,5},{4,8},{5,9},{8,12},{9,13},{12,16},{13,17},{16,20},{17,... | collective-permute-start | bytes 20 | tf_op jit(solution)/shard_map/ppermute | solution.py:534
  178.1 1.1 copy-start.3

commit v5 on v4

--- a/solution.py
+++ b/solution.py
@@ -203,20 +203,18 @@
     operand_count = 6 if second else 5
     operands = refs[4 : 4 + operand_count]
     sketch_ref = refs[4 + operand_count]
-    outputs = refs[5 + operand_count : -11]
+    outputs = refs[5 + operand_count : -9]
     (
         left_ref,
         right_ref,
-        basis_ref,
-        coef_ref,
         two_ref,
         sample_ref,
         gram_ref,
         inverse_ref,
         rows_ref,
+        square_ref,
         in_semaphores,
-        out_semaphores,
-    ) = refs[-11:]
+    ) = refs[-9:]
     send, keep, norm_ref, *extras = outputs
     count, kept, double = sample_ref.shape
     width = double // 2
@@ -319,6 +317,8 @@
 
     lane = lax.broadcasted_iota(jnp.int32, (1, kept), 1)
     for tile in range(kept // LANES):
+        below = slice(tile * LANES, kept)
+
         @pl.loop(0, LANES // PANEL)
         def _(panel):
             first = pl.multiple_of(tile * LANES + panel * PANEL, PANEL)
@@ -339,13 +339,13 @@
                 )
                 inverse_ref[m, here, :] = jnp.where(lane < stop, solved, 0.0)
                 high, middle, low = in_parts(solved)
-                one = jnp.concatenate([high, high, middle, middle, high, low], axis=0)
+                one = jnp.concatenate([high, high, middle, middle, high, low], axis=0)[:, below]
                 two = jnp.concatenate([high, middle, high, middle, low, high], axis=0)
                 change = dot(one, two, FIRST)
-                kept_part = jnp.where((lane >= first) & (lane < stop), 0.0, gram_ref[m])
-                gram_ref[m] = kept_part - change
-
-    norm_ref[...] = jnp.zeros_like(norm_ref)
+                kept_part = jnp.where((lane >= first) & (lane < stop), 0.0, gram_ref[m, below, :])
+                gram_ref[m, below, :] = kept_part - change
+
+    square_ref[...] = jnp.zeros_like(square_ref)
 
     @pl.loop(0, count, unroll=min(UNROLL, count))
     def _(m):
@@ -356,34 +356,25 @@
         )
         solved = solved * math.sqrt(width)
         basis = solved.astype(jnp.bfloat16)
+        coef = dot(basis, two_ref[m], PLAIN)
+        square_ref[...] += jnp.sum(coef * coef, axis=0, keepdims=True)
         if second:
             for s in range(2):
-                turned = jnp.transpose(solved[:, s * width : (s + 1) * width])
-                basis_ref[m, s] = turned.astype(jnp.bfloat16)
+                span = slice(s * width, (s + 1) * width)
+                turned = jnp.transpose(solved[:, span])
+                send[m, s] = jnp.where(is_even, turned, coef[:, span]).astype(jnp.bfloat16)
+                keep[m, s] = jnp.where(is_even, coef[:, span], turned).astype(jnp.bfloat16)
         else:
-            basis_ref[m] = basis
-        coef = dot(basis, two_ref[m], PLAIN)
-        norm_ref[...] += jnp.sum(coef * coef, axis=0, keepdims=True)
-        rounded = coef.astype(jnp.bfloat16)
-        if second:
-            for s in range(2):
-                coef_ref[m, s] = rounded[:, s * width : (s + 1) * width]
-        else:
-            coef_ref[m] = rounded
-
-
-    basis_first = basis_ref.at[pl.ds(0, 1)]
-    coef_last = coef_ref.at[pl.ds(count - 1, 1)]
+            send[m] = jnp.where(is_even, coef, solved).astype(jnp.bfloat16)
+            keep[m] = jnp.where(is_even, solved, coef).astype(jnp.bfloat16)
+
+    norm_ref[0] = jnp.sum(square_ref[...])
     if second:
-        even, odd = [(basis_ref, send), (coef_ref, keep)], [(coef_ref, send), (basis_ref, keep)]
         if extras:
-            even.append((basis_ref.at[pl.ds(0, 1), 1], extras[0]))
-            odd.append((basis_ref.at[pl.ds(0, 1), 1], extras[0]))
+            extras[0][0] = send[0, 1]
     else:
-        even, odd = [(coef_ref, send), (basis_ref, keep)], [(basis_ref, send), (coef_ref, keep)]
-        even.append((coef_last if late else basis_first, extras[0]))
-        odd.append((basis_first if late else coef_last, extras[0]))
-    run_by_parity(even, odd, out_semaphores)
+        at = jnp.where(is_even, count - 1, 0) if late else jnp.where(is_even, 0, count - 1)
+        extras[0][0] = send[at] if late else keep[at]
 
 
 def pair_update(second, late, sizes, partner_sizes, ranks, couplings, operands, sketch_turned):
@@ -395,7 +386,6 @@
     part = next_early if second else early
     count = half - part if late else part
     block = (2, width, kept) if second else (kept, double)
-    coef_block = (2, kept, width) if second else (kept, double)
     extra = [(1, kept, double)]
     if second:
         extra = [(1, width, kept)] if not late or next_early == 0 else []
@@ -412,23 +402,21 @@
         out_shape=[
             jax.ShapeDtypeStruct((count, *block), jnp.bfloat16),
             jax.ShapeDtypeStruct((count, *block), jnp.bfloat16),
-            jax.ShapeDtypeStruct((1, double), jnp.float32),
+            jax.ShapeDtypeStruct((1,), jnp.float32),
             *(jax.ShapeDtypeStruct(shape, jnp.bfloat16) for shape in extra),
         ],
         in_specs=[smem] * 4 + [anywhere] * len(operands) + [vmem],
-        out_specs=[anywhere, anywhere, vmem] + [anywhere] * len(extra),
+        out_specs=[vmem, vmem, smem] + [vmem] * len(extra),
         scratch_shapes=[
             pltpu.VMEM(left_shape, jnp.bfloat16),
             pltpu.VMEM(left_shape, jnp.bfloat16),
-            pltpu.VMEM((count, *block), jnp.bfloat16),
-            pltpu.VMEM((count, *coef_block), jnp.bfloat16),
             pltpu.VMEM((count, double, double), jnp.bfloat16),
             pltpu.VMEM((count, kept, double), jnp.float32),
             pltpu.VMEM((count, kept, kept), jnp.float32),
             pltpu.VMEM((count, kept, kept), jnp.float32),
             pltpu.VMEM((kept // LANES, PANEL * SUB, LANES), jnp.float32),
+            pltpu.VMEM((1, double), jnp.float32),
             pltpu.SemaphoreType.DMA((8,)),
-            pltpu.SemaphoreType.DMA((3,)),
         ],
         compiler_params=pltpu.CompilerParams(vmem_limit_bytes=32 * 2**20),
         cost_estimate=pl.CostEstimate(
@@ -439,7 +427,7 @@
     )(sizes, partner_sizes, ranks, couplings, *operands, sketch_turned)
 
 
-def place_kernel(last, half, scale_ref, refs):
+def place_kernel(last, half, target, norm_refs, refs):
     _, early = chunk_sizes(half)
     late, sectors = half - early, 2 * half
     if last:
@@ -457,11 +445,11 @@
             even_line, odd_line = [(keep_late, 0, late)], [(keep_late, half, late)]
         lower_line = [(whole(lower), sectors, 1)]
         out, buffer, in_semaphores, out_semaphores = refs[-4:]
-    target = out.at[0]
+    site = out.at[0]
     zero_line = [(plane(ref, 0), start, size) for ref, start, size in odd_line]
     one_line = [(plane(ref, 1), start, size) for ref, start, size in odd_line]
-    odd = cut(zero_line, 0, sectors, plane(target, 0))
-    odd += cut(one_line + lower_line, 1, sectors, plane(target, 1))
+    odd = cut(zero_line, 0, sectors, plane(site, 0))
+    odd += cut(one_line + lower_line, 1, sectors, plane(site, 1))
     parts = even_line
     is_even = lax.rem(lax.axis_index("chain"), 2) == 0
 
@@ -471,6 +459,12 @@
 
     @pl.when(is_even)
     def _():
+        norms, from_left, from_second = norm_refs
+        rows = (1, buffer.shape[-1])
+        norm_even = jnp.full(rows, from_left[0] + from_second[0], jnp.float32)
+        norm_odd = jnp.full(rows, norms[1] + from_left[1], jnp.float32)
+        scale_even = jnp.sqrt(target / norm_even)
+        scale = scale_even * jnp.sqrt(target / (scale_even * scale_even * norm_odd))
         coming, going, filled = [], [], 0
         for index, (source, start, size) in enumerate(parts):
             room = buffer.at[pl.ds(filled, size)]
@@ -488,7 +482,7 @@
             @pl.loop(filled, filled + size)
             def _(sector):
                 for s in range(2):
-                    scaled = buffer[sector, s].astype(jnp.float32) * scale_ref[0]
+                    scaled = buffer[sector, s].astype(jnp.float32) * scale
                     buffer[sector, s] = scaled.astype(jnp.bfloat16)
 
             going[index].start()
@@ -497,30 +491,30 @@
             copy.wait()
 
 
-def place(last, half, scale, operands, site):
+def place(last, half, target, norms, operands, site):
     anywhere = pl.BlockSpec(memory_space=pl.ANY)
     _, early = chunk_sizes(half)
     rows = half - early if last else half + early
 
-    def kernel(scale_ref, *refs):
-        place_kernel(last, half, scale_ref, refs)
+    def kernel(*refs):
+        place_kernel(last, half, target, refs[:3], refs[3:])
 
     return pl.pallas_call(
         kernel,
         out_shape=jax.ShapeDtypeStruct(site.shape, site.dtype),
-        in_specs=[pl.BlockSpec(memory_space=pltpu.SMEM)] + [anywhere] * len(operands),
+        in_specs=[pl.BlockSpec(memory_space=pltpu.SMEM)] * 3 + [anywhere] * len(operands),
         out_specs=anywhere,
         scratch_shapes=[
             pltpu.VMEM((rows, *site.shape[2:]), site.dtype),
             pltpu.SemaphoreType.DMA((3,)),
             pltpu.SemaphoreType.DMA((7,)),
         ],
-        input_output_aliases={2: 0} if last else {},
+        input_output_aliases={4: 0} if last else {},
         compiler_params=pltpu.CompilerParams(vmem_limit_bytes=16 * 2**20),
         cost_estimate=pl.CostEstimate(
             flops=0, bytes_accessed=2 * rows * site.size // site.shape[1] * 2, transcendentals=0
         ),
-    )(scale, *operands)
+    )(*norms, *operands)
 
 
 def move(value, target_of):
@@ -587,10 +581,12 @@
     send_late, keep_late, norm_late, halo_late = update(
         False, True, site_tensors, got_early, got_late, edge, corner
     )
-    norm_even = jnp.sum(norm_early) + jnp.sum(norm_late)
-    send_late, carried_early = lax.optimization_barrier((send_late, carried_early))
+    norm_even = norm_early + norm_late
+    send_late, halo_late, carried_early = lax.optimization_barrier(
+        (send_late, halo_late, carried_early)
+    )
+    carried_late = move(send_late, along)
     near = move(halo_late, across)
-    carried_late = move(send_late, along)
 
     back = by_parity(lambda c, b: (c - 1, b), lambda c, b: (c + 1, b))
     norm_odd = 0.0
@@ -599,7 +595,7 @@
         send_early, kept_early, norm_early, lower_first = update(
             True, False, keep_early, keep_early, carried_early, carried_early, far, far
         )
-        norm_odd = jnp.sum(norm_early)
+        norm_odd = norm_early
         send_early, carried_late = lax.optimization_barrier((send_early, carried_late))
         returned_early = move(send_early, back)
         first_parts = (kept_early, returned_early)
@@ -614,17 +610,14 @@
         first_parts = (kept_early, returned_early)
     returned_late = move(send_late, back)
 
-    norm_odd = norm_odd + jnp.sum(norm_late)
-    norms = lax.psum(jnp.stack([norm_even, norm_odd]), "block")
+    norms = lax.psum(joined(norm_even, norm_odd + norm_late), "block")
     from_left = move(norms, by_parity(nowhere, lambda c, b: (c + 1, b)))
-    from_second = move(norms[:1], by_parity(lambda c, b: (c + 2, b), nowhere))
+    from_second = move(norms, by_parity(lambda c, b: (c + 2, b), nowhere))
     target = float(sectors * parts * kept * width)
-    scale = jnp.sqrt(target / (from_left[0] + from_second[0]))
-    scale = scale * jnp.sqrt(target / (scale * scale * (norms[1] + from_left[1])))
-    scale = scale[None]
-
-    site = place(False, half, scale, (kept_late, lower_above, *first_parts), site_tensors)
-    return place(True, half, scale, (returned_late, site), site_tensors)
+    norms = (norms, from_left, from_second)
+
+    site = place(False, half, target, norms, (kept_late, lower_above, *first_parts), site_tensors)
+    return place(True, half, target, norms, (returned_late, site), site_tensors)
 
 
 def solution(mesh):

time: 183 us -> 187 us (1.022)
  waiting for transfers between devices: 43 us -> 56.9 us
  starting transfers between devices: 26.2 us -> 21.9 us
  other arithmetic: 6.86 us -> 3.97 us
  between operations: 5.67 us -> 2.95 us
  Pallas kernels: 85 us -> 87.3 us
  local copies, waits for them, and re-layouts: 7.17 us -> 5.26 us
    ppermute x14, waiting for transfers between devices: 43 us -> 56.9 us  [move(): return lax.ppermute(value, ('chain', 'block'), pairs)]
    ppermute x14, starting transfers between devices: 26.2 us -> 21.9 us  [move(): return lax.ppermute(value, ('chain', 'block'), pairs)]
    reduce_sum x4 -> x0, other arithmetic: 2.6 us -> none  [the longest x2 1.3 us: body(): norm_even = jnp.sum(norm_early) + jnp.sum(norm_late)]
    unnamed x19 -> x17, local copies, waits for them, and re-layouts: 5 us -> 4.35 us
  transfers between devices with their start and end apart: 14 -> 14, of which waited for: 4 -> 5; matrix products, arithmetic and copies ran while one was open for 3% -> 1% of each run, Pallas kernels for 46% -> 46%
where the time goes in v5:
time: 187 us; the launch traced here: 186 us
  Pallas kernels  87.3 us (47%)
  waiting for transfers between devices  56.9 us (30%)
  starting transfers between devices  21.9 us (12%)
  blocking collectives  8.03 us (4%)
  local copies, waits for them, and re-layouts  5.26 us (3%)
  other arithmetic  3.97 us (2%)
  between operations  2.95 us (2%)
    pallas_call x4, Pallas kernels, pair_update(): pl.pallas_call(kernel, out_shape=[jax.ShapeDtypeStruct((count, *block), j...  82.6 us
    ppermute x14, waiting for transfers between devices, move(): return lax.ppermute(value, ('chain', 'block'), pairs)  56.9 us
    ppermute x14, starting transfers between devices, move(): return lax.ppermute(value, ('chain', 'block'), pairs)  21.9 us
    psum x1, blocking collectives, body(): norms = lax.psum(joined(norm_even, norm_odd + norm_late), 'block')  8.03 us
    pallas_call x2, Pallas kernels, place(): pl.pallas_call(kernel, out_shape=jax.ShapeDtypeStruct(site.shape, site.dt...  4.66 us
    unnamed x17, local copies, waits for them, and re-layouts  4.35 us
    select_n x3, other arithmetic, pick(): return jnp.where(is_even, even_value, odd_value)  3.89 us
  transfers between devices with their start and end apart: 14, of which 5 were waited for; matrix products, arithmetic and copies ran while one was open for 1% of the time, Pallas kernels for 46%

profile of v5, /device:TPU:0, one launch (start us, length us, event | category | flops | bytes accessed | tf_op | source)
XLA Modules:
  0.0 186.3 jit_solution(11645890682452081656)
XLA Ops:
  0.0 3.1 %select_bitcast_fusion = bf16[5,2,256,256]{3,2,1,0:T(8,128)(2,1)} fusion(bf16[1,16,2,256,256]{4,3,2,1,0:T(8,128)(2,1)} %refs_4_.3, pred[]{:T(512)S(6)} %eq.5), kind=kLoop, calls=%fused_computation | loop fusion | flops 655360 | bytes 3932161 | tf_op jit(solution)/shard_map/jit(_where)/select_n | solution.py:555
  3.1 2.9 %collective-permute-start.1 = (bf16[5,2,256,256]{3,2,1,0:T(8,128)(2,1)}, bf16[5,2,256,256]{3,2,1,0:T(8,128)(2,1)S(1)}, u32[]{:S(2)}, u32[]{:S(2)}) collective-permute-start(bf16[5,2,256,256]{3,2,1,0:T(8,128)(2,1)} %select_bitcast_fusion), channel_id=1, source_target_pairs={{0,2},{1,3},{2,0},{3,1},{4,6},{5,7},{6,4},{7,5},{8,10},{9,11},{10,... | collective-permute-start | bytes 3932168 | tf_op jit(solution)/shard_map/ppermute | solution.py:528
  8.4 2.2 %collective-permute-start.2 = (bf16[1,2,256,256]{3,2,1,0:T(8,128)(2,1)}, bf16[1,2,256,256]{3,2,1,0:T(8,128)(2,1)S(1)}, u32[]{:S(2)}, u32[]{:S(2)}) collective-permute-start(bf16[1,2,256,256]{3,2,1,0:T(8,128)(2,1)} %select_bitcast_fusion.2), channel_id=1, source_target_pairs={{0,1},{3,2},{4,5},{7,6},{8,9},{11,10},{12,13},{15,14},{16,17},{19,... | collective-permute-start | bytes 786440 | tf_op jit(solution)/shard_map/ppermute | solution.py:528
  10.9 24.1 %collective-permute-done.1.refs_5_.refs_6_ = bf16[5,2,256,256]{3,2,1,0:T(8,128)(2,1)S(1)} collective-permute-done((bf16[5,2,256,256]{3,2,1,0:T(8,128)(2,1)}, bf16[5,2,256,256]{3,2,1,0:T(8,128)(2,1)S(1)}, u32[]{:S(2)}, u32[]{:S(2)}) %collective-permute-start.1) | collective-permute-done | bytes 1310752 | tf_op jit(solution)/shard_map/ppermute | solution.py:528
  35.0 1.7 collective-permute-start.4
  36.8 2.2 %copy-done.1 = bf16[1,16,2,256,256]{4,3,2,1,0:T(8,128)(2,1)S(1)} copy-done((bf16[1,16,2,256,256]{4,3,2,1,0:T(8,128)(2,1)S(1)}, bf16[1,16,2,256,256]{4,3,2,1,0:T(8,128)(2,1)}, u32[]{:S(2)}) %copy-start.1) | copy-done | bytes 4194328
  39.0 20.4 %shard_map.55 = (bf16[4,256,512]{2,1,0:T(8,128)(2,1)S(1)}, bf16[4,256,512]{2,1,0:T(8,128)(2,1)S(1)}, f32[1]{0:T(128)}, bf16[1,256,512]{2,1,0:T(8,128)(2,1)S(1)}) custom-call(s32[1,2,32]{2,1,0:T(2,128)S(1)} %copy-done.4, s32[1,2,32]{2,1,0:T(2,128)S(1)} %collective-permute-done.refs_1_, s32[1,2,32]{2,1,0:T(2,128)S(1)} %copy-done.5, f32[1,2,3]{2,1,0:T(2,128)S(1)} %copy-done.6, ...), custom_call_target="tpu_custom_call" | custom-call | flops 53687091200 | bytes 8388608 | tf_op jit(solution)/shard_map/pallas_call | solution.py:400
  60.1 1.6 collective-permute-start.5
  61.7 20.7 %shard_map.56 = (bf16[4,256,512]{2,1,0:T(8,128)(2,1)S(1)}, bf16[4,256,512]{2,1,0:T(8,128)(2,1)S(1)}, f32[1]{0:T(128)}, bf16[1,256,512]{2,1,0:T(8,128)(2,1)S(1)}) custom-call(s32[1,2,32]{2,1,0:T(2,128)S(1)} %copy-done.4, s32[1,2,32]{2,1,0:T(2,128)S(1)} %collective-permute-done.refs_1_, s32[1,2,32]{2,1,0:T(2,128)S(1)} %copy-done.5, f32[1,2,3]{2,1,0:T(2,128)S(1)} %copy-done.6, ...), custom_call_target="tpu_custom_call" | custom-call | flops 53687091200 | bytes 8388608 | tf_op jit(solution)/shard_map/pallas_call | solution.py:400
  82.3 4.7 %collective-permute-done.5.refs_6_.refs_7_ = bf16[4,256,512]{2,1,0:T(8,128)(2,1)S(1)} collective-permute-done((bf16[4,256,512]{2,1,0:T(8,128)(2,1)S(1)}, bf16[4,256,512]{2,1,0:T(8,128)(2,1)S(1)}, u32[]{:S(2)}, u32[]{:S(2)}) %collective-permute-start.5) | collective-permute-done | bytes 1048608 | tf_op jit(solution)/shard_map/ppermute | solution.py:528
  87.1 2.1 %collective-permute-start.8 = (bf16[1,256,512]{2,1,0:T(8,128)(2,1)S(1)}, bf16[1,256,512]{2,1,0:T(8,128)(2,1)S(1)}, u32[]{:S(2)}, u32[]{:S(2)}) collective-permute-start(bf16[1,256,512]{2,1,0:T(8,128)(2,1)S(1)} %get-tuple-element.44), channel_id=1, source_target_pairs={{0,2},{1,3},{2,0},{3,1},{4,6},{5,7},{6,4},{7,5},{8,10},{9,11},{10,... | collective-permute-start | bytes 786440 | tf_op jit(solution)/shard_map/ppermute | solution.py:528
  89.7 18.3 %shard_map.57 = (bf16[3,2,256,256]{3,2,1,0:T(8,128)(2,1)S(1)}, bf16[3,2,256,256]{3,2,1,0:T(8,128)(2,1)S(1)}, f32[1]{0:T(128)}, bf16[1,256,256]{2,1,0:T(8,128)(2,1)}) custom-call(s32[1,2,32]{2,1,0:T(2,128)S(1)} %copy-done.4, s32[1,2,32]{2,1,0:T(2,128)S(1)} %collective-permute-done.refs_1_, s32[1,2,32]{2,1,0:T(2,128)S(1)} %copy-done.5, ...), custom_call_target="tpu_custom_call" | custom-call | flops 50331648000 | bytes 6291456 | tf_op jit(solution)/shard_map/pallas_call | solution.py:400
  108.0 9.8 %collective-permute-done.7.refs_7_ = bf16[4,256,512]{2,1,0:T(8,128)(2,1)S(1)} collective-permute-done((bf16[4,256,512]{2,1,0:T(8,128)(2,1)S(1)}, bf16[4,256,512]{2,1,0:T(8,128)(2,1)S(1)}, u32[]{:S(2)}, u32[]{:S(2)}) %collective-permute-start.7) | collective-permute-done | bytes 1048608 | tf_op jit(solution)/shard_map/ppermute | solution.py:528
  117.8 4.6 %collective-permute-start.11 = (bf16[3,2,256,256]{3,2,1,0:T(8,128)(2,1)S(1)}, bf16[3,2,256,256]{3,2,1,0:T(8,128)(2,1)S(1)}, u32[]{:S(2)}, u32[]{:S(2)}) collective-permute-start(bf16[3,2,256,256]{3,2,1,0:T(8,128)(2,1)S(1)} %get-tuple-element.47), channel_id=1, source_target_pairs={{0,30},{1,31},{2,4},{3,5},{4,2},{5,3},{6,8},{7,9},{8,6},{9,7},{10,... | collective-permute-start | bytes 2359304 | tf_op jit(solution)/shard_map/ppermute | solution.py:528
  122.3 23.2 %shard_map.58 = (bf16[5,2,256,256]{3,2,1,0:T(8,128)(2,1)}, bf16[5,2,256,256]{3,2,1,0:T(8,128)(2,1)S(1)}, f32[1]{0:T(128)}) custom-call(s32[1,2,32]{2,1,0:T(2,128)S(1)} %copy-done.4, s32[1,2,32]{2,1,0:T(2,128)S(1)} %collective-permute-done.refs_1_, s32[1,2,32]{2,1,0:T(2,128)S(1)} %copy-done.5, f32[1,2,3]{2,1,0:T(2,128)S(1)} %copy-done.6, ...), custom_call_target="tpu_custom_call" | custom-call | flops 57042534400 | bytes 10485760 | tf_op jit(solution)/shard_map/pallas_call | solution.py:400
  146.4 1.1 collective-permute-start.12
  150.8 8.0 %psum.7.refs_0_ = f32[2]{0:T(128)S(1)} all-reduce(f32[2]{0:T(128)S(1)} %pad_maximum_fusion), channel_id=1, replica_groups=mesh['chain'=16,'block'=2] {'block'}, use_global_device_ids=true, to_apply=%region_0.1 | all-reduce | flops 2 | bytes 16 | tf_op jit(solution)/shard_map/psum | solution.py:613
  158.8 1.9 %collective-permute-start.10 = (f32[2]{0:T(128)S(1)}, f32[2]{0:T(128)S(1)}, u32[]{:S(2)}, u32[]{:S(2)}) collective-permute-start(f32[2]{0:T(128)S(1)} %psum.7.refs_0_), channel_id=1, source_target_pairs={{0,4},{1,5},{4,8},{5,9},{8,12},{9,13},{12,16},{13,17},{16,20},{17,... | collective-permute-start | bytes 32 | tf_op jit(solution)/shard_map/ppermute | solution.py:528
  160.7 1.3 collective-permute-start.9
  162.1 4.9 %collective-permute-done.10.refs_2_ = f32[2]{0:T(128)S(1)} collective-permute-done((f32[2]{0:T(128)S(1)}, f32[2]{0:T(128)S(1)}, u32[]{:S(2)}, u32[]{:S(2)}) %collective-permute-start.10) | collective-permute-done | bytes 40 | tf_op jit(solution)/shard_map/ppermute | solution.py:528
  167.0 13.3 %collective-permute-done.9.refs_1_ = f32[2]{0:T(128)S(1)} collective-permute-done((f32[2]{0:T(128)S(1)}, f32[2]{0:T(128)S(1)}, u32[]{:S(2)}, u32[]{:S(2)}) %collective-permute-start.9) | collective-permute-done | bytes 40 | tf_op jit(solution)/shard_map/ppermute | solution.py:528
  180.3 1.1 copy-done.3
  181.4 2.6 %shard_map.59.refs_4_ = bf16[1,16,2,256,256]{4,3,2,1,0:T(8,128)(2,1)} custom-call(f32[2]{0:T(128)S(1)} %psum.7.refs_0_, f32[2]{0:T(128)S(1)} %collective-permute-done.9.refs_1_, f32[2]{0:T(128)S(1)} %collective-permute-done.10.refs_2_, bf16[5,2,256,256]{3,2,1,0:T(8,128)(2,1)S(1)} %get-tuple-element.49.refs_3_, ...), custom_call_target="tpu_custom_call" | custom-call | bytes 5767168 | tf_op jit(solution)/shard_map/pallas_call | solution.py:502
  184.0 2.1 %shard_map.60 = bf16[1,16,2,256,256]{4,3,2,1,0:T(8,128)(2,1)} custom-call(f32[2]{0:T(128)S(1)} %psum.7.refs_0_, f32[2]{0:T(128)S(1)} %collective-permute-done.9.refs_1_, f32[2]{0:T(128)S(1)} %collective-permute-done.10.refs_2_, bf16[5,2,256,256]{3,2,1,0:T(8,128)(2,1)S(1)} %collective-permute-done.12.refs_3_, ...), custom_call_target="tpu_custom_call", output_to_operand_aliasing={{}: (4, {})} | custom-call | bytes 2621440 | tf_op jit(solution)/shard_map/pallas_call | solution.py:502
  (33 shorter events, 5.4 us)
Async XLA Ops:
  0.0 7.6 %copy-start = (bf16[1,16,2,256,256]{4,3,2,1,0:T(8,128)(2,1)S(1)}, bf16[1,16,2,256,256]{4,3,2,1,0:T(8,128)(2,1)}, u32[]{:S(2)}) copy-start(bf16[1,16,2,256,256]{4,3,2,1,0:T(8,128)(2,1)} %refs_4_.3) | copy-start | bytes 12582916
  3.1 31.9 %collective-permute-start.1 = (bf16[5,2,256,256]{3,2,1,0:T(8,128)(2,1)}, bf16[5,2,256,256]{3,2,1,0:T(8,128)(2,1)S(1)}, u32[]{:S(2)}, u32[]{:S(2)}) collective-permute-start(bf16[5,2,256,256]{3,2,1,0:T(8,128)(2,1)} %select_bitcast_fusion), channel_id=1, source_target_pairs={{0,2},{1,3},{2,0},{3,1},{4,6},{5,7},{6,4},{7,5},{8,10},{9,11},{10,... | collective-permute-start | bytes 3932168 | tf_op jit(solution)/shard_map/ppermute | solution.py:528
  6.0 30.7 %collective-permute-start = (s32[1,2,32]{2,1,0:T(2,128)}, s32[1,2,32]{2,1,0:T(2,128)S(1)}, u32[]{:S(2)}, u32[]{:S(2)}) collective-permute-start(s32[1,2,32]{2,1,0:T(2,128)} %refs_0_.7), channel_id=1, source_target_pairs={{0,2},{1,3},{2,0},{3,1},{4,6},{5,7},{6,4},{7,5},{8,10},{9,11},{10,... | collective-permute-start | bytes 776 | tf_op jit(solution)/shard_map/ppermute | solution.py:528
  6.9 29.8 %collective-permute-start.3 = (bf16[1,256,256]{2,1,0:T(8,128)(2,1)S(1)}, bf16[1,256,256]{2,1,0:T(8,128)(2,1)S(1)}, u32[]{:S(2)}, u32[]{:S(2)}) collective-permute-start(bf16[1,256,256]{2,1,0:T(8,128)(2,1)S(1)} %slice_bitcast_fusion), channel_id=1, source_target_pairs={{2,1},{6,5},{10,9},{14,13},{18,17},{22,21},{26,25},{30,29}} | collective-permute-start | bytes 393224 | tf_op jit(solution)/shard_map/ppermute | solution.py:528
  8.4 2.4 %copy-start.7 = (bf16[512,256]{1,0:T(8,128)(2,1)S(1)}, bf16[512,256]{1,0:T(8,128)(2,1)}, u32[]{:S(2)}) copy-start(bf16[512,256]{1,0:T(8,128)(2,1)} %param.6) | copy-start | bytes 786436
  8.4 28.4 %copy-start.4 = (s32[1,2,32]{2,1,0:T(2,128)S(1)}, s32[1,2,32]{2,1,0:T(2,128)}, u32[]{:S(2)}) copy-start(s32[1,2,32]{2,1,0:T(2,128)} %refs_0_.7) | copy-start | bytes 772
  8.4 28.4 %copy-start.5 = (s32[1,2,32]{2,1,0:T(2,128)S(1)}, s32[1,2,32]{2,1,0:T(2,128)}, u32[]{:S(2)}) copy-start(s32[1,2,32]{2,1,0:T(2,128)} %refs_2_.7) | copy-start | bytes 772
  8.4 28.4 %copy-start.6 = (f32[1,2,3]{2,1,0:T(2,128)S(1)}, f32[1,2,3]{2,1,0:T(2,128)}, u32[]{:S(2)}) copy-start(f32[1,2,3]{2,1,0:T(2,128)} %refs_3_.7) | copy-start | bytes 76
  8.4 28.4 %collective-permute-start.2 = (bf16[1,2,256,256]{3,2,1,0:T(8,128)(2,1)}, bf16[1,2,256,256]{3,2,1,0:T(8,128)(2,1)S(1)}, u32[]{:S(2)}, u32[]{:S(2)}) collective-permute-start(bf16[1,2,256,256]{3,2,1,0:T(8,128)(2,1)} %select_bitcast_fusion.2), channel_id=1, source_target_pairs={{0,1},{3,2},{4,5},{7,6},{8,9},{11,10},{12,13},{15,14},{16,17},{19,... | collective-permute-start | bytes 786440 | tf_op jit(solution)/shard_map/ppermute | solution.py:528
  35.0 26.7 %collective-permute-start.4 = (bf16[4,2,256,256]{3,2,1,0:T(8,128)(2,1)S(1)}, bf16[4,2,256,256]{3,2,1,0:T(8,128)(2,1)S(1)}, u32[]{:S(2)}, u32[]{:S(2)}) collective-permute-start(bf16[4,2,256,256]{3,2,1,0:T(8,128)(2,1)S(1)} %select_bitcast_fusion.1), channel_id=1, source_target_pairs={{0,2},{1,3},{2,0},{3,1},{4,6},{5,7},{6,4},{7,5},{8,10},{9,11},{10,... | collective-permute-start | bytes 3145736 | tf_op jit(solution)/shard_map/ppermute | solution.py:528
  36.8 2.2 %copy-start.1 = (bf16[1,16,2,256,256]{4,3,2,1,0:T(8,128)(2,1)S(1)}, bf16[1,16,2,256,256]{4,3,2,1,0:T(8,128)(2,1)}, u32[]{:S(2)}) copy-start(bf16[1,16,2,256,256]{4,3,2,1,0:T(8,128)(2,1)} %refs_4_.3) | copy-start | bytes 12582916
  59.4 30.2 %collective-permute-start.6 = (bf16[1,256,512]{2,1,0:T(8,128)(2,1)S(1)}, bf16[1,256,512]{2,1,0:T(8,128)(2,1)S(1)}, u32[]{:S(2)}, u32[]{:S(2)}) collective-permute-start(bf16[1,256,512]{2,1,0:T(8,128)(2,1)S(1)} %get-tuple-element.38), channel_id=1, source_target_pairs={{1,30},{2,5},{5,2},{6,9},{9,6},{10,13},{13,10},{14,17},{17,14},{18... | collective-permute-start | bytes 786440 | tf_op jit(solution)/shard_map/ppermute | solution.py:528
  60.1 27.0 %collective-permute-start.5 = (bf16[4,256,512]{2,1,0:T(8,128)(2,1)S(1)}, bf16[4,256,512]{2,1,0:T(8,128)(2,1)S(1)}, u32[]{:S(2)}, u32[]{:S(2)}) collective-permute-start(bf16[4,256,512]{2,1,0:T(8,128)(2,1)S(1)} %get-tuple-element.36), channel_id=1, source_target_pairs={{0,4},{1,5},{2,30},{3,31},{4,8},{5,9},{6,2},{7,3},{8,12},{9,13},{1... | collective-permute-start | bytes 3145736 | tf_op jit(solution)/shard_map/ppermute | solution.py:528
  87.1 35.2 %collective-permute-start.8 = (bf16[1,256,512]{2,1,0:T(8,128)(2,1)S(1)}, bf16[1,256,512]{2,1,0:T(8,128)(2,1)S(1)}, u32[]{:S(2)}, u32[]{:S(2)}) collective-permute-start(bf16[1,256,512]{2,1,0:T(8,128)(2,1)S(1)} %get-tuple-element.44), channel_id=1, source_target_pairs={{0,2},{1,3},{2,0},{3,1},{4,6},{5,7},{6,4},{7,5},{8,10},{9,11},{10,... | collective-permute-start | bytes 786440 | tf_op jit(solution)/shard_map/ppermute | solution.py:528
  89.1 28.6 %collective-permute-start.7 = (bf16[4,256,512]{2,1,0:T(8,128)(2,1)S(1)}, bf16[4,256,512]{2,1,0:T(8,128)(2,1)S(1)}, u32[]{:S(2)}, u32[]{:S(2)}) collective-permute-start(bf16[4,256,512]{2,1,0:T(8,128)(2,1)S(1)} %get-tuple-element.42), channel_id=1, source_target_pairs={{0,4},{1,5},{2,30},{3,31},{4,8},{5,9},{6,2},{7,3},{8,12},{9,13},{1... | collective-permute-start | bytes 3145736 | tf_op jit(solution)/shard_map/ppermute | solution.py:528
  117.8 27.8 %collective-permute-start.11 = (bf16[3,2,256,256]{3,2,1,0:T(8,128)(2,1)S(1)}, bf16[3,2,256,256]{3,2,1,0:T(8,128)(2,1)S(1)}, u32[]{:S(2)}, u32[]{:S(2)}) collective-permute-start(bf16[3,2,256,256]{3,2,1,0:T(8,128)(2,1)S(1)} %get-tuple-element.47), channel_id=1, source_target_pairs={{0,30},{1,31},{2,4},{3,5},{4,2},{5,3},{6,8},{7,9},{8,6},{9,7},{10,... | collective-permute-start | bytes 2359304 | tf_op jit(solution)/shard_map/ppermute | solution.py:528
  145.5 0.9 copy-start.2
  146.4 37.6 %collective-permute-start.12 = (bf16[5,2,256,256]{3,2,1,0:T(8,128)(2,1)}, bf16[5,2,256,256]{3,2,1,0:T(8,128)(2,1)S(1)}, u32[]{:S(2)}, u32[]{:S(2)}) collective-permute-start(bf16[5,2,256,256]{3,2,1,0:T(8,128)(2,1)} %get-tuple-element.48), channel_id=1, source_target_pairs={{0,30},{1,31},{2,4},{3,5},{4,2},{5,3},{6,8},{7,9},{8,6},{9,7},{10,... | collective-permute-start | bytes 3932168 | tf_op jit(solution)/shard_map/ppermute | solution.py:528
  147.5 14.6 %collective-permute-start.13 = (bf16[1,256,256]{2,1,0:T(8,128)(2,1)}, bf16[1,256,256]{2,1,0:T(8,128)(2,1)S(1)}, u32[]{:S(2)}, u32[]{:S(2)}) collective-permute-start(bf16[1,256,256]{2,1,0:T(8,128)(2,1)} %get-tuple-element.50), channel_id=1, source_target_pairs={{1,30},{5,2},{9,6},{13,10},{17,14},{21,18},{25,22},{29,26}} | collective-permute-start | bytes 393224 | tf_op jit(solution)/shard_map/ppermute | solution.py:528
  158.8 8.1 %collective-permute-start.10 = (f32[2]{0:T(128)S(1)}, f32[2]{0:T(128)S(1)}, u32[]{:S(2)}, u32[]{:S(2)}) collective-permute-start(f32[2]{0:T(128)S(1)} %psum.7.refs_0_), channel_id=1, source_target_pairs={{0,4},{1,5},{4,8},{5,9},{8,12},{9,13},{12,16},{13,17},{16,20},{17,... | collective-permute-start | bytes 32 | tf_op jit(solution)/shard_map/ppermute | solution.py:528
  160.7 19.5 %collective-permute-start.9 = (f32[2]{0:T(128)S(1)}, f32[2]{0:T(128)S(1)}, u32[]{:S(2)}, u32[]{:S(2)}) collective-permute-start(f32[2]{0:T(128)S(1)} %psum.7.refs_0_), channel_id=1, source_target_pairs={{2,4},{3,5},{6,8},{7,9},{10,12},{11,13},{14,16},{15,17},{18,20},{1... | collective-permute-start | bytes 32 | tf_op jit(solution)/shard_map/ppermute | solution.py:528
  180.3 1.1 copy-start.3

commit v6 on v5

--- a/solution.py
+++ b/solution.py
@@ -215,7 +215,10 @@
         square_ref,
         in_semaphores,
     ) = refs[-9:]
-    send, keep, norm_ref, *extras = outputs
+    if second and late:
+        send, send_last, keep, norm_ref, *extras = outputs
+    else:
+        send, keep, norm_ref, *extras = outputs
     count, kept, double = sample_ref.shape
     width = double // 2
     plans = second_plans if second else first_plans
@@ -347,8 +350,7 @@
 
     square_ref[...] = jnp.zeros_like(square_ref)
 
-    @pl.loop(0, count, unroll=min(UNROLL, count))
-    def _(m):
+    def finish(m, send, place):
         inverse_high, inverse_middle, _ = in_parts(inverse_ref[m])
         sample_high, sample_middle, _ = in_parts(sample_ref[m])
         solved = dot(inverse_high, sample_high, PLAIN) + (
@@ -362,11 +364,20 @@
             for s in range(2):
                 span = slice(s * width, (s + 1) * width)
                 turned = jnp.transpose(solved[:, span])
-                send[m, s] = jnp.where(is_even, turned, coef[:, span]).astype(jnp.bfloat16)
+                send[place, s] = jnp.where(is_even, turned, coef[:, span]).astype(jnp.bfloat16)
                 keep[m, s] = jnp.where(is_even, coef[:, span], turned).astype(jnp.bfloat16)
         else:
-            send[m] = jnp.where(is_even, coef, solved).astype(jnp.bfloat16)
+            send[place] = jnp.where(is_even, coef, solved).astype(jnp.bfloat16)
             keep[m] = jnp.where(is_even, solved, coef).astype(jnp.bfloat16)
+
+    pieces = [(0, send.shape[0], send)]
+    if second and late:
+        pieces.append((send.shape[0], send_last.shape[0], send_last))
+    for start, size, piece in pieces:
+
+        @pl.loop(0, size, unroll=min(UNROLL, size))
+        def _(index, start=start, piece=piece):
+            finish(start + index, piece, index)
 
     norm_ref[0] = jnp.sum(square_ref[...])
     if second:
@@ -389,6 +400,9 @@
     extra = [(1, kept, double)]
     if second:
         extra = [(1, width, kept)] if not late or next_early == 0 else []
+    pieces = [count]
+    if second and late:
+        pieces = [count - count // 2, count // 2]
     left_shape = (count + 1, kept, double) if second else (count + 1, 2, width, width)
     vmem = pl.BlockSpec(memory_space=pltpu.VMEM)
     smem = pl.BlockSpec(memory_space=pltpu.SMEM)
@@ -400,13 +414,13 @@
     return pl.pallas_call(
         kernel,
         out_shape=[
-            jax.ShapeDtypeStruct((count, *block), jnp.bfloat16),
+            *(jax.ShapeDtypeStruct((size, *block), jnp.bfloat16) for size in pieces),
             jax.ShapeDtypeStruct((count, *block), jnp.bfloat16),
             jax.ShapeDtypeStruct((1,), jnp.float32),
             *(jax.ShapeDtypeStruct(shape, jnp.bfloat16) for shape in extra),
         ],
         in_specs=[smem] * 4 + [anywhere] * len(operands) + [vmem],
-        out_specs=[vmem, vmem, smem] + [vmem] * len(extra),
+        out_specs=[vmem] * len(pieces) + [vmem, smem] + [vmem] * len(extra),
         scratch_shapes=[
             pltpu.VMEM(left_shape, jnp.bfloat16),
             pltpu.VMEM(left_shape, jnp.bfloat16),
@@ -430,19 +444,21 @@
 def place_kernel(last, half, target, norm_refs, refs):
     _, early = chunk_sizes(half)
     late, sectors = half - early, 2 * half
+    final = late // 2
+    main = late - final
     if last:
-        returned_late, _, out, buffer, in_semaphores, out_semaphores = refs
-        even_line = [(returned_late, half, late)]
-        odd_line = [(returned_late, early, late)]
+        returned_last, _, out, buffer, in_semaphores, out_semaphores = refs
+        even_line = [(returned_last, half + main, final)]
+        odd_line = [(returned_last, early + main, final)]
         lower_line = []
     else:
+        keep_late, returned_late, lower = refs[:3]
+        even_line = [(keep_late, early, late), (returned_late, half, main)]
+        odd_line = [(returned_late, early, main), (keep_late, half, late)]
         if early:
-            keep_late, lower, keep_early, returned_early = refs[:4]
-            even_line = [(keep_early, 0, early), (keep_late, early, late), (returned_early, sectors - early, early)]
-            odd_line = [(returned_early, 0, early), (keep_late, half, late), (keep_early, sectors - early, early)]
-        else:
-            keep_late, lower = refs[:2]
-            even_line, odd_line = [(keep_late, 0, late)], [(keep_late, half, late)]
+            keep_early, returned_early = refs[3:5]
+            even_line += [(keep_early, 0, early), (returned_early, sectors - early, early)]
+            odd_line += [(returned_early, 0, early), (keep_early, sectors - early, early)]
         lower_line = [(whole(lower), sectors, 1)]
         out, buffer, in_semaphores, out_semaphores = refs[-4:]
     site = out.at[0]
@@ -494,7 +510,8 @@
 def place(last, half, target, norms, operands, site):
     anywhere = pl.BlockSpec(memory_space=pl.ANY)
     _, early = chunk_sizes(half)
-    rows = half - early if last else half + early
+    final = (half - early) // 2
+    rows = final if last else 2 * half - final
 
     def kernel(*refs):
         place_kernel(last, half, target, refs[:3], refs[3:])
@@ -506,8 +523,8 @@
         out_specs=anywhere,
         scratch_shapes=[
             pltpu.VMEM((rows, *site.shape[2:]), site.dtype),
-            pltpu.SemaphoreType.DMA((3,)),
-            pltpu.SemaphoreType.DMA((7,)),
+            pltpu.SemaphoreType.DMA((4,)),
+            pltpu.SemaphoreType.DMA((9,)),
         ],
         input_output_aliases={4: 0} if last else {},
         compiler_params=pltpu.CompilerParams(vmem_limit_bytes=16 * 2**20),
@@ -582,9 +599,6 @@
         False, True, site_tensors, got_early, got_late, edge, corner
     )
     norm_even = norm_early + norm_late
-    send_late, halo_late, carried_early = lax.optimization_barrier(
-        (send_late, halo_late, carried_early)
-    )
     carried_late = move(send_late, along)
     near = move(halo_late, across)
 
@@ -599,25 +613,31 @@
         send_early, carried_late = lax.optimization_barrier((send_early, carried_late))
         returned_early = move(send_early, back)
         first_parts = (kept_early, returned_early)
-    send_late, kept_late, norm_late, *lower = update(
+    send_late, send_last, kept_late, norm_late, *lower = update(
         True, True, keep_early, keep_late, carried_early, carried_late, far, near
     )
     if next_early == 0:
         lower_first = lower[0]
     lower_above = move(lower_first, by_parity(lambda c, b: (c - 1, b - 1), nowhere))
     if next_early:
-        send_late, returned_early = lax.optimization_barrier((send_late, returned_early))
+        send_late, returned_early, lower_above = lax.optimization_barrier(
+            (send_late, returned_early, lower_above)
+        )
         first_parts = (kept_early, returned_early)
     returned_late = move(send_late, back)
 
     norms = lax.psum(joined(norm_even, norm_odd + norm_late), "block")
     from_left = move(norms, by_parity(nowhere, lambda c, b: (c + 1, b)))
     from_second = move(norms, by_parity(lambda c, b: (c + 2, b), nowhere))
+    send_last, from_left, from_second = lax.optimization_barrier(
+        (send_last, from_left, from_second)
+    )
+    returned_last = move(send_last, back)
     target = float(sectors * parts * kept * width)
     norms = (norms, from_left, from_second)
-
-    site = place(False, half, target, norms, (kept_late, lower_above, *first_parts), site_tensors)
-    return place(True, half, target, norms, (returned_late, site), site_tensors)
+    ready = (kept_late, returned_late, lower_above, *first_parts)
+    site = place(False, half, target, norms, ready, site_tensors)
+    return place(True, half, target, norms, (returned_last, site), site_tensors)
 
 
 def solution(mesh):

time: 187 us -> 188 us (level)
  the two profiles are of different devices: /device:TPU:0 before, /device:TPU:31 now
where the time goes in v6:
time: 188 us
  Pallas kernels  109 us (58%)
  starting transfers between devices  33.9 us (18%)
  waiting for transfers between devices  32.1 us (17%)
  local copies, waits for them, and re-layouts  4.06 us (2%)
  other arithmetic  3.97 us (2%)
  between operations  2.93 us (2%)
  blocking collectives  2.45 us (1%)
    pallas_call x4, Pallas kernels, pair_update(): pl.pallas_call(kernel, out_shape=[*(jax.ShapeDtypeStruct((size, *block),...  81.5 us
    ppermute x15, starting transfers between devices, move(): return lax.ppermute(value, ('chain', 'block'), pairs)  33.9 us
    ppermute x15, waiting for transfers between devices, move(): return lax.ppermute(value, ('chain', 'block'), pairs)  32.1 us
    pallas_call x2, Pallas kernels, place(): pl.pallas_call(kernel, out_shape=jax.ShapeDtypeStruct(site.shape, site.dt...  27.1 us
    select_n x3, other arithmetic, pick(): return jnp.where(is_even, even_value, odd_value)  3.9 us
  transfers between devices with their start and end apart: 15, of which 3 were waited for; matrix products, arithmetic and copies ran while one was open for 1% of the time, Pallas kernels for 57%

profile of v6, /device:TPU:31, one launch (start us, length us, event | category | flops | bytes accessed | tf_op | source)
XLA Modules:
  0.0 188.0 jit_solution(11632841587820833696)
XLA Ops:
  0.0 3.1 %select_bitcast_fusion = bf16[5,2,256,256]{3,2,1,0:T(8,128)(2,1)} fusion(bf16[1,16,2,256,256]{4,3,2,1,0:T(8,128)(2,1)} %refs_4_.3, pred[]{:T(512)S(6)} %eq.5), kind=kLoop, calls=%fused_computation | loop fusion | flops 655360 | bytes 3932161 | tf_op jit(solution)/shard_map/jit(_where)/select_n | solution.py:572
  3.3 1.2 collective-permute-start
  4.6 0.9 slice_bitcast_fusion
  5.5 0.7 collective-permute-start.3
  6.2 0.7 select_bitcast_fusion.2
  6.9 3.8 %collective-permute-start.2 = (bf16[1,2,256,256]{3,2,1,0:T(8,128)(2,1)}, bf16[1,2,256,256]{3,2,1,0:T(8,128)(2,1)S(1)}, u32[]{:S(2)}, u32[]{:S(2)}) collective-permute-start(bf16[1,2,256,256]{3,2,1,0:T(8,128)(2,1)} %select_bitcast_fusion.2), channel_id=1, source_target_pairs={{0,1},{3,2},{4,5},{7,6},{8,9},{11,10},{12,13},{15,14},{16,17},{19,... | collective-permute-start | bytes 786440 | tf_op jit(solution)/shard_map/ppermute | solution.py:545
  11.0 22.0 %collective-permute-done.1.refs_5_.refs_6_ = bf16[5,2,256,256]{3,2,1,0:T(8,128)(2,1)S(1)} collective-permute-done((bf16[5,2,256,256]{3,2,1,0:T(8,128)(2,1)}, bf16[5,2,256,256]{3,2,1,0:T(8,128)(2,1)S(1)}, u32[]{:S(2)}, u32[]{:S(2)}) %collective-permute-start.1) | collective-permute-done | bytes 1310752 | tf_op jit(solution)/shard_map/ppermute | solution.py:545
  33.3 2.2 %copy-done.1 = bf16[1,16,2,256,256]{4,3,2,1,0:T(8,128)(2,1)S(1)} copy-done((bf16[1,16,2,256,256]{4,3,2,1,0:T(8,128)(2,1)S(1)}, bf16[1,16,2,256,256]{4,3,2,1,0:T(8,128)(2,1)}, u32[]{:S(2)}) %copy-start.1) | copy-done | bytes 4194328
  35.4 20.4 %shard_map.55 = (bf16[4,256,512]{2,1,0:T(8,128)(2,1)S(1)}, bf16[4,256,512]{2,1,0:T(8,128)(2,1)S(1)}, f32[1]{0:T(128)}, bf16[1,256,512]{2,1,0:T(8,128)(2,1)S(1)}) custom-call(s32[1,2,32]{2,1,0:T(2,128)S(1)} %copy-done.3, s32[1,2,32]{2,1,0:T(2,128)S(1)} %collective-permute-done.refs_1_, s32[1,2,32]{2,1,0:T(2,128)S(1)} %copy-done.4, f32[1,2,3]{2,1,0:T(2,128)S(1)} %copy-done.5, ...), custom_call_target="tpu_custom_call" | custom-call | flops 53687091200 | bytes 8388608 | tf_op jit(solution)/shard_map/pallas_call | solution.py:414
  55.9 0.7 collective-permute-start.6
  56.9 20.5 %shard_map.56 = (bf16[4,256,512]{2,1,0:T(8,128)(2,1)S(1)}, bf16[4,256,512]{2,1,0:T(8,128)(2,1)S(1)}, f32[1]{0:T(128)}, bf16[1,256,512]{2,1,0:T(8,128)(2,1)S(1)}) custom-call(s32[1,2,32]{2,1,0:T(2,128)S(1)} %copy-done.3, s32[1,2,32]{2,1,0:T(2,128)S(1)} %collective-permute-done.refs_1_, s32[1,2,32]{2,1,0:T(2,128)S(1)} %copy-done.4, f32[1,2,3]{2,1,0:T(2,128)S(1)} %copy-done.5, ...), custom_call_target="tpu_custom_call" | custom-call | flops 53687091200 | bytes 8388608 | tf_op jit(solution)/shard_map/pallas_call | solution.py:414
  77.3 8.3 %collective-permute-start.8 = (bf16[1,256,512]{2,1,0:T(8,128)(2,1)S(1)}, bf16[1,256,512]{2,1,0:T(8,128)(2,1)S(1)}, u32[]{:S(2)}, u32[]{:S(2)}) collective-permute-start(bf16[1,256,512]{2,1,0:T(8,128)(2,1)S(1)} %get-tuple-element.43), channel_id=1, source_target_pairs={{0,2},{1,3},{2,0},{3,1},{4,6},{5,7},{6,4},{7,5},{8,10},{9,11},{10,... | collective-permute-start | bytes 786440 | tf_op jit(solution)/shard_map/ppermute | solution.py:545
  85.7 18.3 %shard_map.57 = (bf16[3,2,256,256]{3,2,1,0:T(8,128)(2,1)S(1)}, bf16[3,2,256,256]{3,2,1,0:T(8,128)(2,1)S(1)}, f32[1]{0:T(128)}, bf16[1,256,256]{2,1,0:T(8,128)(2,1)S(1)}) custom-call(s32[1,2,32]{2,1,0:T(2,128)S(1)} %copy-done.3, s32[1,2,32]{2,1,0:T(2,128)S(1)} %collective-permute-done.refs_1_, s32[1,2,32]{2,1,0:T(2,128)S(1)} %copy-done.4, ...), custom_call_target="tpu_custom_call" | custom-call | flops 50331648000 | bytes 6291456 | tf_op jit(solution)/shard_map/pallas_call | solution.py:414
  104.7 5.9 %collective-permute-done.7.refs_7_ = bf16[4,256,512]{2,1,0:T(8,128)(2,1)S(1)} collective-permute-done((bf16[4,256,512]{2,1,0:T(8,128)(2,1)S(1)}, bf16[4,256,512]{2,1,0:T(8,128)(2,1)S(1)}, u32[]{:S(2)}, u32[]{:S(2)}) %collective-permute-start.7) | collective-permute-done | bytes 1048608 | tf_op jit(solution)/shard_map/ppermute | solution.py:545
  110.6 2.4 %collective-permute-start.12 = (bf16[3,2,256,256]{3,2,1,0:T(8,128)(2,1)S(1)}, bf16[3,2,256,256]{3,2,1,0:T(8,128)(2,1)S(1)}, u32[]{:S(2)}, u32[]{:S(2)}) collective-permute-start(bf16[3,2,256,256]{3,2,1,0:T(8,128)(2,1)S(1)} %get-tuple-element.51), channel_id=1, source_target_pairs={{0,30},{1,31},{2,4},{3,5},{4,2},{5,3},{6,8},{7,9},{8,6},{9,7},{10,... | collective-permute-start | bytes 2359304 | tf_op jit(solution)/shard_map/ppermute | solution.py:545
  113.0 22.3 %shard_map.58 = (bf16[3,2,256,256]{3,2,1,0:T(8,128)(2,1)}, bf16[2,2,256,256]{3,2,1,0:T(8,128)(2,1)S(1)}, bf16[5,2,256,256]{3,2,1,0:T(8,128)(2,1)S(1)}, f32[1]{0:T(128)}) custom-call(s32[1,2,32]{2,1,0:T(2,128)S(1)} %copy-done.3, s32[1,2,32]{2,1,0:T(2,128)S(1)} %collective-permute-done.refs_1_, s32[1,2,32]{2,1,0:T(2,128)S(1)} %copy-done.4, ...), custom_call_target="tpu_custom_call" | custom-call | flops 57042534400 | bytes 10485760 | tf_op jit(solution)/shard_map/pallas_call | solution.py:414
  135.3 0.8 copy-done.2
  136.1 2.7 %collective-permute-start.14 = (bf16[3,2,256,256]{3,2,1,0:T(8,128)(2,1)}, bf16[3,2,256,256]{3,2,1,0:T(8,128)(2,1)}, u32[]{:S(2)}, u32[]{:S(2)}) collective-permute-start(bf16[3,2,256,256]{3,2,1,0:T(8,128)(2,1)} %get-tuple-element.53), channel_id=1, source_target_pairs={{0,30},{1,31},{2,4},{3,5},{4,2},{5,3},{6,8},{7,9},{8,6},{9,7},{10,... | collective-permute-start | bytes 2359304 | tf_op jit(solution)/shard_map/ppermute | solution.py:545
  141.4 2.5 %psum.7.refs_0_ = f32[2]{0:T(128)S(1)} all-reduce(f32[2]{0:T(128)S(1)} %pad_maximum_fusion), channel_id=1, replica_groups=mesh['chain'=16,'block'=2] {'block'}, use_global_device_ids=true, to_apply=%region_0.1 | all-reduce | flops 2 | bytes 16 | tf_op jit(solution)/shard_map/psum | solution.py:629
  144.5 6.5 %collective-permute-start.9 = (f32[2]{0:T(128)S(1)}, f32[2]{0:T(128)S(1)}, u32[]{:S(2)}, u32[]{:S(2)}) collective-permute-start(f32[2]{0:T(128)S(1)} %psum.7.refs_0_), channel_id=1, source_target_pairs={{2,4},{3,5},{6,8},{7,9},{10,12},{11,13},{14,16},{15,17},{18,20},{1... | collective-permute-start | bytes 32 | tf_op jit(solution)/shard_map/ppermute | solution.py:545
  151.0 4.2 %collective-permute-done.9.refs_1_ = f32[2]{0:T(128)S(1)} collective-permute-done((f32[2]{0:T(128)S(1)}, f32[2]{0:T(128)S(1)}, u32[]{:S(2)}, u32[]{:S(2)}) %collective-permute-start.9) | collective-permute-done | bytes 40 | tf_op jit(solution)/shard_map/ppermute | solution.py:545
  155.2 5.5 %collective-permute-start.11 = (bf16[2,2,256,256]{3,2,1,0:T(8,128)(2,1)}, bf16[2,2,256,256]{3,2,1,0:T(8,128)(2,1)S(1)}, u32[]{:S(2)}, u32[]{:S(2)}) collective-permute-start(bf16[2,2,256,256]{3,2,1,0:T(8,128)(2,1)} %copy-done.2), channel_id=1, source_target_pairs={{0,30},{1,31},{2,4},{3,5},{4,2},{5,3},{6,8},{7,9},{8,6},{9,7},{10,... | collective-permute-start | bytes 1572872 | tf_op jit(solution)/shard_map/ppermute | solution.py:545
  160.7 25.6 %shard_map.59.refs_4_ = bf16[1,16,2,256,256]{4,3,2,1,0:T(8,128)(2,1)} custom-call(f32[2]{0:T(128)S(1)} %psum.7.refs_0_, f32[2]{0:T(128)S(1)} %collective-permute-done.9.refs_1_, f32[2]{0:T(128)S(1)} %collective-permute-done.10.refs_2_, bf16[5,2,256,256]{3,2,1,0:T(8,128)(2,1)S(1)} %get-tuple-element.49.refs_3_, ...), custom_call_target="tpu_custom_call" | custom-call | bytes 7340032 | tf_op jit(solution)/shard_map/pallas_call | solution.py:519
  186.3 1.5 shard_map.60
  (33 shorter events, 2.5 us)
Async XLA Ops:
  0.0 6.1 %copy-start = (bf16[1,16,2,256,256]{4,3,2,1,0:T(8,128)(2,1)S(1)}, bf16[1,16,2,256,256]{4,3,2,1,0:T(8,128)(2,1)}, u32[]{:S(2)}) copy-start(bf16[1,16,2,256,256]{4,3,2,1,0:T(8,128)(2,1)} %refs_4_.3) | copy-start | bytes 12582916
  0.0 10.8 %copy-start.6 = (bf16[512,256]{1,0:T(8,128)(2,1)S(1)}, bf16[512,256]{1,0:T(8,128)(2,1)}, u32[]{:S(2)}) copy-start(bf16[512,256]{1,0:T(8,128)(2,1)} %param.6) | copy-start | bytes 786436
  0.0 33.2 %copy-start.3 = (s32[1,2,32]{2,1,0:T(2,128)S(1)}, s32[1,2,32]{2,1,0:T(2,128)}, u32[]{:S(2)}) copy-start(s32[1,2,32]{2,1,0:T(2,128)} %refs_0_.7) | copy-start | bytes 772
  0.0 33.2 %copy-start.4 = (s32[1,2,32]{2,1,0:T(2,128)S(1)}, s32[1,2,32]{2,1,0:T(2,128)}, u32[]{:S(2)}) copy-start(s32[1,2,32]{2,1,0:T(2,128)} %refs_2_.7) | copy-start | bytes 772
  0.0 33.2 %copy-start.5 = (f32[1,2,3]{2,1,0:T(2,128)S(1)}, f32[1,2,3]{2,1,0:T(2,128)}, u32[]{:S(2)}) copy-start(f32[1,2,3]{2,1,0:T(2,128)} %refs_3_.7) | copy-start | bytes 76
  3.1 29.9 %collective-permute-start.1 = (bf16[5,2,256,256]{3,2,1,0:T(8,128)(2,1)}, bf16[5,2,256,256]{3,2,1,0:T(8,128)(2,1)S(1)}, u32[]{:S(2)}, u32[]{:S(2)}) collective-permute-start(bf16[5,2,256,256]{3,2,1,0:T(8,128)(2,1)} %select_bitcast_fusion), channel_id=1, source_target_pairs={{0,2},{1,3},{2,0},{3,1},{4,6},{5,7},{6,4},{7,5},{8,10},{9,11},{10,... | collective-permute-start | bytes 3932168 | tf_op jit(solution)/shard_map/ppermute | solution.py:545
  3.3 29.9 %collective-permute-start = (s32[1,2,32]{2,1,0:T(2,128)}, s32[1,2,32]{2,1,0:T(2,128)S(1)}, u32[]{:S(2)}, u32[]{:S(2)}) collective-permute-start(s32[1,2,32]{2,1,0:T(2,128)} %refs_0_.7), channel_id=1, source_target_pairs={{0,2},{1,3},{2,0},{3,1},{4,6},{5,7},{6,4},{7,5},{8,10},{9,11},{10,... | collective-permute-start | bytes 776 | tf_op jit(solution)/shard_map/ppermute | solution.py:545
  5.5 27.7 %collective-permute-start.3 = (bf16[1,256,256]{2,1,0:T(8,128)(2,1)S(1)}, bf16[1,256,256]{2,1,0:T(8,128)(2,1)S(1)}, u32[]{:S(2)}, u32[]{:S(2)}) collective-permute-start(bf16[1,256,256]{2,1,0:T(8,128)(2,1)S(1)} %slice_bitcast_fusion), channel_id=1, source_target_pairs={{2,1},{6,5},{10,9},{14,13},{18,17},{22,21},{26,25},{30,29}} | collective-permute-start | bytes 393224 | tf_op jit(solution)/shard_map/ppermute | solution.py:545
  6.9 26.3 %collective-permute-start.2 = (bf16[1,2,256,256]{3,2,1,0:T(8,128)(2,1)}, bf16[1,2,256,256]{3,2,1,0:T(8,128)(2,1)S(1)}, u32[]{:S(2)}, u32[]{:S(2)}) collective-permute-start(bf16[1,2,256,256]{3,2,1,0:T(8,128)(2,1)} %select_bitcast_fusion.2), channel_id=1, source_target_pairs={{0,1},{3,2},{4,5},{7,6},{8,9},{11,10},{12,13},{15,14},{16,17},{19,... | collective-permute-start | bytes 786440 | tf_op jit(solution)/shard_map/ppermute | solution.py:545
  32.9 23.9 %collective-permute-start.4 = (bf16[4,2,256,256]{3,2,1,0:T(8,128)(2,1)S(1)}, bf16[4,2,256,256]{3,2,1,0:T(8,128)(2,1)S(1)}, u32[]{:S(2)}, u32[]{:S(2)}) collective-permute-start(bf16[4,2,256,256]{3,2,1,0:T(8,128)(2,1)S(1)} %select_bitcast_fusion.1), channel_id=1, source_target_pairs={{0,2},{1,3},{2,0},{3,1},{4,6},{5,7},{6,4},{7,5},{8,10},{9,11},{10,... | collective-permute-start | bytes 3145736 | tf_op jit(solution)/shard_map/ppermute | solution.py:545
  33.2 2.2 %copy-start.1 = (bf16[1,16,2,256,256]{4,3,2,1,0:T(8,128)(2,1)S(1)}, bf16[1,16,2,256,256]{4,3,2,1,0:T(8,128)(2,1)}, u32[]{:S(2)}) copy-start(bf16[1,16,2,256,256]{4,3,2,1,0:T(8,128)(2,1)} %refs_4_.3) | copy-start | bytes 12582916
  55.9 29.8 %collective-permute-start.6 = (bf16[1,256,512]{2,1,0:T(8,128)(2,1)S(1)}, bf16[1,256,512]{2,1,0:T(8,128)(2,1)S(1)}, u32[]{:S(2)}, u32[]{:S(2)}) collective-permute-start(bf16[1,256,512]{2,1,0:T(8,128)(2,1)S(1)} %get-tuple-element.37), channel_id=1, source_target_pairs={{1,30},{2,5},{5,2},{6,9},{9,6},{10,13},{13,10},{14,17},{17,14},{18... | collective-permute-start | bytes 786440 | tf_op jit(solution)/shard_map/ppermute | solution.py:545
  56.6 29.1 %collective-permute-start.5 = (bf16[4,256,512]{2,1,0:T(8,128)(2,1)S(1)}, bf16[4,256,512]{2,1,0:T(8,128)(2,1)S(1)}, u32[]{:S(2)}, u32[]{:S(2)}) collective-permute-start(bf16[4,256,512]{2,1,0:T(8,128)(2,1)S(1)} %get-tuple-element.36), channel_id=1, source_target_pairs={{0,4},{1,5},{2,30},{3,31},{4,8},{5,9},{6,2},{7,3},{8,12},{9,13},{1... | collective-permute-start | bytes 3145736 | tf_op jit(solution)/shard_map/ppermute | solution.py:545
  77.3 35.7 %collective-permute-start.8 = (bf16[1,256,512]{2,1,0:T(8,128)(2,1)S(1)}, bf16[1,256,512]{2,1,0:T(8,128)(2,1)S(1)}, u32[]{:S(2)}, u32[]{:S(2)}) collective-permute-start(bf16[1,256,512]{2,1,0:T(8,128)(2,1)S(1)} %get-tuple-element.43), channel_id=1, source_target_pairs={{0,2},{1,3},{2,0},{3,1},{4,6},{5,7},{6,4},{7,5},{8,10},{9,11},{10,... | collective-permute-start | bytes 786440 | tf_op jit(solution)/shard_map/ppermute | solution.py:545
  85.7 25.0 %collective-permute-start.7 = (bf16[4,256,512]{2,1,0:T(8,128)(2,1)S(1)}, bf16[4,256,512]{2,1,0:T(8,128)(2,1)S(1)}, u32[]{:S(2)}, u32[]{:S(2)}) collective-permute-start(bf16[4,256,512]{2,1,0:T(8,128)(2,1)S(1)} %get-tuple-element.41), channel_id=1, source_target_pairs={{0,4},{1,5},{2,30},{3,31},{4,8},{5,9},{6,2},{7,3},{8,12},{9,13},{1... | collective-permute-start | bytes 3145736 | tf_op jit(solution)/shard_map/ppermute | solution.py:545
  104.0 32.1 %collective-permute-start.13 = (bf16[1,256,256]{2,1,0:T(8,128)(2,1)S(1)}, bf16[1,256,256]{2,1,0:T(8,128)(2,1)S(1)}, u32[]{:S(2)}, u32[]{:S(2)}) collective-permute-start(bf16[1,256,256]{2,1,0:T(8,128)(2,1)S(1)} %get-tuple-element.52), channel_id=1, source_target_pairs={{1,30},{5,2},{9,6},{13,10},{17,14},{21,18},{25,22},{29,26}} | collective-permute-start | bytes 393224 | tf_op jit(solution)/shard_map/ppermute | solution.py:545
  110.6 25.5 %collective-permute-start.12 = (bf16[3,2,256,256]{3,2,1,0:T(8,128)(2,1)S(1)}, bf16[3,2,256,256]{3,2,1,0:T(8,128)(2,1)S(1)}, u32[]{:S(2)}, u32[]{:S(2)}) collective-permute-start(bf16[3,2,256,256]{3,2,1,0:T(8,128)(2,1)S(1)} %get-tuple-element.51), channel_id=1, source_target_pairs={{0,30},{1,31},{2,4},{3,5},{4,2},{5,3},{6,8},{7,9},{8,6},{9,7},{10,... | collective-permute-start | bytes 2359304 | tf_op jit(solution)/shard_map/ppermute | solution.py:545
  135.3 0.8 copy-start.2
  136.1 24.6 %collective-permute-start.14 = (bf16[3,2,256,256]{3,2,1,0:T(8,128)(2,1)}, bf16[3,2,256,256]{3,2,1,0:T(8,128)(2,1)}, u32[]{:S(2)}, u32[]{:S(2)}) collective-permute-start(bf16[3,2,256,256]{3,2,1,0:T(8,128)(2,1)} %get-tuple-element.53), channel_id=1, source_target_pairs={{0,30},{1,31},{2,4},{3,5},{4,2},{5,3},{6,8},{7,9},{8,6},{9,7},{10,... | collective-permute-start | bytes 2359304 | tf_op jit(solution)/shard_map/ppermute | solution.py:545
  143.9 7.2 %collective-permute-start.10 = (f32[2]{0:T(128)S(1)}, f32[2]{0:T(128)S(1)}, u32[]{:S(2)}, u32[]{:S(2)}) collective-permute-start(f32[2]{0:T(128)S(1)} %psum.7.refs_0_), channel_id=1, source_target_pairs={{0,4},{1,5},{4,8},{5,9},{8,12},{9,13},{12,16},{13,17},{16,20},{17,... | collective-permute-start | bytes 32 | tf_op jit(solution)/shard_map/ppermute | solution.py:545
  144.5 10.7 %collective-permute-start.9 = (f32[2]{0:T(128)S(1)}, f32[2]{0:T(128)S(1)}, u32[]{:S(2)}, u32[]{:S(2)}) collective-permute-start(f32[2]{0:T(128)S(1)} %psum.7.refs_0_), channel_id=1, source_target_pairs={{2,4},{3,5},{6,8},{7,9},{10,12},{11,13},{14,16},{15,17},{18,20},{1... | collective-permute-start | bytes 32 | tf_op jit(solution)/shard_map/ppermute | solution.py:545
  155.2 31.1 %collective-permute-start.11 = (bf16[2,2,256,256]{3,2,1,0:T(8,128)(2,1)}, bf16[2,2,256,256]{3,2,1,0:T(8,128)(2,1)S(1)}, u32[]{:S(2)}, u32[]{:S(2)}) collective-permute-start(bf16[2,2,256,256]{3,2,1,0:T(8,128)(2,1)} %copy-done.2), channel_id=1, source_target_pairs={{0,30},{1,31},{2,4},{3,5},{4,2},{5,3},{6,8},{7,9},{8,6},{9,7},{10,... | collective-permute-start | bytes 1572872 | tf_op jit(solution)/shard_map/ppermute | solution.py:545

commit v7 on v5

--- a/solution.py
+++ b/solution.py
@@ -199,11 +199,11 @@
     early, next_early = chunk_sizes(half)
     part = next_early if second else early
     first_of = (part, half) if late else (0, sectors - part)
-    sizes, partner_sizes, ranks, couplings = refs[:4]
+    table, partner_sizes = refs[:2]
     operand_count = 6 if second else 5
-    operands = refs[4 : 4 + operand_count]
-    sketch_ref = refs[4 + operand_count]
-    outputs = refs[5 + operand_count : -9]
+    operands = refs[2 : 2 + operand_count]
+    sketch_ref = refs[2 + operand_count]
+    outputs = refs[3 + operand_count : -9]
     (
         left_ref,
         right_ref,
@@ -225,20 +225,24 @@
     is_even = parity == 0
     first = lax.axis_index("block") * sectors + jnp.where(is_even, *first_of)
     bond = parity if second else 1 - parity
-    total = sizes.shape[2]
+    total = table.shape[1]
+
+    def size_of(row, sector):
+        return table[row, sector].astype(jnp.int32)
+
 
     def left_size(sector):
         at = jnp.clip(sector, 0, total - 1)
-        return jnp.where(is_even, sizes[0, 0, at], partner_sizes[0, 0, at])
+        return jnp.where(is_even, size_of(0, at), partner_sizes[0, 0, at])
 
     def middle_size(sector):
         at = jnp.clip(sector, 0, total - 1)
-        size = jnp.where(is_even, sizes[0, 1, at], sizes[0, 0, at])
+        size = size_of(jnp.where(is_even, 1, 0), at)
         return jnp.where(sector < total, size, 0)
 
     def right_size(sector):
         at = jnp.clip(sector, 0, total - 1)
-        size = jnp.where(is_even, partner_sizes[0, 1, at], sizes[0, 1, at])
+        size = jnp.where(is_even, partner_sizes[0, 1, at], size_of(1, at))
         return jnp.where(sector < total, size, 0)
 
     row_index = lax.broadcasted_iota(jnp.int32, (kept, 1), 0)
@@ -273,7 +277,7 @@
         two_ref[m, rows, columns] = value.astype(jnp.bfloat16)
 
     w_empty, w_stay, w_swap, w_full = gate_terms(
-        *(jnp.full((1, width), couplings[0, bond, term], jnp.float32) for term in range(3))
+        *(jnp.full((1, width), table[4 + bond, term], jnp.float32) for term in range(3))
     )
 
     @pl.loop(0, count, unroll=min(UNROLL, count))
@@ -305,7 +309,7 @@
         )
         put(m, high, high, w_full * product(below_one, next_one), rows_high, columns_high)
         sample = dot(sketch_ref[...], two_ref[m], LAST)
-        keep_rows = row_index < ranks[0, bond, sector]
+        keep_rows = row_index < size_of(2 + bond, sector)
         sample = jnp.where(keep_rows, sample, 0.0)
         sample_ref[m] = sample
         high_part, middle_part, low_part = in_parts(sample)
@@ -377,10 +381,10 @@
         extras[0][0] = send[at] if late else keep[at]
 
 
-def pair_update(second, late, sizes, partner_sizes, ranks, couplings, operands, sketch_turned):
+def pair_update(second, late, table, partner_sizes, operands, sketch_turned):
     kept, double = sketch_turned.shape
     width = double // 2
-    sectors = sizes.shape[2] // lax.axis_size("block")
+    sectors = table.shape[1] // lax.axis_size("block")
     half = sectors // 2
     early, next_early = chunk_sizes(half)
     part = next_early if second else early
@@ -405,7 +409,7 @@
             jax.ShapeDtypeStruct((1,), jnp.float32),
             *(jax.ShapeDtypeStruct(shape, jnp.bfloat16) for shape in extra),
         ],
-        in_specs=[smem] * 4 + [anywhere] * len(operands) + [vmem],
+        in_specs=[smem] * 2 + [anywhere] * len(operands) + [vmem],
         out_specs=[vmem, vmem, smem] + [vmem] * len(extra),
         scratch_shapes=[
             pltpu.VMEM(left_shape, jnp.bfloat16),
@@ -424,7 +428,7 @@
             bytes_accessed=8 * count * kept * double * 2,
             transcendentals=0,
         ),
-    )(sizes, partner_sizes, ranks, couplings, *operands, sketch_turned)
+    )(table, partner_sizes, *operands, sketch_turned)
 
 
 def place_kernel(last, half, target, norm_refs, refs):
@@ -459,10 +463,10 @@
 
     @pl.when(is_even)
     def _():
-        norms, from_left, from_second = norm_refs
+        norms, from_second = norm_refs
         rows = (1, buffer.shape[-1])
-        norm_even = jnp.full(rows, from_left[0] + from_second[0], jnp.float32)
-        norm_odd = jnp.full(rows, norms[1] + from_left[1], jnp.float32)
+        norm_even = jnp.full(rows, from_second[0], jnp.float32)
+        norm_odd = jnp.full(rows, norms[1] + from_second[1], jnp.float32)
         scale_even = jnp.sqrt(target / norm_even)
         scale = scale_even * jnp.sqrt(target / (scale_even * scale_even * norm_odd))
         coming, going, filled = [], [], 0
@@ -497,19 +501,19 @@
     rows = half - early if last else half + early
 
     def kernel(*refs):
-        place_kernel(last, half, target, refs[:3], refs[3:])
+        place_kernel(last, half, target, refs[:2], refs[2:])
 
     return pl.pallas_call(
         kernel,
         out_shape=jax.ShapeDtypeStruct(site.shape, site.dtype),
-        in_specs=[pl.BlockSpec(memory_space=pltpu.SMEM)] * 3 + [anywhere] * len(operands),
+        in_specs=[pl.BlockSpec(memory_space=pltpu.SMEM)] * 2 + [anywhere] * len(operands),
         out_specs=anywhere,
         scratch_shapes=[
             pltpu.VMEM((rows, *site.shape[2:]), site.dtype),
             pltpu.SemaphoreType.DMA((3,)),
             pltpu.SemaphoreType.DMA((7,)),
         ],
-        input_output_aliases={4: 0} if last else {},
+        input_output_aliases={3: 0} if last else {},
         compiler_params=pltpu.CompilerParams(vmem_limit_bytes=16 * 2**20),
         cost_estimate=pl.CostEstimate(
             flops=0, bytes_accessed=2 * rows * site.size // site.shape[1] * 2, transcendentals=0
@@ -551,12 +555,17 @@
     own = site_tensors[0]
     sketch_turned = jnp.transpose(sketch)
 
+    terms = jnp.pad(couplings[0], ((0, 0), (0, bond_sizes.shape[2] - couplings.shape[2])))
+    table = joined(
+        bond_sizes[0].astype(jnp.float32), kept_ranks[0].astype(jnp.float32), terms
+    )
+
     def pick(even_value, odd_value):
         return jnp.where(is_even, even_value, odd_value)
 
     def update(second, late, *operands):
         return pair_update(
-            second, late, bond_sizes, partner_sizes, kept_ranks, couplings, operands, sketch_turned
+            second, late, table, partner_sizes, operands, sketch_turned
         )
 
     across = by_parity(lambda c, b: (c + 1, b), lambda c, b: (c - 1, b))
@@ -582,9 +591,6 @@
         False, True, site_tensors, got_early, got_late, edge, corner
     )
     norm_even = norm_early + norm_late
-    send_late, halo_late, carried_early = lax.optimization_barrier(
-        (send_late, halo_late, carried_early)
-    )
     carried_late = move(send_late, along)
     near = move(halo_late, across)
 
@@ -606,15 +612,20 @@
         lower_first = lower[0]
     lower_above = move(lower_first, by_parity(lambda c, b: (c - 1, b - 1), nowhere))
     if next_early:
-        send_late, returned_early = lax.optimization_barrier((send_late, returned_early))
+        send_late, returned_early, lower_above = lax.optimization_barrier(
+            (send_late, returned_early, lower_above)
+        )
         first_parts = (kept_early, returned_early)
     returned_late = move(send_late, back)
 
     norms = lax.psum(joined(norm_even, norm_odd + norm_late), "block")
-    from_left = move(norms, by_parity(nowhere, lambda c, b: (c + 1, b)))
-    from_second = move(norms, by_parity(lambda c, b: (c + 2, b), nowhere))
+    from_right = move(norms, by_parity(nowhere, lambda c, b: (c - 1, b)))
+    from_second = move(
+        from_right + jnp.where(jnp.arange(2) == 0, norms, 0.0),
+        by_parity(lambda c, b: (c + 2, b), nowhere),
+    )
     target = float(sectors * parts * kept * width)
-    norms = (norms, from_left, from_second)
+    norms = (norms, from_second)
 
     site = place(False, half, target, norms, (kept_late, lower_above, *first_parts), site_tensors)
     return place(True, half, target, norms, (returned_late, site), site_tensors)

time: 187 us -> 183 us (0.979)
  blocking collectives: 8.03 us -> 2.44 us
  starting transfers between devices: 21.9 us -> 24.2 us
    psum x1, blocking collectives: 8.03 us -> 2.44 us  [body(): norms = lax.psum(joined(norm_even, norm_odd + norm_late), 'block')]
    ppermute x14, starting transfers between devices: 21.9 us -> 24.2 us  [move(): return lax.ppermute(value, ('chain', 'block'), pairs)]
  transfers between devices with their start and end apart: 14 -> 14, of which waited for: 5 -> 4; matrix products, arithmetic and copies ran while one was open for 1% -> 1% of each run, Pallas kernels for 46% -> 47%
where the time goes in v7:
time: 183 us
  Pallas kernels  87.3 us (48%)
  waiting for transfers between devices  56.7 us (31%)
  starting transfers between devices  24.2 us (13%)
  local copies, waits for them, and re-layouts  5.91 us (3%)
  other arithmetic  3.29 us (2%)
  between operations  2.97 us (2%)
  blocking collectives  2.44 us (1%)
    pallas_call x4, Pallas kernels, pair_update(): pl.pallas_call(kernel, out_shape=[jax.ShapeDtypeStruct((count, *block), j...  82.7 us
    ppermute x14, waiting for transfers between devices, move(): return lax.ppermute(value, ('chain', 'block'), pairs)  56.7 us
    ppermute x14, starting transfers between devices, move(): return lax.ppermute(value, ('chain', 'block'), pairs)  24.2 us
    pallas_call x2, Pallas kernels, place(): pl.pallas_call(kernel, out_shape=jax.ShapeDtypeStruct(site.shape, site.dt...  4.64 us
    unnamed x17, local copies, waits for them, and re-layouts  4.36 us
  transfers between devices with their start and end apart: 14, of which 4 were waited for; matrix products, arithmetic and copies ran while one was open for 1% of the time, Pallas kernels for 47%

profile of v7, /device:TPU:0, one launch (start us, length us, event | category | flops | bytes accessed | tf_op | source)
XLA Modules:
  0.0 182.8 jit_solution(4947548725679420652)
XLA Ops:
  0.0 3.1 %select_bitcast_fusion = bf16[5,2,256,256]{3,2,1,0:T(8,128)(2,1)} fusion(bf16[1,16,2,256,256]{4,3,2,1,0:T(8,128)(2,1)} %refs_2_.3, pred[]{:T(512)S(6)} %eq.8), kind=kLoop, calls=%fused_computation | loop fusion | flops 655360 | bytes 3932161 | tf_op jit(solution)/shard_map/jit(_where)/select_n | solution.py:564
  3.1 2.9 %collective-permute-start.1 = (bf16[5,2,256,256]{3,2,1,0:T(8,128)(2,1)}, bf16[5,2,256,256]{3,2,1,0:T(8,128)(2,1)S(1)}, u32[]{:S(2)}, u32[]{:S(2)}) collective-permute-start(bf16[5,2,256,256]{3,2,1,0:T(8,128)(2,1)} %select_bitcast_fusion), channel_id=1, source_target_pairs={{0,2},{1,3},{2,0},{3,1},{4,6},{5,7},{6,4},{7,5},{8,10},{9,11},{10,... | collective-permute-start | bytes 3932168 | tf_op jit(solution)/shard_map/ppermute | solution.py:532
  6.0 1.6 slice_bitcast_fusion
  8.3 2.2 %collective-permute-start.2 = (bf16[1,2,256,256]{3,2,1,0:T(8,128)(2,1)S(1)}, bf16[1,2,256,256]{3,2,1,0:T(8,128)(2,1)S(1)}, u32[]{:S(2)}, u32[]{:S(2)}) collective-permute-start(bf16[1,2,256,256]{3,2,1,0:T(8,128)(2,1)S(1)} %select_bitcast_fusion.2), channel_id=1, source_target_pairs={{0,1},{3,2},{4,5},{7,6},{8,9},{11,10},{12,13},{15,14},{16,17},{19,... | collective-permute-start | bytes 786440 | tf_op jit(solution)/shard_map/ppermute | solution.py:532
  10.9 24.1 %collective-permute-done.1.refs_3_.refs_4_ = bf16[5,2,256,256]{3,2,1,0:T(8,128)(2,1)S(1)} collective-permute-done((bf16[5,2,256,256]{3,2,1,0:T(8,128)(2,1)}, bf16[5,2,256,256]{3,2,1,0:T(8,128)(2,1)S(1)}, u32[]{:S(2)}, u32[]{:S(2)}) %collective-permute-start.1) | collective-permute-done | bytes 1310752 | tf_op jit(solution)/shard_map/ppermute | solution.py:532
  35.0 1.7 collective-permute-start.4
  36.8 2.2 %copy-done.1 = bf16[1,16,2,256,256]{4,3,2,1,0:T(8,128)(2,1)S(1)} copy-done((bf16[1,16,2,256,256]{4,3,2,1,0:T(8,128)(2,1)S(1)}, bf16[1,16,2,256,256]{4,3,2,1,0:T(8,128)(2,1)}, u32[]{:S(2)}) %copy-start.1) | copy-done | bytes 4194328
  38.9 20.4 %shard_map.55 = (bf16[4,256,512]{2,1,0:T(8,128)(2,1)S(1)}, bf16[4,256,512]{2,1,0:T(8,128)(2,1)S(1)}, f32[1]{0:T(128)}, bf16[1,256,512]{2,1,0:T(8,128)(2,1)S(1)}) custom-call(f32[6,32]{1,0:T(8,128)S(1)} %select_maximum_fusion.refs_0_, s32[1,2,32]{2,1,0:T(2,128)S(1)} %collective-permute-done.refs_1_, bf16[1,16,2,256,256]{4,3,2,1,0:T(8,128)(2,1)S(1)} %copy-done.1, ...), custom_call_target="tpu_custom_call" | custom-call | flops 53687091200 | bytes 8388608 | tf_op jit(solution)/shard_map/pallas_call | solution.py:404
  60.1 1.6 collective-permute-start.5
  61.7 20.7 %shard_map.56 = (bf16[4,256,512]{2,1,0:T(8,128)(2,1)S(1)}, bf16[4,256,512]{2,1,0:T(8,128)(2,1)S(1)}, f32[1]{0:T(128)}, bf16[1,256,512]{2,1,0:T(8,128)(2,1)S(1)}) custom-call(f32[6,32]{1,0:T(8,128)S(1)} %select_maximum_fusion.refs_0_, s32[1,2,32]{2,1,0:T(2,128)S(1)} %collective-permute-done.refs_1_, bf16[1,16,2,256,256]{4,3,2,1,0:T(8,128)(2,1)S(1)} %copy-done.1, ...), custom_call_target="tpu_custom_call" | custom-call | flops 53687091200 | bytes 8388608 | tf_op jit(solution)/shard_map/pallas_call | solution.py:404
  82.3 4.8 %collective-permute-start.8 = (bf16[1,256,512]{2,1,0:T(8,128)(2,1)S(1)}, bf16[1,256,512]{2,1,0:T(8,128)(2,1)S(1)}, u32[]{:S(2)}, u32[]{:S(2)}) collective-permute-start(bf16[1,256,512]{2,1,0:T(8,128)(2,1)S(1)} %get-tuple-element.39), channel_id=1, source_target_pairs={{0,2},{1,3},{2,0},{3,1},{4,6},{5,7},{6,4},{7,5},{8,10},{9,11},{10,... | collective-permute-start | bytes 786440 | tf_op jit(solution)/shard_map/ppermute | solution.py:532
  87.2 18.3 %shard_map.57 = (bf16[3,2,256,256]{3,2,1,0:T(8,128)(2,1)S(1)}, bf16[3,2,256,256]{3,2,1,0:T(8,128)(2,1)S(1)}, f32[1]{0:T(128)}, bf16[1,256,256]{2,1,0:T(8,128)(2,1)S(1)}) custom-call(f32[6,32]{1,0:T(8,128)S(1)} %select_maximum_fusion.refs_0_, s32[1,2,32]{2,1,0:T(2,128)S(1)} %collective-permute-done.refs_1_, ...), custom_call_target="tpu_custom_call" | custom-call | flops 50331648000 | bytes 6291456 | tf_op jit(solution)/shard_map/pallas_call | solution.py:404
  106.2 8.4 %collective-permute-done.7.refs_5_ = bf16[4,256,512]{2,1,0:T(8,128)(2,1)S(1)} collective-permute-done((bf16[4,256,512]{2,1,0:T(8,128)(2,1)S(1)}, bf16[4,256,512]{2,1,0:T(8,128)(2,1)S(1)}, u32[]{:S(2)}, u32[]{:S(2)}) %collective-permute-start.7) | collective-permute-done | bytes 1048608 | tf_op jit(solution)/shard_map/ppermute | solution.py:532
  114.8 23.2 %shard_map.58 = (bf16[5,2,256,256]{3,2,1,0:T(8,128)(2,1)}, bf16[5,2,256,256]{3,2,1,0:T(8,128)(2,1)S(1)}, f32[1]{0:T(128)}) custom-call(f32[6,32]{1,0:T(8,128)S(1)} %select_maximum_fusion.refs_0_, s32[1,2,32]{2,1,0:T(2,128)S(1)} %collective-permute-done.refs_1_, bf16[4,256,512]{2,1,0:T(8,128)(2,1)S(1)} %get-tuple-element.31.refs_2_.refs_3_, ...), custom_call_target="tpu_custom_call" | custom-call | flops 57042534400 | bytes 10485760 | tf_op jit(solution)/shard_map/pallas_call | solution.py:404
  138.1 0.9 copy-done.2
  139.0 5.4 %collective-permute-start.13 = (bf16[5,2,256,256]{3,2,1,0:T(8,128)(2,1)}, bf16[5,2,256,256]{3,2,1,0:T(8,128)(2,1)S(1)}, u32[]{:S(2)}, u32[]{:S(2)}) collective-permute-start(bf16[5,2,256,256]{3,2,1,0:T(8,128)(2,1)} %get-tuple-element.44), channel_id=1, source_target_pairs={{0,30},{1,31},{2,4},{3,5},{4,2},{5,3},{6,8},{7,9},{8,6},{9,7},{10,... | collective-permute-start | bytes 3932168 | tf_op jit(solution)/shard_map/ppermute | solution.py:532
  147.0 2.4 %psum.7.refs_0_ = f32[2]{0:T(128)S(1)} all-reduce(f32[2]{0:T(128)S(1)} %pad_maximum_fusion), channel_id=1, replica_groups=mesh['chain'=16,'block'=2] {'block'}, use_global_device_ids=true, to_apply=%region_0.1 | all-reduce | flops 2 | bytes 16 | tf_op jit(solution)/shard_map/psum | solution.py:621
  149.4 1.3 collective-permute-start.9
  150.7 18.0 %collective-permute-done.9 = f32[2]{0:T(128)S(1)} collective-permute-done((f32[2]{0:T(128)S(1)}, f32[2]{0:T(128)S(1)}, u32[]{:S(2)}, u32[]{:S(2)}) %collective-permute-start.9) | collective-permute-done | bytes 40 | tf_op jit(solution)/shard_map/ppermute | solution.py:532
  168.7 1.9 %collective-permute-start.10 = (f32[2]{0:T(128)S(1)}, f32[2]{0:T(128)S(1)}, u32[]{:S(2)}, u32[]{:S(2)}) collective-permute-start(f32[2]{0:T(128)S(1)} %fusion), channel_id=1, source_target_pairs={{0,4},{1,5},{4,8},{5,9},{8,12},{9,13},{12,16},{13,17},{16,20},{17,... | collective-permute-start | bytes 32 | tf_op jit(solution)/shard_map/ppermute | solution.py:532
  170.7 6.2 %collective-permute-done.10.refs_1_ = f32[2]{0:T(128)S(1)} collective-permute-done((f32[2]{0:T(128)S(1)}, f32[2]{0:T(128)S(1)}, u32[]{:S(2)}, u32[]{:S(2)}) %collective-permute-start.10) | collective-permute-done | bytes 40 | tf_op jit(solution)/shard_map/ppermute | solution.py:532
  176.9 1.1 copy-done.3
  178.0 2.6 %shard_map.59.refs_3_ = bf16[1,16,2,256,256]{4,3,2,1,0:T(8,128)(2,1)} custom-call(f32[2]{0:T(128)S(1)} %psum.7.refs_0_, f32[2]{0:T(128)S(1)} %collective-permute-done.10.refs_1_, bf16[5,2,256,256]{3,2,1,0:T(8,128)(2,1)S(1)} %get-tuple-element.45.refs_2_, bf16[1,256,256]{2,1,0:T(8,128)(2,1)S(1)} %collective-permute-done.12.refs_3_, ...), custom_call_target="tpu_custom_call" | custom-call | bytes 5767168 | tf_op jit(solution)/shard_map/pallas_call | solution.py:506
  180.6 2.1 %shard_map.60 = bf16[1,16,2,256,256]{4,3,2,1,0:T(8,128)(2,1)} custom-call(f32[2]{0:T(128)S(1)} %psum.7.refs_0_, f32[2]{0:T(128)S(1)} %collective-permute-done.10.refs_1_, bf16[5,2,256,256]{3,2,1,0:T(8,128)(2,1)S(1)} %collective-permute-done.13.refs_2_, bf16[1,16,2,256,256]{4,3,2,1,0:T(8,128)(2,1)} %shard_map.59.refs_3_), custom_call_target="tpu_custom_call", output_to_operand_aliasing={{}: (3, {})} | custom-call | bytes 2621440 | tf_op jit(solution)/shard_map/pallas_call | solution.py:506
  (36 shorter events, 2.7 us)
Async XLA Ops:
  0.0 8.2 %copy-start = (bf16[1,16,2,256,256]{4,3,2,1,0:T(8,128)(2,1)S(1)}, bf16[1,16,2,256,256]{4,3,2,1,0:T(8,128)(2,1)}, u32[]{:S(2)}) copy-start(bf16[1,16,2,256,256]{4,3,2,1,0:T(8,128)(2,1)} %refs_2_.3) | copy-start | bytes 12582916
  3.1 31.9 %collective-permute-start.1 = (bf16[5,2,256,256]{3,2,1,0:T(8,128)(2,1)}, bf16[5,2,256,256]{3,2,1,0:T(8,128)(2,1)S(1)}, u32[]{:S(2)}, u32[]{:S(2)}) collective-permute-start(bf16[5,2,256,256]{3,2,1,0:T(8,128)(2,1)} %select_bitcast_fusion), channel_id=1, source_target_pairs={{0,2},{1,3},{2,0},{3,1},{4,6},{5,7},{6,4},{7,5},{8,10},{9,11},{10,... | collective-permute-start | bytes 3932168 | tf_op jit(solution)/shard_map/ppermute | solution.py:532
  6.0 30.7 %collective-permute-start = (s32[1,2,32]{2,1,0:T(2,128)}, s32[1,2,32]{2,1,0:T(2,128)S(1)}, u32[]{:S(2)}, u32[]{:S(2)}) collective-permute-start(s32[1,2,32]{2,1,0:T(2,128)} %param.7), channel_id=1, source_target_pairs={{0,2},{1,3},{2,0},{3,1},{4,6},{5,7},{6,4},{7,5},{8,10},{9,11},{10,... | collective-permute-start | bytes 776 | tf_op jit(solution)/shard_map/ppermute | solution.py:532
  7.6 29.2 %collective-permute-start.3 = (bf16[1,256,256]{2,1,0:T(8,128)(2,1)}, bf16[1,256,256]{2,1,0:T(8,128)(2,1)S(1)}, u32[]{:S(2)}, u32[]{:S(2)}) collective-permute-start(bf16[1,256,256]{2,1,0:T(8,128)(2,1)} %slice_bitcast_fusion), channel_id=1, source_target_pairs={{2,1},{6,5},{10,9},{14,13},{18,17},{22,21},{26,25},{30,29}} | collective-permute-start | bytes 393224 | tf_op jit(solution)/shard_map/ppermute | solution.py:532
  8.3 2.4 %copy-start.6 = (s32[1,2,32]{2,1,0:T(2,128)S(1)}, s32[1,2,32]{2,1,0:T(2,128)}, u32[]{:S(2)}) copy-start(s32[1,2,32]{2,1,0:T(2,128)} %param.8) | copy-start | bytes 772
  8.3 2.4 %copy-start.7 = (s32[1,2,32]{2,1,0:T(2,128)S(1)}, s32[1,2,32]{2,1,0:T(2,128)}, u32[]{:S(2)}) copy-start(s32[1,2,32]{2,1,0:T(2,128)} %param.7) | copy-start | bytes 772
  8.3 2.4 %copy-start.4 = (bf16[512,256]{1,0:T(8,128)(2,1)S(1)}, bf16[512,256]{1,0:T(8,128)(2,1)}, u32[]{:S(2)}) copy-start(bf16[512,256]{1,0:T(8,128)(2,1)} %param.6) | copy-start | bytes 786436
  8.3 2.6 %copy-start.5 = (f32[1,2,3]{2,1,0:T(2,128)S(1)}, f32[1,2,3]{2,1,0:T(2,128)}, u32[]{:S(2)}) copy-start(f32[1,2,3]{2,1,0:T(2,128)} %param.9) | copy-start | bytes 76
  8.3 28.4 %collective-permute-start.2 = (bf16[1,2,256,256]{3,2,1,0:T(8,128)(2,1)S(1)}, bf16[1,2,256,256]{3,2,1,0:T(8,128)(2,1)S(1)}, u32[]{:S(2)}, u32[]{:S(2)}) collective-permute-start(bf16[1,2,256,256]{3,2,1,0:T(8,128)(2,1)S(1)} %select_bitcast_fusion.2), channel_id=1, source_target_pairs={{0,1},{3,2},{4,5},{7,6},{8,9},{11,10},{12,13},{15,14},{16,17},{19,... | collective-permute-start | bytes 786440 | tf_op jit(solution)/shard_map/ppermute | solution.py:532
  35.0 26.7 %collective-permute-start.4 = (bf16[4,2,256,256]{3,2,1,0:T(8,128)(2,1)S(1)}, bf16[4,2,256,256]{3,2,1,0:T(8,128)(2,1)S(1)}, u32[]{:S(2)}, u32[]{:S(2)}) collective-permute-start(bf16[4,2,256,256]{3,2,1,0:T(8,128)(2,1)S(1)} %select_bitcast_fusion.1), channel_id=1, source_target_pairs={{0,2},{1,3},{2,0},{3,1},{4,6},{5,7},{6,4},{7,5},{8,10},{9,11},{10,... | collective-permute-start | bytes 3145736 | tf_op jit(solution)/shard_map/ppermute | solution.py:532
  36.7 2.2 %copy-start.1 = (bf16[1,16,2,256,256]{4,3,2,1,0:T(8,128)(2,1)S(1)}, bf16[1,16,2,256,256]{4,3,2,1,0:T(8,128)(2,1)}, u32[]{:S(2)}) copy-start(bf16[1,16,2,256,256]{4,3,2,1,0:T(8,128)(2,1)} %refs_2_.3) | copy-start | bytes 12582916
  59.4 27.8 %collective-permute-start.6 = (bf16[1,256,512]{2,1,0:T(8,128)(2,1)S(1)}, bf16[1,256,512]{2,1,0:T(8,128)(2,1)S(1)}, u32[]{:S(2)}, u32[]{:S(2)}) collective-permute-start(bf16[1,256,512]{2,1,0:T(8,128)(2,1)S(1)} %get-tuple-element.33), channel_id=1, source_target_pairs={{1,30},{2,5},{5,2},{6,9},{9,6},{10,13},{13,10},{14,17},{17,14},{18... | collective-permute-start | bytes 786440 | tf_op jit(solution)/shard_map/ppermute | solution.py:532
  60.1 27.1 %collective-permute-start.5 = (bf16[4,256,512]{2,1,0:T(8,128)(2,1)S(1)}, bf16[4,256,512]{2,1,0:T(8,128)(2,1)S(1)}, u32[]{:S(2)}, u32[]{:S(2)}) collective-permute-start(bf16[4,256,512]{2,1,0:T(8,128)(2,1)S(1)} %get-tuple-element.32), channel_id=1, source_target_pairs={{0,4},{1,5},{2,30},{3,31},{4,8},{5,9},{6,2},{7,3},{8,12},{9,13},{1... | collective-permute-start | bytes 3145736 | tf_op jit(solution)/shard_map/ppermute | solution.py:532
  82.3 32.5 %collective-permute-start.8 = (bf16[1,256,512]{2,1,0:T(8,128)(2,1)S(1)}, bf16[1,256,512]{2,1,0:T(8,128)(2,1)S(1)}, u32[]{:S(2)}, u32[]{:S(2)}) collective-permute-start(bf16[1,256,512]{2,1,0:T(8,128)(2,1)S(1)} %get-tuple-element.39), channel_id=1, source_target_pairs={{0,2},{1,3},{2,0},{3,1},{4,6},{5,7},{6,4},{7,5},{8,10},{9,11},{10,... | collective-permute-start | bytes 786440 | tf_op jit(solution)/shard_map/ppermute | solution.py:532
  87.2 27.4 %collective-permute-start.7 = (bf16[4,256,512]{2,1,0:T(8,128)(2,1)S(1)}, bf16[4,256,512]{2,1,0:T(8,128)(2,1)S(1)}, u32[]{:S(2)}, u32[]{:S(2)}) collective-permute-start(bf16[4,256,512]{2,1,0:T(8,128)(2,1)S(1)} %get-tuple-element.37), channel_id=1, source_target_pairs={{0,4},{1,5},{2,30},{3,31},{4,8},{5,9},{6,2},{7,3},{8,12},{9,13},{1... | collective-permute-start | bytes 3145736 | tf_op jit(solution)/shard_map/ppermute | solution.py:532
  105.6 32.5 %collective-permute-start.12 = (bf16[1,256,256]{2,1,0:T(8,128)(2,1)S(1)}, bf16[1,256,256]{2,1,0:T(8,128)(2,1)S(1)}, u32[]{:S(2)}, u32[]{:S(2)}) collective-permute-start(bf16[1,256,256]{2,1,0:T(8,128)(2,1)S(1)} %get-tuple-element.43), channel_id=1, source_target_pairs={{1,30},{5,2},{9,6},{13,10},{17,14},{21,18},{25,22},{29,26}} | collective-permute-start | bytes 393224 | tf_op jit(solution)/shard_map/ppermute | solution.py:532
  114.6 23.5 %collective-permute-start.11 = (bf16[3,2,256,256]{3,2,1,0:T(8,128)(2,1)S(1)}, bf16[3,2,256,256]{3,2,1,0:T(8,128)(2,1)S(1)}, u32[]{:S(2)}, u32[]{:S(2)}) collective-permute-start(bf16[3,2,256,256]{3,2,1,0:T(8,128)(2,1)S(1)} %get-tuple-element.42), channel_id=1, source_target_pairs={{0,30},{1,31},{2,4},{3,5},{4,2},{5,3},{6,8},{7,9},{8,6},{9,7},{10,... | collective-permute-start | bytes 2359304 | tf_op jit(solution)/shard_map/ppermute | solution.py:532
  138.1 0.9 copy-start.2
  139.0 41.6 %collective-permute-start.13 = (bf16[5,2,256,256]{3,2,1,0:T(8,128)(2,1)}, bf16[5,2,256,256]{3,2,1,0:T(8,128)(2,1)S(1)}, u32[]{:S(2)}, u32[]{:S(2)}) collective-permute-start(bf16[5,2,256,256]{3,2,1,0:T(8,128)(2,1)} %get-tuple-element.44), channel_id=1, source_target_pairs={{0,30},{1,31},{2,4},{3,5},{4,2},{5,3},{6,8},{7,9},{8,6},{9,7},{10,... | collective-permute-start | bytes 3932168 | tf_op jit(solution)/shard_map/ppermute | solution.py:532
  149.4 19.3 %collective-permute-start.9 = (f32[2]{0:T(128)S(1)}, f32[2]{0:T(128)S(1)}, u32[]{:S(2)}, u32[]{:S(2)}) collective-permute-start(f32[2]{0:T(128)S(1)} %psum.7.refs_0_), channel_id=1, source_target_pairs={{2,0},{3,1},{6,4},{7,5},{10,8},{11,9},{14,12},{15,13},{18,16},{19,... | collective-permute-start | bytes 32 | tf_op jit(solution)/shard_map/ppermute | solution.py:532
  168.7 8.1 %collective-permute-start.10 = (f32[2]{0:T(128)S(1)}, f32[2]{0:T(128)S(1)}, u32[]{:S(2)}, u32[]{:S(2)}) collective-permute-start(f32[2]{0:T(128)S(1)} %fusion), channel_id=1, source_target_pairs={{0,4},{1,5},{4,8},{5,9},{8,12},{9,13},{12,16},{13,17},{16,20},{17,... | collective-permute-start | bytes 32 | tf_op jit(solution)/shard_map/ppermute | solution.py:532
  176.9 1.1 copy-start.3

commit v8 on v7

--- a/solution.py
+++ b/solution.py
@@ -397,6 +397,9 @@
     vmem = pl.BlockSpec(memory_space=pltpu.VMEM)
     smem = pl.BlockSpec(memory_space=pltpu.SMEM)
     anywhere = pl.BlockSpec(memory_space=pl.ANY)
+    places = [anywhere] * len(operands)
+    if not second:
+        places[0] = pl.BlockSpec(memory_space=pltpu.HBM)
 
     def kernel(*refs):
         pair_kernel(second, late, sectors, refs)
@@ -409,7 +412,7 @@
             jax.ShapeDtypeStruct((1,), jnp.float32),
             *(jax.ShapeDtypeStruct(shape, jnp.bfloat16) for shape in extra),
         ],
-        in_specs=[smem] * 2 + [anywhere] * len(operands) + [vmem],
+        in_specs=[smem] * 2 + places + [vmem],
         out_specs=[vmem, vmem, smem] + [vmem] * len(extra),
         scratch_shapes=[
             pltpu.VMEM(left_shape, jnp.bfloat16),
@@ -498,6 +501,9 @@
 def place(last, half, target, norms, operands, site):
     anywhere = pl.BlockSpec(memory_space=pl.ANY)
     _, early = chunk_sizes(half)
+    places = [anywhere] * len(operands)
+    if not last and early:
+        places[-1] = pl.BlockSpec(memory_space=pltpu.HBM)
     rows = half - early if last else half + early
 
     def kernel(*refs):
@@ -506,7 +512,7 @@
     return pl.pallas_call(
         kernel,
         out_shape=jax.ShapeDtypeStruct(site.shape, site.dtype),
-        in_specs=[pl.BlockSpec(memory_space=pltpu.SMEM)] * 2 + [anywhere] * len(operands),
+        in_specs=[pl.BlockSpec(memory_space=pltpu.SMEM)] * 2 + places,
         out_specs=anywhere,
         scratch_shapes=[
             pltpu.VMEM((rows, *site.shape[2:]), site.dtype),
@@ -616,10 +622,10 @@
             (send_late, returned_early, lower_above)
         )
         first_parts = (kept_early, returned_early)
-    returned_late = move(send_late, back)
-
     norms = lax.psum(joined(norm_even, norm_odd + norm_late), "block")
     from_right = move(norms, by_parity(nowhere, lambda c, b: (c - 1, b)))
+    send_late, from_right = lax.optimization_barrier((send_late, from_right))
+    returned_late = move(send_late, back)
     from_second = move(
         from_right + jnp.where(jnp.arange(2) == 0, norms, 0.0),
         by_parity(lambda c, b: (c + 2, b), nowhere),

time: 183 us -> 185 us (1.011)
  waiting for transfers between devices: 56.7 us -> 60.9 us
  starting transfers between devices: 24.2 us -> 20.6 us
    ppermute x14, waiting for transfers between devices: 56.7 us -> 60.9 us  [move(): return lax.ppermute(value, ('chain', 'block'), pairs)]
    ppermute x14, starting transfers between devices: 24.2 us -> 20.6 us  [move(): return lax.ppermute(value, ('chain', 'block'), pairs)]
    unnamed x17 -> x15, local copies, waits for them, and re-layouts: 4.36 us -> 3.4 us
  transfers between devices with their start and end apart: 14 -> 14, of which waited for: 4 -> 5; matrix products, arithmetic and copies ran while one was open for 1% -> 2% of each run, Pallas kernels for 47% -> 46%
where the time goes in v8:
time: 185 us
  Pallas kernels  87.2 us (47%)
  waiting for transfers between devices  60.9 us (33%)
  starting transfers between devices  20.6 us (11%)
  local copies, waits for them, and re-layouts  4.95 us (3%)
  blocking collectives  3.96 us (2%)
  other arithmetic  3.9 us (2%)
  between operations  2.93 us (2%)
    pallas_call x4, Pallas kernels, pair_update(): pl.pallas_call(kernel, out_shape=[jax.ShapeDtypeStruct((count, *block), j...  82.6 us
    ppermute x14, waiting for transfers between devices, move(): return lax.ppermute(value, ('chain', 'block'), pairs)  60.9 us
    ppermute x14, starting transfers between devices, move(): return lax.ppermute(value, ('chain', 'block'), pairs)  20.6 us
    pallas_call x2, Pallas kernels, place(): pl.pallas_call(kernel, out_shape=jax.ShapeDtypeStruct(site.shape, site.dt...  4.63 us
    psum x1, blocking collectives, body(): norms = lax.psum(joined(norm_even, norm_odd + norm_late), 'block')  3.96 us
    select_n x3, other arithmetic, pick(): return jnp.where(is_even, even_value, odd_value)  3.81 us
  transfers between devices with their start and end apart: 14, of which 5 were waited for; matrix products, arithmetic and copies ran while one was open for 2% of the time, Pallas kernels for 46%

profile of v8, /device:TPU:0, one launch (start us, length us, event | category | flops | bytes accessed | tf_op | source)
XLA Modules:
  0.0 184.5 jit_solution(17033493735800983188)
XLA Ops:
  0.0 2.0 %select_bitcast_fusion = bf16[5,2,256,256]{3,2,1,0:T(8,128)(2,1)S(1)} fusion(bf16[1,16,2,256,256]{4,3,2,1,0:T(8,128)(2,1)} %refs_2_.3, pred[]{:T(512)S(6)} %eq.8), kind=kLoop, calls=%fused_computation | loop fusion | flops 655360 | bytes 3932161 | tf_op jit(solution)/shard_map/jit(_where)/select_n | solution.py:570
  2.0 3.0 %collective-permute-start.1 = (bf16[5,2,256,256]{3,2,1,0:T(8,128)(2,1)S(1)}, bf16[5,2,256,256]{3,2,1,0:T(8,128)(2,1)S(1)}, u32[]{:S(2)}, u32[]{:S(2)}) collective-permute-start(bf16[5,2,256,256]{3,2,1,0:T(8,128)(2,1)S(1)} %select_bitcast_fusion), channel_id=1, source_target_pairs={{0,2},{1,3},{2,0},{3,1},{4,6},{5,7},{6,4},{7,5},{8,10},{9,11},{10,... | collective-permute-start | bytes 3932168 | tf_op jit(solution)/shard_map/ppermute | solution.py:538
  5.1 1.5 slice_bitcast_fusion
  8.1 2.2 %collective-permute-start.2 = (bf16[1,2,256,256]{3,2,1,0:T(8,128)(2,1)}, bf16[1,2,256,256]{3,2,1,0:T(8,128)(2,1)S(1)}, u32[]{:S(2)}, u32[]{:S(2)}) collective-permute-start(bf16[1,2,256,256]{3,2,1,0:T(8,128)(2,1)} %select_bitcast_fusion.2), channel_id=1, source_target_pairs={{0,1},{3,2},{4,5},{7,6},{8,9},{11,10},{12,13},{15,14},{16,17},{19,... | collective-permute-start | bytes 786440 | tf_op jit(solution)/shard_map/ppermute | solution.py:538
  10.3 1.1 select_bitcast_fusion.1
  11.6 22.2 %collective-permute-done.1.refs_3_.refs_4_ = bf16[5,2,256,256]{3,2,1,0:T(8,128)(2,1)S(1)} collective-permute-done((bf16[5,2,256,256]{3,2,1,0:T(8,128)(2,1)S(1)}, bf16[5,2,256,256]{3,2,1,0:T(8,128)(2,1)S(1)}, u32[]{:S(2)}, u32[]{:S(2)}) %collective-permute-start.1) | collective-permute-done | bytes 1310752 | tf_op jit(solution)/shard_map/ppermute | solution.py:538
  33.8 1.7 collective-permute-start.4
  35.6 2.2 %copy-done.1 = bf16[1,16,2,256,256]{4,3,2,1,0:T(8,128)(2,1)S(1)} copy-done((bf16[1,16,2,256,256]{4,3,2,1,0:T(8,128)(2,1)S(1)}, bf16[1,16,2,256,256]{4,3,2,1,0:T(8,128)(2,1)}, u32[]{:S(2)}) %copy-start.1) | copy-done | bytes 4194328
  37.7 20.5 %shard_map.55 = (bf16[4,256,512]{2,1,0:T(8,128)(2,1)S(1)}, bf16[4,256,512]{2,1,0:T(8,128)(2,1)S(1)}, f32[1]{0:T(128)}, bf16[1,256,512]{2,1,0:T(8,128)(2,1)S(1)}) custom-call(f32[6,32]{1,0:T(8,128)S(1)} %select_maximum_fusion.refs_0_, s32[1,2,32]{2,1,0:T(2,128)S(1)} %collective-permute-done.refs_1_, bf16[1,16,2,256,256]{4,3,2,1,0:T(8,128)(2,1)S(1)} %copy-done.1, ...), custom_call_target="tpu_custom_call" | custom-call | flops 53687091200 | bytes 8388608 | tf_op jit(solution)/shard_map/pallas_call | solution.py:407
  58.9 1.6 collective-permute-start.5
  60.5 20.7 %shard_map.56 = (bf16[4,256,512]{2,1,0:T(8,128)(2,1)S(1)}, bf16[4,256,512]{2,1,0:T(8,128)(2,1)S(1)}, f32[1]{0:T(128)}, bf16[1,256,512]{2,1,0:T(8,128)(2,1)S(1)}) custom-call(f32[6,32]{1,0:T(8,128)S(1)} %select_maximum_fusion.refs_0_, s32[1,2,32]{2,1,0:T(2,128)S(1)} %collective-permute-done.refs_1_, bf16[1,16,2,256,256]{4,3,2,1,0:T(8,128)(2,1)S(1)} %copy-done.1, ...), custom_call_target="tpu_custom_call" | custom-call | flops 53687091200 | bytes 8388608 | tf_op jit(solution)/shard_map/pallas_call | solution.py:407
  81.2 4.8 %collective-permute-start.8 = (bf16[1,256,512]{2,1,0:T(8,128)(2,1)S(1)}, bf16[1,256,512]{2,1,0:T(8,128)(2,1)S(1)}, u32[]{:S(2)}, u32[]{:S(2)}) collective-permute-start(bf16[1,256,512]{2,1,0:T(8,128)(2,1)S(1)} %get-tuple-element.41), channel_id=1, source_target_pairs={{0,2},{1,3},{2,0},{3,1},{4,6},{5,7},{6,4},{7,5},{8,10},{9,11},{10,... | collective-permute-start | bytes 786440 | tf_op jit(solution)/shard_map/ppermute | solution.py:538
  86.1 18.7 %shard_map.57 = (bf16[3,2,256,256]{3,2,1,0:T(8,128)(2,1)}, bf16[3,2,256,256]{3,2,1,0:T(8,128)(2,1)S(1)}, f32[1]{0:T(128)}, bf16[1,256,256]{2,1,0:T(8,128)(2,1)S(1)}) custom-call(f32[6,32]{1,0:T(8,128)S(1)} %select_maximum_fusion.refs_0_, s32[1,2,32]{2,1,0:T(2,128)S(1)} %collective-permute-done.refs_1_, ...), custom_call_target="tpu_custom_call" | custom-call | flops 50331648000 | bytes 6291456 | tf_op jit(solution)/shard_map/pallas_call | solution.py:407
  106.7 6.8 %collective-permute-done.7.refs_5_ = bf16[4,256,512]{2,1,0:T(8,128)(2,1)S(1)} collective-permute-done((bf16[4,256,512]{2,1,0:T(8,128)(2,1)S(1)}, bf16[4,256,512]{2,1,0:T(8,128)(2,1)S(1)}, u32[]{:S(2)}, u32[]{:S(2)}) %collective-permute-start.7) | collective-permute-done | bytes 1048608 | tf_op jit(solution)/shard_map/ppermute | solution.py:538
  114.1 22.6 %shard_map.58 = (bf16[5,2,256,256]{3,2,1,0:T(8,128)(2,1)S(1)}, bf16[5,2,256,256]{3,2,1,0:T(8,128)(2,1)S(1)}, f32[1]{0:T(128)}) custom-call(f32[6,32]{1,0:T(8,128)S(1)} %select_maximum_fusion.refs_0_, s32[1,2,32]{2,1,0:T(2,128)S(1)} %collective-permute-done.refs_1_, bf16[4,256,512]{2,1,0:T(8,128)(2,1)S(1)} %get-tuple-element.33.refs_2_.refs_3_, ...), custom_call_target="tpu_custom_call" | custom-call | flops 57042534400 | bytes 10485760 | tf_op jit(solution)/shard_map/pallas_call | solution.py:407
  139.2 4.0 %psum.7.refs_0_ = f32[2]{0:T(128)S(1)} all-reduce(f32[2]{0:T(128)S(1)} %pad_maximum_fusion), channel_id=1, replica_groups=mesh['chain'=16,'block'=2] {'block'}, use_global_device_ids=true, to_apply=%region_0.1 | all-reduce | flops 2 | bytes 16 | tf_op jit(solution)/shard_map/psum | solution.py:625
  143.2 1.3 collective-permute-start.11
  144.5 4.1 %collective-permute-done.11 = f32[2]{0:T(128)S(1)} collective-permute-done((f32[2]{0:T(128)S(1)}, f32[2]{0:T(128)S(1)}, u32[]{:S(2)}, u32[]{:S(2)}) %collective-permute-start.11) | collective-permute-done | bytes 40 | tf_op jit(solution)/shard_map/ppermute | solution.py:538
  148.6 1.4 collective-permute-start.13
  150.0 1.9 %collective-permute-start.12 = (f32[2]{0:T(128)S(1)}, f32[2]{0:T(128)S(1)}, u32[]{:S(2)}, u32[]{:S(2)}) collective-permute-start(f32[2]{0:T(128)S(1)} %fusion), channel_id=1, source_target_pairs={{0,4},{1,5},{4,8},{5,9},{8,12},{9,13},{12,16},{13,17},{16,20},{17,... | collective-permute-start | bytes 32 | tf_op jit(solution)/shard_map/ppermute | solution.py:538
  151.9 6.2 %collective-permute-done.12.refs_1_ = f32[2]{0:T(128)S(1)} collective-permute-done((f32[2]{0:T(128)S(1)}, f32[2]{0:T(128)S(1)}, u32[]{:S(2)}, u32[]{:S(2)}) %collective-permute-start.12) | collective-permute-done | bytes 40 | tf_op jit(solution)/shard_map/ppermute | solution.py:538
  158.1 2.6 %shard_map.59.refs_3_ = bf16[1,16,2,256,256]{4,3,2,1,0:T(8,128)(2,1)} custom-call(f32[2]{0:T(128)S(1)} %psum.7.refs_0_, f32[2]{0:T(128)S(1)} %collective-permute-done.12.refs_1_, bf16[5,2,256,256]{3,2,1,0:T(8,128)(2,1)S(1)} %get-tuple-element.49.refs_2_, bf16[1,256,256]{2,1,0:T(8,128)(2,1)S(1)} %collective-permute-done.10.refs_3_, ...), custom_call_target="tpu_custom_call" | custom-call | bytes 5767168 | tf_op jit(solution)/shard_map/pallas_call | solution.py:512
  160.7 21.6 %collective-permute-done.13.refs_2_ = bf16[5,2,256,256]{3,2,1,0:T(8,128)(2,1)S(1)} collective-permute-done((bf16[5,2,256,256]{3,2,1,0:T(8,128)(2,1)}, bf16[5,2,256,256]{3,2,1,0:T(8,128)(2,1)S(1)}, u32[]{:S(2)}, u32[]{:S(2)}) %collective-permute-start.13) | collective-permute-done | bytes 1310752 | tf_op jit(solution)/shard_map/ppermute | solution.py:538
  182.3 2.1 %shard_map.60 = bf16[1,16,2,256,256]{4,3,2,1,0:T(8,128)(2,1)} custom-call(f32[2]{0:T(128)S(1)} %psum.7.refs_0_, f32[2]{0:T(128)S(1)} %collective-permute-done.12.refs_1_, bf16[5,2,256,256]{3,2,1,0:T(8,128)(2,1)S(1)} %collective-permute-done.13.refs_2_, bf16[1,16,2,256,256]{4,3,2,1,0:T(8,128)(2,1)} %shard_map.59.refs_3_), custom_call_target="tpu_custom_call", output_to_operand_aliasing={{}: (3, {})} | custom-call | bytes 2621440 | tf_op jit(solution)/shard_map/pallas_call | solution.py:512
  (34 shorter events, 4.8 us)
Async XLA Ops:
  0.0 7.3 %copy-start = (bf16[1,16,2,256,256]{4,3,2,1,0:T(8,128)(2,1)S(1)}, bf16[1,16,2,256,256]{4,3,2,1,0:T(8,128)(2,1)}, u32[]{:S(2)}) copy-start(bf16[1,16,2,256,256]{4,3,2,1,0:T(8,128)(2,1)} %refs_2_.3) | copy-start | bytes 12582916
  2.0 31.8 %collective-permute-start.1 = (bf16[5,2,256,256]{3,2,1,0:T(8,128)(2,1)S(1)}, bf16[5,2,256,256]{3,2,1,0:T(8,128)(2,1)S(1)}, u32[]{:S(2)}, u32[]{:S(2)}) collective-permute-start(bf16[5,2,256,256]{3,2,1,0:T(8,128)(2,1)S(1)} %select_bitcast_fusion), channel_id=1, source_target_pairs={{0,2},{1,3},{2,0},{3,1},{4,6},{5,7},{6,4},{7,5},{8,10},{9,11},{10,... | collective-permute-start | bytes 3932168 | tf_op jit(solution)/shard_map/ppermute | solution.py:538
  5.0 30.5 %collective-permute-start = (s32[1,2,32]{2,1,0:T(2,128)}, s32[1,2,32]{2,1,0:T(2,128)S(1)}, u32[]{:S(2)}, u32[]{:S(2)}) collective-permute-start(s32[1,2,32]{2,1,0:T(2,128)} %param.7), channel_id=1, source_target_pairs={{0,2},{1,3},{2,0},{3,1},{4,6},{5,7},{6,4},{7,5},{8,10},{9,11},{10,... | collective-permute-start | bytes 776 | tf_op jit(solution)/shard_map/ppermute | solution.py:538
  6.6 28.9 %collective-permute-start.3 = (bf16[1,256,256]{2,1,0:T(8,128)(2,1)}, bf16[1,256,256]{2,1,0:T(8,128)(2,1)S(1)}, u32[]{:S(2)}, u32[]{:S(2)}) collective-permute-start(bf16[1,256,256]{2,1,0:T(8,128)(2,1)} %slice_bitcast_fusion), channel_id=1, source_target_pairs={{2,1},{6,5},{10,9},{14,13},{18,17},{22,21},{26,25},{30,29}} | collective-permute-start | bytes 393224 | tf_op jit(solution)/shard_map/ppermute | solution.py:538
  8.0 3.3 %copy-start.5 = (s32[1,2,32]{2,1,0:T(2,128)S(1)}, s32[1,2,32]{2,1,0:T(2,128)}, u32[]{:S(2)}) copy-start(s32[1,2,32]{2,1,0:T(2,128)} %param.8) | copy-start | bytes 772
  8.0 3.3 %copy-start.6 = (s32[1,2,32]{2,1,0:T(2,128)S(1)}, s32[1,2,32]{2,1,0:T(2,128)}, u32[]{:S(2)}) copy-start(s32[1,2,32]{2,1,0:T(2,128)} %param.7) | copy-start | bytes 772
  8.0 3.3 %copy-start.3 = (bf16[512,256]{1,0:T(8,128)(2,1)S(1)}, bf16[512,256]{1,0:T(8,128)(2,1)}, u32[]{:S(2)}) copy-start(bf16[512,256]{1,0:T(8,128)(2,1)} %param.6) | copy-start | bytes 786436
  8.0 3.5 %copy-start.4 = (f32[1,2,3]{2,1,0:T(2,128)S(1)}, f32[1,2,3]{2,1,0:T(2,128)}, u32[]{:S(2)}) copy-start(f32[1,2,3]{2,1,0:T(2,128)} %param.9) | copy-start | bytes 76
  8.1 27.5 %collective-permute-start.2 = (bf16[1,2,256,256]{3,2,1,0:T(8,128)(2,1)}, bf16[1,2,256,256]{3,2,1,0:T(8,128)(2,1)S(1)}, u32[]{:S(2)}, u32[]{:S(2)}) collective-permute-start(bf16[1,2,256,256]{3,2,1,0:T(8,128)(2,1)} %select_bitcast_fusion.2), channel_id=1, source_target_pairs={{0,1},{3,2},{4,5},{7,6},{8,9},{11,10},{12,13},{15,14},{16,17},{19,... | collective-permute-start | bytes 786440 | tf_op jit(solution)/shard_map/ppermute | solution.py:538
  33.8 26.7 %collective-permute-start.4 = (bf16[4,2,256,256]{3,2,1,0:T(8,128)(2,1)}, bf16[4,2,256,256]{3,2,1,0:T(8,128)(2,1)S(1)}, u32[]{:S(2)}, u32[]{:S(2)}) collective-permute-start(bf16[4,2,256,256]{3,2,1,0:T(8,128)(2,1)} %select_bitcast_fusion.1), channel_id=1, source_target_pairs={{0,2},{1,3},{2,0},{3,1},{4,6},{5,7},{6,4},{7,5},{8,10},{9,11},{10,... | collective-permute-start | bytes 3145736 | tf_op jit(solution)/shard_map/ppermute | solution.py:538
  35.5 2.2 %copy-start.1 = (bf16[1,16,2,256,256]{4,3,2,1,0:T(8,128)(2,1)S(1)}, bf16[1,16,2,256,256]{4,3,2,1,0:T(8,128)(2,1)}, u32[]{:S(2)}) copy-start(bf16[1,16,2,256,256]{4,3,2,1,0:T(8,128)(2,1)} %refs_2_.3) | copy-start | bytes 12582916
  58.2 27.8 %collective-permute-start.6 = (bf16[1,256,512]{2,1,0:T(8,128)(2,1)S(1)}, bf16[1,256,512]{2,1,0:T(8,128)(2,1)S(1)}, u32[]{:S(2)}, u32[]{:S(2)}) collective-permute-start(bf16[1,256,512]{2,1,0:T(8,128)(2,1)S(1)} %get-tuple-element.35), channel_id=1, source_target_pairs={{1,30},{2,5},{5,2},{6,9},{9,6},{10,13},{13,10},{14,17},{17,14},{18... | collective-permute-start | bytes 786440 | tf_op jit(solution)/shard_map/ppermute | solution.py:538
  58.9 27.1 %collective-permute-start.5 = (bf16[4,256,512]{2,1,0:T(8,128)(2,1)S(1)}, bf16[4,256,512]{2,1,0:T(8,128)(2,1)S(1)}, u32[]{:S(2)}, u32[]{:S(2)}) collective-permute-start(bf16[4,256,512]{2,1,0:T(8,128)(2,1)S(1)} %get-tuple-element.34), channel_id=1, source_target_pairs={{0,4},{1,5},{2,30},{3,31},{4,8},{5,9},{6,2},{7,3},{8,12},{9,13},{1... | collective-permute-start | bytes 3145736 | tf_op jit(solution)/shard_map/ppermute | solution.py:538
  81.2 32.9 %collective-permute-start.8 = (bf16[1,256,512]{2,1,0:T(8,128)(2,1)S(1)}, bf16[1,256,512]{2,1,0:T(8,128)(2,1)S(1)}, u32[]{:S(2)}, u32[]{:S(2)}) collective-permute-start(bf16[1,256,512]{2,1,0:T(8,128)(2,1)S(1)} %get-tuple-element.41), channel_id=1, source_target_pairs={{0,2},{1,3},{2,0},{3,1},{4,6},{5,7},{6,4},{7,5},{8,10},{9,11},{10,... | collective-permute-start | bytes 786440 | tf_op jit(solution)/shard_map/ppermute | solution.py:538
  86.0 27.4 %collective-permute-start.7 = (bf16[4,256,512]{2,1,0:T(8,128)(2,1)S(1)}, bf16[4,256,512]{2,1,0:T(8,128)(2,1)S(1)}, u32[]{:S(2)}, u32[]{:S(2)}) collective-permute-start(bf16[4,256,512]{2,1,0:T(8,128)(2,1)S(1)} %get-tuple-element.39), channel_id=1, source_target_pairs={{0,4},{1,5},{2,30},{3,31},{4,8},{5,9},{6,2},{7,3},{8,12},{9,13},{1... | collective-permute-start | bytes 3145736 | tf_op jit(solution)/shard_map/ppermute | solution.py:538
  104.8 39.7 %collective-permute-start.10 = (bf16[1,256,256]{2,1,0:T(8,128)(2,1)S(1)}, bf16[1,256,256]{2,1,0:T(8,128)(2,1)S(1)}, u32[]{:S(2)}, u32[]{:S(2)}) collective-permute-start(bf16[1,256,256]{2,1,0:T(8,128)(2,1)S(1)} %get-tuple-element.45), channel_id=1, source_target_pairs={{1,30},{5,2},{9,6},{13,10},{17,14},{21,18},{25,22},{29,26}} | collective-permute-start | bytes 393224 | tf_op jit(solution)/shard_map/ppermute | solution.py:538
  113.5 31.0 %collective-permute-start.9 = (bf16[3,2,256,256]{3,2,1,0:T(8,128)(2,1)}, bf16[3,2,256,256]{3,2,1,0:T(8,128)(2,1)S(1)}, u32[]{:S(2)}, u32[]{:S(2)}) collective-permute-start(bf16[3,2,256,256]{3,2,1,0:T(8,128)(2,1)} %get-tuple-element.44), channel_id=1, source_target_pairs={{0,30},{1,31},{2,4},{3,5},{4,2},{5,3},{6,8},{7,9},{8,6},{9,7},{10,... | collective-permute-start | bytes 2359304 | tf_op jit(solution)/shard_map/ppermute | solution.py:538
  136.7 1.1 copy-start.2
  143.2 5.4 %collective-permute-start.11 = (f32[2]{0:T(128)S(1)}, f32[2]{0:T(128)S(1)}, u32[]{:S(2)}, u32[]{:S(2)}) collective-permute-start(f32[2]{0:T(128)S(1)} %psum.7.refs_0_), channel_id=1, source_target_pairs={{2,0},{3,1},{6,4},{7,5},{10,8},{11,9},{14,12},{15,13},{18,16},{19,... | collective-permute-start | bytes 32 | tf_op jit(solution)/shard_map/ppermute | solution.py:538
  148.6 33.7 %collective-permute-start.13 = (bf16[5,2,256,256]{3,2,1,0:T(8,128)(2,1)}, bf16[5,2,256,256]{3,2,1,0:T(8,128)(2,1)S(1)}, u32[]{:S(2)}, u32[]{:S(2)}) collective-permute-start(bf16[5,2,256,256]{3,2,1,0:T(8,128)(2,1)} %copy-done.2), channel_id=1, source_target_pairs={{0,30},{1,31},{2,4},{3,5},{4,2},{5,3},{6,8},{7,9},{8,6},{9,7},{10,... | collective-permute-start | bytes 3932168 | tf_op jit(solution)/shard_map/ppermute | solution.py:538
  150.0 8.1 %collective-permute-start.12 = (f32[2]{0:T(128)S(1)}, f32[2]{0:T(128)S(1)}, u32[]{:S(2)}, u32[]{:S(2)}) collective-permute-start(f32[2]{0:T(128)S(1)} %fusion), channel_id=1, source_target_pairs={{0,4},{1,5},{4,8},{5,9},{8,12},{9,13},{12,16},{13,17},{16,20},{17,... | collective-permute-start | bytes 32 | tf_op jit(solution)/shard_map/ppermute | solution.py:538
